TPU v7x, 32 devices: a whole 2x2x4 slice. The times are simulated.
32 devices in a mesh: batch: 8 (over z, x), hidden: 4 (over y, core).
Axes of the slice: x: 2, y: 2, z: 4, core: 2. Of those that a mesh axis runs over, the one named last changes fastest.
Arguments:
- tokens: bfloat16 [5120, 4096], P('batch', 'hidden'), may hold values from -18 to 18
- segments: int32 [8, 640], P('batch'), may hold values from 0 to 5, never falling along the last dimension, each value on 1 to 256 neighbouring positions
- rel_bias: float32 [32, 64], P(None, 'hidden'), may hold values from -4 to 4
- ln_gain: float32 [4096], replicated, may hold values from 0.25 to 1.75
- w_query: bfloat16 [4096, 4096], P('batch', 'hidden'), may hold values from -0.04 to 0.04
- w_key: bfloat16 [4096, 4096], P('batch', 'hidden'), may hold values from -1 to 1
- w_value: bfloat16 [4096, 4096], P('batch', 'hidden'), may hold values from -0.09375 to 0.09375
- w_out: bfloat16 [4096, 4096], P('hidden', 'batch'), may hold values from -0.09375 to 0.09375
Outputs:
- output: bfloat16 [5120, 4096], P('batch', 'hidden')
Inputs may be any that keep to these rules, and one draw needn't show every extreme that they name: `segments`: in each row (the 640 tokens of one group) passage ids start at 0 and grow by one at each new passage; every passage has 1 to 256 tokens, one has exactly 256, and all 6 ids occur.
All inputs are finite; a program needn't handle non-finite values.
Results may differ from a plain program's by a relative error of at most 0.0098.
Values may be sent and summed in bfloat16 or wider, within the bound.
No kernel may reach another device: no remote copies, remote signals or barrier semaphores. Data moves between devices by JAX's collectives and lax.ppermute only.
A program may use at most 128 MiB of HBM per device.

v0:
```python
import jax
import jax.numpy as jnp
from jax import lax
from jax.sharding import PartitionSpec as P

PASSAGE = 256
QBLOCK = 640
KWIN = 640


norm_epsilon = 1e-06
bucket_edges = (12, 16, 23, 32, 46, 64, 91)
masked_score = -1e30


def bucket_of(offsets):
    distance = jnp.abs(offsets)
    reached = sum(((distance >= threshold).astype(jnp.int32) for threshold in bucket_edges))
    within = jnp.where(distance < 8, distance, 8 + reached)
    return within + jnp.where(offsets > 0, 16, 0)


def rms_normed(activations, ln_gain):
    widened = activations.astype(jnp.float32)
    variance = jnp.mean(widened * widened, axis=1, keepdims=True)
    return (widened * lax.rsqrt(variance + norm_epsilon) * ln_gain).astype(jnp.bfloat16)


def attend(queries, keys_here, values_here, passage, bias_table):
    heads_here = queries.shape[0]
    length_here = queries.shape[1]
    head_width = queries.shape[2]
    halves = 2
    group_heads = heads_here // halves
    relative = (
        jnp.arange(KWIN, dtype=jnp.int32)[None, :] - jnp.arange(QBLOCK, dtype=jnp.int32)[:, None]
    )
    table_rows = bias_table.shape[0]

    def one_block(block_index, result):
        first_row = (block_index * QBLOCK).astype(jnp.int32)
        window_start = jnp.clip(first_row - PASSAGE, 0, length_here - KWIN)
        buckets = bucket_of(window_start - first_row + relative)
        same_passage = passage[:, None] == passage[None, :]

        def head_group(group_index):
            lowest = group_index * group_heads
            query_part = lax.dynamic_slice_in_dim(queries, lowest, group_heads, 0)
            key_part = lax.dynamic_slice_in_dim(keys_here, lowest, group_heads, 0)
            value_part = lax.dynamic_slice_in_dim(values_here, lowest, group_heads, 0)
            bias_part = lax.dynamic_slice_in_dim(bias_table, lowest, group_heads, 1)
            scores = jnp.einsum(
                "hqe,hke->hqk", query_part, key_part, preferred_element_type=jnp.float32
            )
            position_bias = sum(
                (
                    jnp.where(buckets[None] == level, bias_part[level][:, None, None], 0.0)
                    for level in range(table_rows)
                )
            )
            scores = jnp.where(same_passage[None], scores + position_bias, masked_score)
            row_max = jnp.max(scores, axis=2, keepdims=True)
            raised = jnp.exp(scores - row_max)
            attention_weights = (raised / jnp.sum(raised, axis=2, keepdims=True)).astype(
                jnp.bfloat16
            )
            combined = jnp.einsum(
                "hqk,hke->hqe", attention_weights, value_part, preferred_element_type=jnp.float32
            )
            return combined.astype(jnp.bfloat16)

        grouped = lax.map(head_group, jnp.arange(halves, dtype=jnp.int32))
        grouped = grouped.reshape(heads_here, QBLOCK, head_width)
        return grouped

    blank = jnp.zeros((heads_here, length_here, head_width), jnp.bfloat16)
    return lax.fori_loop(0, length_here // QBLOCK, one_block, blank)


def per_device(tokens, segments, rel_bias, ln_gain, w_query, w_key, w_value, w_out):
    gathered = lax.all_gather(tokens, "hidden", axis=1, tiled=True)
    normed = rms_normed(gathered, ln_gain)
    heads_here = rel_bias.shape[1]
    head_width = w_query.shape[1] // heads_here

    def add_product(portion):
        shaped = portion.reshape(portion.shape[0], heads_here, head_width)
        return jnp.einsum("td,dhe->hte", normed, shaped, preferred_element_type=jnp.float32)

    query_sum = add_product(lax.all_gather(w_query, "batch", axis=0, tiled=True))
    key_sum = add_product(lax.all_gather(w_key, "batch", axis=0, tiled=True))
    value_sum = add_product(lax.all_gather(w_value, "batch", axis=0, tiled=True))
    queries = query_sum.astype(jnp.bfloat16)
    keys_here = key_sum.astype(jnp.bfloat16)
    values_here = value_sum.astype(jnp.bfloat16)
    attended = attend(queries, keys_here, values_here, segments[0], rel_bias)
    portion = lax.all_gather(w_out, "batch", axis=1, tiled=True)
    shaped = portion.reshape(heads_here, head_width, portion.shape[1])
    partial_terms = jnp.einsum("hte,hec->tc", attended, shaped, preferred_element_type=jnp.float32)
    summed = lax.psum_scatter(
        partial_terms.astype(jnp.bfloat16), "hidden", scatter_dimension=1, tiled=True
    ).astype(jnp.float32)
    return (tokens.astype(jnp.float32) + summed).astype(jnp.bfloat16)


def solution(mesh):
    placed = (
        P("batch", "hidden"),
        P("batch", None),
        P(None, "hidden"),
        P(),
        P("batch", "hidden"),
        P("batch", "hidden"),
        P("batch", "hidden"),
        P("hidden", "batch"),
    )
    return jax.shard_map(
        per_device, mesh=mesh, in_specs=placed, out_specs=P("batch", "hidden"), check_vma=False
    )
```

profile of v0, /device:TPU:0, one launch (start us, length us, event | category | flops | bytes accessed | tf_op | source)
XLA Modules:
  0.0 714.4 jit_solution(13980944424839782651)
XLA Ops:
  10.0 42.1 %all-gather.6.cloned.1.call-done = bf16[640,4096]{1,0:T(8,128)(2,1)} async-done(((bf16[640,1024]{1,0:T(8,128)(2,1)}), bf16[640,4096]{1,0:T(8,128)(2,1)}) %all-gather.6.cloned.1.call-update) | async-done | bytes 5242896 | tf_op jit(solution)/shard_map/all_gather | solution.py:81
  52.1 3.6 fusion.52
  55.7 123.5 %all-gather.8.cloned.1.call-done = bf16[4096,1024]{1,0:T(8,128)(2,1)} async-done(((bf16[512,1024]{1,0:T(8,128)(2,1)}), bf16[4096,1024]{1,0:T(8,128)(2,1)}) %all-gather.8.cloned.1.call-update) | async-done | bytes 8388624 | tf_op jit(solution)/shard_map/all_gather | solution.py:90
  179.2 11.1 %fusion.59 = f32[640,1024]{0,1:S(1)} fusion(bf16[4096,1024]{1,0:T(8,128)(2,1)} %all-gather.8.cloned.1.call-done, bf16[640,4096]{1,0:T(8,128)(2,1)} %all-gather.6.cloned.1.call-done, f32[4096]{0:T(1024)S(1)} %copy-done.6, f32[640]{0:T(1024)S(1)} %add_rsqrt_fusion), kind=kOutput, calls=%fused_computation.75 | convolution fusion | flops 5379194880 | bytes 16271872
  190.2 1.3 convert_bitcast_fusion.2
  191.5 112.9 %all-gather.12.cloned.1.call-done = bf16[4096,1024]{1,0:T(8,128)(2,1)} async-done(((bf16[512,1024]{1,0:T(8,128)(2,1)}), bf16[4096,1024]{1,0:T(8,128)(2,1)}) %all-gather.12.cloned.1.call-update) | async-done | bytes 8388624 | tf_op jit(solution)/shard_map/all_gather | solution.py:92
  304.4 11.0 %fusion.55 = f32[640,1024]{0,1:S(1)} fusion(bf16[4096,1024]{1,0:T(8,128)(2,1)} %all-gather.12.cloned.1.call-done, bf16[640,4096]{1,0:T(8,128)(2,1)} %all-gather.6.cloned.1.call-done, f32[4096]{0:T(1024)S(1)} %copy-done.6, f32[640]{0:T(1024)S(1)} %add_rsqrt_fusion), kind=kOutput, calls=%fused_computation.73 | convolution fusion | flops 5379194880 | bytes 16271872
  315.4 114.1 %all-gather.10.cloned.1.call-done = bf16[4096,1024]{1,0:T(8,128)(2,1)} async-done(((bf16[512,1024]{1,0:T(8,128)(2,1)}), bf16[4096,1024]{1,0:T(8,128)(2,1)}) %all-gather.10.cloned.1.call-update) | async-done | bytes 8388624 | tf_op jit(solution)/shard_map/all_gather | solution.py:91
  429.5 11.1 %fusion.57 = f32[640,1024]{0,1:S(1)} fusion(bf16[4096,1024]{1,0:T(8,128)(2,1)} %all-gather.10.cloned.1.call-done, bf16[640,4096]{1,0:T(8,128)(2,1)} %all-gather.6.cloned.1.call-done, f32[4096]{0:T(1024)S(1)} %copy-done.6, f32[640]{0:T(1024)S(1)} %add_rsqrt_fusion), kind=kOutput, calls=%fused_computation.74 | convolution fusion | flops 5379194880 | bytes 16271872
  440.6 1.9 convert_bitcast_fusion
  442.5 202.0 %while.20 = (s32[]{:T(128)}, bf16[2,8,640,64]{2,3,1,0:T(8,128)(2,1)}, s32[2]{0:T(128)S(1)}, bf16[16,640,64]{1,2,0:T(8,128)(2,1)}, bf16[16,640,64]{1,2,0:T(8,128)...) while((s32[]{:T(128)}, ...), condition=%wide.region_4.5_spmd.clone.clone, body=%wide.region_1.4_spmd.clone.clone.sunk | while | flops 1265588480 | bytes 97880328 | solution.py:72
  466.1 0.8 fusion.100
  466.9 0.8 fusion.101
  467.7 0.8 fusion.102
  468.5 0.8 fusion.103
  469.3 0.8 broadcast_compare_fusion.11
  470.1 0.8 fusion.104
  470.9 0.8 fusion.105
  472.5 0.8 broadcast_compare_fusion.12
  473.3 0.8 fusion.107
  474.1 0.8 fusion.108
  474.9 0.8 fusion.109
  475.7 0.8 fusion.110
  478.4 50.8 %add_select_fusion.2 = f32[8,640,640]{1,2,0:T(8,128)} fusion(f32[8]{0:T(128)S(1)} %bitcast.160, f32[8]{0:T(128)S(1)} %bitcast.141, f32[8]{0:T(128)S(1)} %bitcast.142, f32[8]{0:T(128)S(1)} %bitcast.143, f32[8]{0:T(128)S(1)} %bitcast.144, f32[8]{0:T(128)S(1)} %bitcast.145, f32[8]{0:T(128)S(1)} %bitcast.146, f32[8]{0:T(128)S(1)} %bitcast.147, ...), kind=kOutput, calls=%fused_computation.5.clone.1 | convolution fusion | flops 632422400 | bytes 27952128 | tf_op jit(solution)/shard_map/while/body/eval_jaxpr/while/body/eval_jaxpr/hqe,hke->hqk/dot_general | solution.py:52
  529.3 11.1 %fusion.113 = f32[8,640]{1,0:T(8,128)S(1)} fusion(f32[8,640,640]{1,2,0:T(8,128)} %add_select_fusion.2), kind=kOutput, calls=%fused_computation.78.clone.1 | output fusion | flops 6554239 | bytes 13127680 | tf_op jit(solution)/shard_map/while/body/eval_jaxpr/while/body/eval_jaxpr/sub | solution.py:63
  540.5 12.5 %fusion.114 = bf16[2,8,640,64]{2,3,1,0:T(8,128)(2,1)} fusion(bf16[2,8,640,64]{2,3,1,0:T(8,128)(2,1)} %get-tuple-element.524, s32[]{:T(128)} %get-tuple-element.523, f32[8,640]{1,0:T(8,128)S(1)} %fusion.113, bf16[16,640,64]{1,2,0:T(8,128)(2,1)S(1)} %copy-done.2, s32[]{:T(128)S(6)} %select_n.615, f32[8,640,640]{1,2,0:T(8,128)} %add_select_fusion.2), kind=kOutput, calls=%fused_computation.21.clone.1 | convolution fusion | flops 429594240 | bytes 27546116 | tf_op jit(solution)/shard_map/while/body/eval_jaxpr/while/body/eval_jaxpr/hqk,hke->hqe/dot_general | solution.py:67
  570.1 50.8 %add_select_fusion.2 = f32[8,640,640]{1,2,0:T(8,128)} fusion(f32[8]{0:T(128)S(1)} %bitcast.160, f32[8]{0:T(128)S(1)} %bitcast.141, f32[8]{0:T(128)S(1)} %bitcast.142, f32[8]{0:T(128)S(1)} %bitcast.143, f32[8]{0:T(128)S(1)} %bitcast.144, f32[8]{0:T(128)S(1)} %bitcast.145, f32[8]{0:T(128)S(1)} %bitcast.146, f32[8]{0:T(128)S(1)} %bitcast.147, ...), kind=kOutput, calls=%fused_computation.5.clone.1 | convolution fusion | flops 632422400 | bytes 27952128 | tf_op jit(solution)/shard_map/while/body/eval_jaxpr/while/body/eval_jaxpr/hqe,hke->hqk/dot_general | solution.py:52
  621.0 10.8 %fusion.113 = f32[8,640]{1,0:T(8,128)S(1)} fusion(f32[8,640,640]{1,2,0:T(8,128)} %add_select_fusion.2), kind=kOutput, calls=%fused_computation.78.clone.1 | output fusion | flops 6554239 | bytes 13127680 | tf_op jit(solution)/shard_map/while/body/eval_jaxpr/while/body/eval_jaxpr/sub | solution.py:63
  631.8 12.5 %fusion.114 = bf16[2,8,640,64]{2,3,1,0:T(8,128)(2,1)} fusion(bf16[2,8,640,64]{2,3,1,0:T(8,128)(2,1)} %get-tuple-element.524, s32[]{:T(128)} %get-tuple-element.523, f32[8,640]{1,0:T(8,128)S(1)} %fusion.113, bf16[16,640,64]{1,2,0:T(8,128)(2,1)S(1)} %copy-done.2, s32[]{:T(128)S(6)} %select_n.615, f32[8,640,640]{1,2,0:T(8,128)} %add_select_fusion.2), kind=kOutput, calls=%fused_computation.21.clone.1 | convolution fusion | flops 429594240 | bytes 27546116 | tf_op jit(solution)/shard_map/while/body/eval_jaxpr/while/body/eval_jaxpr/hqk,hke->hqe/dot_general | solution.py:67
  644.5 10.0 %bitcast_convert_fusion = bf16[640,4096]{1,0:T(8,128)(2,1)} fusion(bf16[16,640,64]{1,2,0:T(8,128)(2,1)} %bitcast.174, bf16[16,64,4096]{2,1,0:T(8,128)(2,1)} %bitcast.173), kind=kOutput, calls=%fused_computation.67 | convolution fusion | flops 5371330560 | bytes 14942208 | tf_op jit(solution)/shard_map/hte,hec->tc/dot_general | solution.py:99
  654.5 49.7 %reduce-scatter.2.cloned.1.call-done = bf16[640,1024]{1,0:T(8,128)(2,1)} async-done(((bf16[640,4096]{1,0:T(8,128)(2,1)}), bf16[640,1024]{1,0:T(8,128)(2,1)}) %reduce-scatter.2.cloned.1.call-update) | async-done | bytes 1310736 | tf_op jit(solution)/shard_map/reduce_scatter | solution.py:100
  704.3 2.9 add_convert_fusion
  (131 shorter events, 26.7 us)
Async XLA Ops:
  6.5 45.5 %all-gather.6.cloned.1.call-start = ((), (), s32[]{:S(2)}) async-start(), calls=%async_computation.1 | async-start | bytes 6553600 | tf_op jit(solution)/shard_map/all_gather | solution.py:81
  7.3 171.9 %all-gather.8.cloned.1.call-start = ((), (), s32[]{:S(2)}) async-start(), calls=%async_computation.2 | async-start | bytes 9437184 | tf_op jit(solution)/shard_map/all_gather | solution.py:90
  8.0 2.0 copy-start.5
  8.0 296.4 %all-gather.12.cloned.1.call-start = ((), (), s32[]{:S(2)}) async-start(), calls=%async_computation.4 | async-start | bytes 9437184 | tf_op jit(solution)/shard_map/all_gather | solution.py:92
  8.8 420.8 %all-gather.10.cloned.1.call-start = ((), (), s32[]{:S(2)}) async-start(), calls=%async_computation.3 | async-start | bytes 9437184 | tf_op jit(solution)/shard_map/all_gather | solution.py:91
  9.3 635.2 %all-gather.14.cloned.1.call-start = ((), (), s32[]{:S(2)}) async-start(), calls=%async_computation.5 | async-start | bytes 9437184 | tf_op jit(solution)/shard_map/all_gather | solution.py:97
  9.9 694.4 %reduce-scatter.2.cloned.1.call-start = ((), (), s32[]{:S(2)}) async-start(), calls=%async_computation.6 | async-start | bytes 6553600 | tf_op jit(solution)/shard_map/reduce_scatter | solution.py:100
  10.0 169.2 %copy-start.6 = (f32[4096]{0:T(1024)S(1)}, f32[4096]{0:T(1024)}, u32[]{:S(2)}) copy-start(f32[4096]{0:T(1024)} %param.13) | copy-start | bytes 49156
  440.6 1.9 copy-start.4
  475.7 2.7 copy-start.1
  475.7 2.7 copy-start.3
  529.3 11.2 %copy-start.2 = (bf16[16,640,64]{1,2,0:T(8,128)(2,1)S(1)}, bf16[16,640,64]{1,2,0:T(8,128)(2,1)}, u32[]{:S(2)}) copy-start(bf16[16,640,64]{1,2,0:T(8,128)(2,1)} %get-tuple-element.541) | copy-start | bytes 3932164 | tf_op jit(solution)/shard_map/while/body/eval_jaxpr/while
  567.4 2.7 copy-start.1
  567.4 2.7 copy-start.3
  621.0 10.8 %copy-start.2 = (bf16[16,640,64]{1,2,0:T(8,128)(2,1)S(1)}, bf16[16,640,64]{1,2,0:T(8,128)(2,1)}, u32[]{:S(2)}) copy-start(bf16[16,640,64]{1,2,0:T(8,128)(2,1)} %get-tuple-element.541) | copy-start | bytes 3932164 | tf_op jit(solution)/shard_map/while/body/eval_jaxpr/while
  654.5 49.8 %copy-start = (bf16[640,1024]{1,0:T(8,128)(2,1)S(1)}, bf16[640,1024]{1,0:T(8,128)(2,1)}, u32[]{:S(2)}) copy-start(bf16[640,1024]{1,0:T(8,128)(2,1)} %param.10) | copy-start | bytes 3932164
Sparse Core Ops, SparseCore 0:
  8.9 43.1 all-gather.5
  54.2 124.9 all-gather.7
  181.3 123.1 all-gather.11
  306.4 123.0 all-gather.9
  431.4 123.5 all-gather.13
  654.7 49.5 reduce-scatter.1
where the time goes:
time: 724 us; the launch traced here: 714 us
  waiting for transfers between devices  446 us (62%)
  matrix products  170 us (23%)
  other arithmetic  57.7 us (8%)
  loops' own time  20.5 us (3%)
  between operations  13.9 us (2%)
    all_gather x1, waiting for transfers between devices, per_device(): lax.all_gather(w_query, 'batch', axis=0, tiled=True)  124 us
    all_gather x1, waiting for transfers between devices, per_device(): key_sum = add_product(lax.all_gather(w_key, 'batch', axis=0, tiled=True))  114 us
    all_gather x1, waiting for transfers between devices, per_device(): lax.all_gather(w_value, 'batch', axis=0, tiled=True)  113 us
    dot_general x2, matrix products, head_group(): jnp.einsum('hqe,hke->hqk', query_part, key_part, preferred_element_type=j...  102 us
    reduce_scatter x1, waiting for transfers between devices, per_device(): lax.psum_scatter(partial_terms.astype(jnp.bfloat16), 'hidden', scatter_di...  49.7 us
    all_gather x1, waiting for transfers between devices, per_device(): gathered = lax.all_gather(tokens, 'hidden', axis=1, tiled=True)  42.1 us
    unnamed x3, matrix products  33.1 us
    eq x32, other arithmetic, head_group(): buckets[None] == level  25.5 us
  transfers between devices with their start and end apart: 6, of which 5 were waited for; matrix products, arithmetic and copies ran while one was open for 31% of the time, Pallas kernels for 0%

commit v1 on v0

v1 whole, which is shorter than its diff:
```python
import functools

import jax
import jax.numpy as jnp
from jax import lax
from jax.experimental import pallas as pl
from jax.experimental.pallas import tpu as pltpu
from jax.sharding import PartitionSpec as P

PASSAGE = 256
BLOCK = 128

norm_epsilon = 1e-06
bucket_edges = (12, 16, 23, 32, 46, 64, 91)
masked_score = -1e30


def bucket_of(offsets):
    distance = jnp.abs(offsets)
    reached = sum(((distance >= threshold).astype(jnp.int32) for threshold in bucket_edges))
    within = jnp.where(distance < 8, distance, 8 + reached)
    return within + jnp.where(offsets > 0, 16, 0)


def bias_tiles(table):
    rows = 2 * PASSAGE + BLOCK
    offsets = (
        jnp.arange(rows, dtype=jnp.int32)[:, None]
        - PASSAGE
        - jnp.arange(BLOCK, dtype=jnp.int32)[None, :]
    )
    buckets = bucket_of(offsets)[None]
    tiles = jnp.zeros((table.shape[1], rows, BLOCK), jnp.float32)
    for level in range(table.shape[0]):
        tiles = jnp.where(buckets == level, table[level][:, None, None], tiles)
    return tiles


def attention_kernel(width, q_ids, k_ids, bias, queries, keys, values, out):
    length = keys.shape[0]
    blocks = length // BLOCK
    reach = PASSAGE // BLOCK
    heads = keys.shape[1] // width
    for i in range(blocks):
        low, high = max(0, i - reach) * BLOCK, min(blocks, i + reach + 1) * BLOCK
        columns = slice(i * BLOCK, (i + 1) * BLOCK)
        first = low - i * BLOCK + PASSAGE
        same = k_ids[low:high, :] == q_ids[:, columns]
        for h in range(heads):
            rows = slice(h * width, (h + 1) * width)
            own = queries[rows, columns]
            blank = jnp.zeros_like(own)
            spread = jnp.concatenate([own if g == h else blank for g in range(heads)], axis=0)
            scores = jnp.dot(keys[low:high, :], spread, preferred_element_type=jnp.float32)
            scores = jnp.where(same, scores + bias[h, first : first + high - low, :], masked_score)
            raised = jnp.exp(scores - jnp.max(scores, axis=0, keepdims=True)).astype(jnp.bfloat16)
            extended = jnp.concatenate(
                [values[rows, low:high], jnp.ones((16, high - low), jnp.bfloat16)], axis=0
            )
            total = jnp.dot(extended, raised, preferred_element_type=jnp.float32)
            out[rows, columns] = (total[:width] / total[width : width + 1]).astype(jnp.bfloat16)


def attend(queries, keys, values, ids, bias, group, width):
    length = ids.shape[0]
    features = keys.shape[1]
    pair = 128 // width
    wide_ids = jnp.broadcast_to(ids[:, None], (length, BLOCK))
    return pl.pallas_call(
        functools.partial(attention_kernel, width),
        grid=(features // 128,),
        in_specs=[
            pl.BlockSpec((1, length), lambda p: (0, 0)),
            pl.BlockSpec((length, BLOCK), lambda p: (0, 0)),
            pl.BlockSpec((pair,) + bias.shape[1:], lambda p: (p, 0, 0)),
            pl.BlockSpec((128, length), lambda p: (p, group)),
            pl.BlockSpec((length, 128), lambda p: (group, p)),
            pl.BlockSpec((128, length), lambda p: (p, group)),
        ],
        out_specs=pl.BlockSpec((128, length), lambda p: (p, 0)),
        out_shape=jax.ShapeDtypeStruct((features, length), jnp.bfloat16),
        compiler_params=pltpu.CompilerParams(vmem_limit_bytes=24 * 1024 * 1024),
        cost_estimate=pl.CostEstimate(
            flops=8 * features * length * length,
            bytes_accessed=16 * features * length,
            transcendentals=features // width * length * length,
        ),
    )(ids[None, :], wide_ids, bias, queries, keys, values)


def after(value, earlier):
    return lax.optimization_barrier((value, earlier))[0]


def per_device(n_batch, n_hidden, tokens, segments, rel_bias, ln_gain, w_query, w_key, w_value, w_out):
    place = lax.axis_index("batch")
    column = lax.axis_index("hidden")
    parity = (place >> 1) & 1
    length, own_width = tokens.shape
    heads = rel_bias.shape[1] // 2
    half = w_query.shape[1] // 2
    width = half // heads

    def swap(value, step, axis="batch"):
        count = n_batch if axis == "batch" else n_hidden
        return lax.ppermute(value, axis, [(i, i ^ step) for i in range(count)])

    peer_tokens = swap(tokens, 2)
    peer_ids = swap(segments, 2)
    gathered = [
        lax.all_gather(part, "hidden", axis=1, tiled=True) for part in (tokens, peer_tokens)
    ]

    history_far, history_near = [peer_tokens, peer_tokens], []

    def paced(value, step, history):
        if len(history) >= 2:
            value = after(value, history[-2])
        received = swap(value, step)
        history.append(received)
        return received

    def collect(weight, axis):
        halves = [
            lax.dynamic_slice_in_dim(weight, side * (weight.shape[axis] // 2), weight.shape[axis] // 2, axis)
            for side in (parity, 1 - parity)
        ]
        pieces = {0: halves[0]}
        far = list(range(n_batch - 2, 0, -2))
        for step in far:
            pieces[step] = paced(halves[(step >> 1) & 1], step, history_far)
        for step in [0] + far:
            pieces[step ^ 1] = paced(pieces[step], 1, history_near)
        return pieces

    key_pieces = collect(w_key, 1)
    query_pieces = collect(w_query, 1)
    value_pieces = collect(w_value, 1)
    out_pieces = collect(w_out, 0)

    table = lax.dynamic_slice_in_dim(rel_bias, parity * heads, heads, 1)
    bias = bias_tiles(table)

    both = jnp.concatenate(gathered, axis=0).astype(jnp.float32)
    scale = lax.rsqrt(jnp.mean(both * both, axis=1, keepdims=True) + norm_epsilon)
    depth = w_query.shape[0]

    def normed_part(step):
        start = (place ^ step) * depth
        return (
            lax.dynamic_slice_in_dim(both, start, depth, 1)
            * scale
            * lax.dynamic_slice_in_dim(ln_gain, start, depth, 0)
        ).astype(jnp.bfloat16)

    order = [s for e in [0] + list(range(n_batch - 2, 0, -2)) for s in (e, e ^ 1)]
    rounds = [order[: n_batch // 2], order[n_batch // 2 :]]
    normed = [jnp.concatenate([normed_part(step) for step in steps], axis=1) for steps in rounds]

    def project(pieces, form):
        total = None
        for part, steps in zip(normed, rounds):
            rows = jnp.concatenate([pieces[step] for step in steps], axis=0)
            term = jnp.einsum(form, part, rows, preferred_element_type=jnp.float32)
            total = term if total is None else total + term
        return total.astype(jnp.bfloat16)

    keys = project(key_pieces, "td,df->tf")
    queries = project(query_pieces, "td,df->ft")
    values = project(value_pieces, "td,df->ft")

    out_width = w_out.shape[1]
    w_out_here = jnp.zeros((half, out_width * n_batch), jnp.bfloat16)
    for step in range(n_batch):
        w_out_here = lax.dynamic_update_slice_in_dim(
            w_out_here, out_pieces[step], (place ^ step) * out_width, 1
        )

    def partial_sums(attended):
        def block(step):
            rows = lax.dynamic_slice_in_dim(w_out_here, (column ^ step) * own_width, own_width, 1)
            return jnp.einsum("ft,fc->tc", attended, rows, preferred_element_type=jnp.float32)

        def rounded(value):
            return value.astype(jnp.bfloat16)

        far = swap(rounded(block(3)), 1, "hidden")
        near = swap(rounded(block(1)), 1, "hidden")
        across = swap(rounded(block(2) + far.astype(jnp.float32)), 2, "hidden")
        return block(0) + near.astype(jnp.float32) + across.astype(jnp.float32)

    peer = partial_sums(attend(queries, keys, values, peer_ids[0], bias, 1, width))
    from_peer = swap(peer.astype(jnp.bfloat16), 2)
    own = partial_sums(attend(queries, keys, values, segments[0], bias, 0, width))
    return (tokens.astype(jnp.float32) + own + from_peer.astype(jnp.float32)).astype(jnp.bfloat16)


def solution(mesh):
    placed = (
        P("batch", "hidden"),
        P("batch", None),
        P(None, "hidden"),
        P(),
        P("batch", "hidden"),
        P("batch", "hidden"),
        P("batch", "hidden"),
        P("hidden", "batch"),
    )
    return jax.shard_map(
        functools.partial(per_device, mesh.shape["batch"], mesh.shape["hidden"]),
        mesh=mesh,
        in_specs=placed,
        out_specs=P("batch", "hidden"),
        check_vma=False,
    )
```

time: 724 us -> 442 us (0.61)
  waiting for transfers between devices: 446 us -> 221 us
  matrix products: 170 us -> 39.3 us
  starting transfers between devices: 0.19 us -> 72.6 us
  Pallas kernels: 0 us -> 22 us
  loops' own time: 20.5 us -> 0 us
  local copies, waits for them, and re-layouts: 6.78 us -> 22 us
  other arithmetic: 57.7 us -> 46.7 us
    all_gather x5 -> x2, waiting for transfers between devices: 393 us -> 0.01 us  [per_device(): lax.all_gather(part, 'hidden', axis=1, tiled=True)]
    ppermute x0 -> x37, waiting for transfers between devices: none -> 220 us  [swap(): return lax.ppermute(value, axis, [(i, i ^ step) for i in range(count)])]
    dot_general x5 -> x14, matrix products: 137 us -> 39.3 us  [the longest x6 22.7 us: project(): term = jnp.einsum(form, part, rows, preferred_element_type=jnp.float32)]
    ppermute x0 -> x37, starting transfers between devices: none -> 72.5 us  [swap(): return lax.ppermute(value, axis, [(i, i ^ step) for i in range(count)])]
    reduce_scatter x1 -> x0, waiting for transfers between devices: 49.7 us -> none  [per_device(): lax.psum_scatter(partial_terms.astype(jnp.bfloat16), 'hidden', scatter_di...]
    unnamed x3 -> x0, matrix products: 33.1 us -> none
    eq x34 -> x1, other arithmetic: 26 us -> 2.68 us  [bias_tiles(): tiles = jnp.where(buckets == level, table[level][:, None, None], tiles)]
    pallas_call x0 -> x2, Pallas kernels: none -> 22 us  [attend(): pl.pallas_call(functools.partial(attention_kernel, width), grid=(features...]
  transfers between devices with their start and end apart: 6 -> 39, of which waited for: 5 -> 21; matrix products, arithmetic and copies ran while one was open for 31% -> 10% of each run, Pallas kernels for 0% -> 3%
where the time goes in v1:
time: 442 us; the launch traced here: 438 us
  waiting for transfers between devices  221 us (50%)
  starting transfers between devices  72.6 us (16%)
  other arithmetic  46.7 us (11%)
  matrix products  39.3 us (9%)
  local copies, waits for them, and re-layouts  22 us (5%)
  Pallas kernels  22 us (5%)
  between operations  14.4 us (3%)
    ppermute x37, waiting for transfers between devices, swap(): return lax.ppermute(value, axis, [(i, i ^ step) for i in range(count)])  220 us
    ppermute x37, starting transfers between devices, swap(): return lax.ppermute(value, axis, [(i, i ^ step) for i in range(count)])  72.5 us
    dot_general x6, matrix products, project(): term = jnp.einsum(form, part, rows, preferred_element_type=jnp.float32)  22.7 us
    pallas_call x2, Pallas kernels, attend(): pl.pallas_call(functools.partial(attention_kernel, width), grid=(features...  22 us
    dot_general x8, matrix products, block(): jnp.einsum('ft,fc->tc', attended, rows, preferred_element_type=jnp.float32)  16.6 us
    convert_element_type x1, other arithmetic, per_device(): both = jnp.concatenate(gathered, axis=0).astype(jnp.float32)  13.9 us
    dynamic_update_slice x8, local copies, waits for them, and re-layouts, per_device(): lax.dynamic_update_slice_in_dim(w_out_here, out_pieces[step], (place ^ st...  12.3 us
    select_n x1, other arithmetic, bias_tiles(): tiles = jnp.where(buckets == level, table[level][:, None, None], tiles)  9.63 us
  transfers between devices with their start and end apart: 39, of which 21 were waited for; matrix products, arithmetic and copies ran while one was open for 10% of the time, Pallas kernels for 3%

profile of v1, /device:TPU:0, one launch (start us, length us, event | category | flops | bytes accessed | tf_op | source)
XLA Modules:
  0.0 437.7 jit_solution(10009650190290378584)
XLA Ops:
  10.4 29.0 %collective-permute-done = bf16[640,1024]{1,0:T(8,128)(2,1)S(1)} collective-permute-done((bf16[640,1024]{1,0:T(8,128)(2,1)}, bf16[640,1024]{1,0:T(8,128)(2,1)S(1)}, u32[]{:S(2)}, u32[]{:S(2)}) %collective-permute-start) | collective-permute-done | bytes 1310752 | tf_op jit(solution)/shard_map/ppermute | solution.py:106
  40.6 3.8 collective-permute-start.6
  44.5 12.9 %collective-permute-done.6 = bf16[512,512]{1,0:T(8,128)(2,1)S(1)} collective-permute-done((bf16[512,512]{1,0:T(8,128)(2,1)S(1)}, bf16[512,512]{1,0:T(8,128)(2,1)S(1)}, u32[]{:S(2)}, u32[]{:S(2)}) %collective-permute-start.6) | collective-permute-done | bytes 524320 | tf_op jit(solution)/shard_map/ppermute | solution.py:106
  57.4 21.5 %collective-permute-start.7 = (bf16[512,512]{1,0:T(8,128)(2,1)S(1)}, bf16[512,512]{1,0:T(8,128)(2,1)S(1)}, u32[]{:S(2)}, u32[]{:S(2)}) collective-permute-start(bf16[512,512]{1,0:T(8,128)(2,1)S(1)} %get-tuple-element.36), channel_id=1, source_target_pairs={{0,8},{4,12},{8,0},{12,4},{16,24},{20,28},{24,16},{28,20},{1,9},{5... | collective-permute-start | bytes 1572872 | tf_op jit(solution)/shard_map/ppermute | solution.py:106
  81.1 7.6 %collective-permute-done.1 = bf16[512,512]{1,0:T(8,128)(2,1)S(1)} collective-permute-done((bf16[512,512]{1,0:T(8,128)(2,1)S(1)}, bf16[512,512]{1,0:T(8,128)(2,1)S(1)}, u32[]{:S(2)}, u32[]{:S(2)}) %collective-permute-start.1) | collective-permute-done | bytes 524320 | tf_op jit(solution)/shard_map/ppermute | solution.py:106
  91.4 19.3 %collective-permute-done.7 = bf16[512,512]{1,0:T(8,128)(2,1)S(1)} collective-permute-done((bf16[512,512]{1,0:T(8,128)(2,1)S(1)}, bf16[512,512]{1,0:T(8,128)(2,1)S(1)}, u32[]{:S(2)}, u32[]{:S(2)}) %collective-permute-start.7) | collective-permute-done | bytes 524320 | tf_op jit(solution)/shard_map/ppermute | solution.py:106
  114.9 10.7 %collective-permute-done.9 = bf16[512,512]{1,0:T(8,128)(2,1)} collective-permute-done((bf16[512,512]{1,0:T(8,128)(2,1)S(1)}, bf16[512,512]{1,0:T(8,128)(2,1)}, u32[]{:S(2)}, u32[]{:S(2)}) %collective-permute-start.9) | collective-permute-done | bytes 524320 | tf_op jit(solution)/shard_map/ppermute | solution.py:106
  127.2 9.6 %collective-permute-done.3 = bf16[512,512]{1,0:T(8,128)(2,1)S(1)} collective-permute-done((bf16[512,512]{1,0:T(8,128)(2,1)S(1)}, bf16[512,512]{1,0:T(8,128)(2,1)S(1)}, u32[]{:S(2)}, u32[]{:S(2)}) %collective-permute-start.3) | collective-permute-done | bytes 524320 | tf_op jit(solution)/shard_map/ppermute | solution.py:106
  141.7 6.3 %collective-permute-done.10 = bf16[512,512]{1,0:T(8,128)(2,1)S(1)} collective-permute-done((bf16[512,512]{1,0:T(8,128)(2,1)S(1)}, bf16[512,512]{1,0:T(8,128)(2,1)S(1)}, u32[]{:S(2)}, u32[]{:S(2)}) %collective-permute-start.10) | collective-permute-done | bytes 524320 | tf_op jit(solution)/shard_map/ppermute | solution.py:106
  149.6 9.7 %collective-permute-done.4 = bf16[512,512]{1,0:T(8,128)(2,1)S(1)} collective-permute-done((bf16[512,512]{1,0:T(8,128)(2,1)S(1)}, bf16[512,512]{1,0:T(8,128)(2,1)S(1)}, u32[]{:S(2)}, u32[]{:S(2)}) %collective-permute-start.4) | collective-permute-done | bytes 524320 | tf_op jit(solution)/shard_map/ppermute | solution.py:106
  160.9 12.1 %collective-permute-start.20 = (bf16[512,512]{1,0:T(8,128)(2,1)}, bf16[512,512]{1,0:T(8,128)(2,1)}, u32[]{:S(2)}, u32[]{:S(2)}) collective-permute-start(bf16[512,512]{1,0:T(8,128)(2,1)} %get-tuple-element.48), channel_id=1, source_target_pairs={{0,8},{4,12},{8,0},{12,4},{16,24},{20,28},{24,16},{28,20},{1,9},{5... | collective-permute-start | bytes 1572872 | tf_op jit(solution)/shard_map/ppermute | solution.py:106
  176.8 5.0 %collective-permute-done.12 = bf16[512,512]{1,0:T(8,128)(2,1)} collective-permute-done((bf16[512,512]{1,0:T(8,128)(2,1)S(1)}, bf16[512,512]{1,0:T(8,128)(2,1)}, u32[]{:S(2)}, u32[]{:S(2)}) %collective-permute-start.12) | collective-permute-done | bytes 524320 | tf_op jit(solution)/shard_map/ppermute | solution.py:106
  185.7 15.2 %collective-permute-done.20 = bf16[512,512]{1,0:T(8,128)(2,1)} collective-permute-done((bf16[512,512]{1,0:T(8,128)(2,1)}, bf16[512,512]{1,0:T(8,128)(2,1)}, u32[]{:S(2)}, u32[]{:S(2)}) %collective-permute-start.20) | collective-permute-done | bytes 524320 | tf_op jit(solution)/shard_map/ppermute | solution.py:106
  207.4 8.6 %collective-permute-done.21 = bf16[512,512]{1,0:T(8,128)(2,1)S(1)} collective-permute-done((bf16[512,512]{1,0:T(8,128)(2,1)}, bf16[512,512]{1,0:T(8,128)(2,1)S(1)}, u32[]{:S(2)}, u32[]{:S(2)}) %collective-permute-start.21) | collective-permute-done | bytes 524320 | tf_op jit(solution)/shard_map/ppermute | solution.py:106
  219.8 7.4 %collective-permute-done.19 = bf16[512,512]{1,0:T(8,128)(2,1)S(1)} collective-permute-done((bf16[512,512]{1,0:T(8,128)(2,1)}, bf16[512,512]{1,0:T(8,128)(2,1)S(1)}, u32[]{:S(2)}, u32[]{:S(2)}) %collective-permute-start.19) | collective-permute-done | bytes 524320 | tf_op jit(solution)/shard_map/ppermute | solution.py:106
  228.2 10.2 %collective-permute-done.25 = bf16[512,512]{1,0:T(8,128)(2,1)S(1)} collective-permute-done((bf16[512,512]{1,0:T(8,128)(2,1)S(1)}, bf16[512,512]{1,0:T(8,128)(2,1)S(1)}, u32[]{:S(2)}, u32[]{:S(2)}) %collective-permute-start.25) | collective-permute-done | bytes 524320 | tf_op jit(solution)/shard_map/ppermute | solution.py:106
  239.5 9.6 %select_select_fusion.bias = f32[8,640,128]{2,1,0:T(8,128)S(1)} fusion(f32[8]{0:T(128)S(1)} %get-tuple-element.58, f32[8]{0:T(128)S(1)} %get-tuple-element.59, f32[8]{0:T(128)S(1)} %get-tuple-element.60, f32[8]{0:T(128)S(1)} %get-tuple-element.61, f32[8]{0:T(128)S(1)} %get-tuple-element.62, f32[8]{0:T(128)S(1)} %get-tuple-element.63, ...), kind=kLoop, calls=%fused_computation.22 | loop fusion | flops 20971520 | bytes 5243904 | tf_op jit(solution)/shard_map/jit(_where)/select_n | solution.py:35
  254.8 6.2 %collective-permute-done.26 = bf16[512,512]{1,0:T(8,128)(2,1)} collective-permute-done((bf16[512,512]{1,0:T(8,128)(2,1)}, bf16[512,512]{1,0:T(8,128)(2,1)}, u32[]{:S(2)}, u32[]{:S(2)}) %collective-permute-start.26) | collective-permute-done | bytes 524320 | tf_op jit(solution)/shard_map/ppermute | solution.py:106
  264.9 5.5 %collective-permute-done.28 = bf16[512,512]{1,0:T(8,128)(2,1)} collective-permute-done((bf16[512,512]{1,0:T(8,128)(2,1)}, bf16[512,512]{1,0:T(8,128)(2,1)}, u32[]{:S(2)}, u32[]{:S(2)}) %collective-permute-start.28) | collective-permute-done | bytes 524320 | tf_op jit(solution)/shard_map/ppermute | solution.py:106
  274.0 6.6 %multiply_reduce_fusion = f32[1280]{0:T(1024)S(1)} fusion(bf16[640,4096]{1,0:T(8,128)(2,1)} %all-gather.5.cloned.1.call-done, bf16[640,4096]{1,0:T(8,128)(2,1)} %all-gather.3.cloned.1.call-done), kind=kLoop, calls=%fused_computation | loop fusion | flops 31456000 | bytes 10490880 | tf_op jit(solution)/shard_map/reduce_sum | solution.py:145
  280.6 13.9 %maximum_convert_fusion = f32[1280,4096]{1,0:T(8,128)} fusion(bf16[640,4096]{1,0:T(8,128)(2,1)} %all-gather.5.cloned.1.call-done, bf16[640,4096]{1,0:T(8,128)(2,1)} %all-gather.3.cloned.1.call-done), kind=kLoop, calls=%fused_computation.1 | loop fusion | flops 20971520 | bytes 31457280 | tf_op jit(solution)/shard_map/convert_element_type | solution.py:144
  294.5 8.9 %multiply_convert_fusion.7 = (bf16[1280,512]{1,0:T(8,128)(2,1)S(1)}, bf16[1280,512]{1,0:T(8,128)(2,1)S(1)}, bf16[1280,512]{1,0:T(8,128)(2,1)S(1)}, bf16[1280,512...) fusion(f32[1280,4096]{1,0:T(8,128)} %maximum_convert_fusion, ...), kind=kLoop, calls=%fused_computation.21 | loop fusion | flops 15728640 | bytes 31478816 | tf_op jit(solution)/shard_map/convert_element_type | solution.py:154
  303.5 4.2 fusion.40
  307.9 4.1 fusion.25
  312.0 4.1 fusion.10
  316.1 4.3 fusion.2.values
  326.8 10.9 %shard_map.83 = bf16[512,640]{1,0:T(8,128)(2,1)S(1)} custom-call(s32[1,640]{1,0:T(1,128)S(1)} %collective-permute-done.32.q_ids, s32[640,128]{1,0:T(8,128)S(1)} %broadcast_in_dim.527.k_ids, f32[8,640,128]{2,1,0:T(8,128)S(1)} %select_select_fusion.bias, bf16[512,1280]{1,0:T(8,128)(2,1)S(1)} %fusion.queries, bf16[1280,512]{1,0:T(8,128)(2,1)S(1)} %fusion.1.keys, ...), custom_call_target="tpu_custom_call" | custom-call | flops 1677721600 | bytes 5242880 | tf_op jit(solution)/shard_map/pallas_call | solution.py:69
  345.0 11.1 %shard_map.82 = bf16[512,640]{1,0:T(8,128)(2,1)S(1)} custom-call(s32[1,640]{1,0:T(1,128)S(1)} %copy-done.10, s32[640,128]{1,0:T(8,128)S(1)} %broadcast_in_dim.427.k_ids, f32[8,640,128]{2,1,0:T(8,128)S(1)} %select_select_fusion.bias, bf16[512,1280]{1,0:T(8,128)(2,1)S(1)} %copy-done.7, bf16[1280,512]{1,0:T(8,128)(2,1)S(1)} %copy-done.5, ...), custom_call_target="tpu_custom_call" | custom-call | flops 1677721600 | bytes 5242880 | tf_op jit(solution)/shard_map/pallas_call | solution.py:69
  360.5 3.3 add_convert_fusion.2
  371.6 24.2 %collective-permute-done.35 = bf16[640,1024]{1,0:T(8,128)(2,1)} collective-permute-done((bf16[640,1024]{1,0:T(8,128)(2,1)}, bf16[640,1024]{1,0:T(8,128)(2,1)}, u32[]{:S(2)}, u32[]{:S(2)}) %collective-permute-start.35) | collective-permute-done | bytes 1310752 | tf_op jit(solution)/shard_map/ppermute | solution.py:106
  399.2 24.1 %collective-permute-done.31 = bf16[640,1024]{1,0:T(8,128)(2,1)S(1)} collective-permute-done((bf16[640,1024]{1,0:T(8,128)(2,1)S(1)}, bf16[640,1024]{1,0:T(8,128)(2,1)S(1)}, u32[]{:S(2)}, u32[]{:S(2)}) %collective-permute-start.31) | collective-permute-done | bytes 1310752 | tf_op jit(solution)/shard_map/ppermute | solution.py:106
  423.3 4.9 %collective-permute-done.36 = bf16[640,1024]{1,0:T(8,128)(2,1)S(1)} collective-permute-done((bf16[640,1024]{1,0:T(8,128)(2,1)S(1)}, bf16[640,1024]{1,0:T(8,128)(2,1)S(1)}, u32[]{:S(2)}, u32[]{:S(2)}) %collective-permute-start.36) | collective-permute-done | bytes 1310752 | tf_op jit(solution)/shard_map/ppermute | solution.py:106
  (211 shorter events, 88.4 us)
Async XLA Ops:
  6.5 267.5 %all-gather.3.cloned.1.call-start = ((), (), s32[]{:S(2)}) async-start(), calls=%async_computation | async-start | bytes 6553600 | tf_op jit(solution)/shard_map/all_gather | solution.py:111
  7.3 266.7 %all-gather.5.cloned.1.call-start = ((), (), s32[]{:S(2)}) async-start(), calls=%async_computation.1 | async-start | bytes 6553600 | tf_op jit(solution)/shard_map/all_gather | solution.py:111
  7.3 32.1 %collective-permute-start = (bf16[640,1024]{1,0:T(8,128)(2,1)}, bf16[640,1024]{1,0:T(8,128)(2,1)S(1)}, u32[]{:S(2)}, u32[]{:S(2)}) collective-permute-start(bf16[640,1024]{1,0:T(8,128)(2,1)} %param.8), channel_id=1, source_target_pairs={{0,8},{4,12},{8,0},{12,4},{16,24},{20,28},{24,16},{28,20},{1,9},{5... | collective-permute-start | bytes 3932168 | tf_op jit(solution)/shard_map/ppermute | solution.py:106
  44.5 44.2 %collective-permute-start.1 = (bf16[512,512]{1,0:T(8,128)(2,1)S(1)}, bf16[512,512]{1,0:T(8,128)(2,1)S(1)}, u32[]{:S(2)}, u32[]{:S(2)}) collective-permute-start(bf16[512,512]{1,0:T(8,128)(2,1)S(1)} %get-tuple-element.31), channel_id=1, source_target_pairs={{0,16},{4,20},{8,24},{12,28},{16,0},{20,4},{24,8},{28,12},{1,17},{... | collective-permute-start | bytes 1572872 | tf_op jit(solution)/shard_map/ppermute | solution.py:106
  57.4 53.2 %collective-permute-start.7 = (bf16[512,512]{1,0:T(8,128)(2,1)S(1)}, bf16[512,512]{1,0:T(8,128)(2,1)S(1)}, u32[]{:S(2)}, u32[]{:S(2)}) collective-permute-start(bf16[512,512]{1,0:T(8,128)(2,1)S(1)} %get-tuple-element.36), channel_id=1, source_target_pairs={{0,8},{4,12},{8,0},{12,4},{16,24},{20,28},{24,16},{28,20},{1,9},{5... | collective-permute-start | bytes 1572872 | tf_op jit(solution)/shard_map/ppermute | solution.py:106
  78.9 31.8 %collective-permute-start.8 = (bf16[512,512]{1,0:T(8,128)(2,1)S(1)}, bf16[512,512]{1,0:T(8,128)(2,1)S(1)}, u32[]{:S(2)}, u32[]{:S(2)}) collective-permute-start(bf16[512,512]{1,0:T(8,128)(2,1)S(1)} %collective-permute-done.6), channel_id=1, source_target_pairs={{0,4},{4,0},{8,12},{12,8},{16,20},{20,16},{24,28},{28,24},{1,5},{5... | collective-permute-start | bytes 1572872 | tf_op jit(solution)/shard_map/ppermute | solution.py:106
  80.4 32.0 %collective-permute-start.2 = (bf16[512,512]{1,0:T(8,128)(2,1)S(1)}, bf16[512,512]{1,0:T(8,128)(2,1)S(1)}, u32[]{:S(2)}, u32[]{:S(2)}) collective-permute-start(bf16[512,512]{1,0:T(8,128)(2,1)S(1)} %get-tuple-element.31), channel_id=1, source_target_pairs={{0,4},{4,0},{8,12},{12,8},{16,20},{20,16},{24,28},{28,24},{1,5},{5... | collective-permute-start | bytes 1572872 | tf_op jit(solution)/shard_map/ppermute | solution.py:106
  88.6 24.1 %collective-permute-start.5 = (bf16[512,512]{1,0:T(8,128)(2,1)S(1)}, bf16[512,512]{1,0:T(8,128)(2,1)S(1)}, u32[]{:S(2)}, u32[]{:S(2)}) collective-permute-start(bf16[512,512]{1,0:T(8,128)(2,1)S(1)} %get-tuple-element.41), channel_id=1, source_target_pairs={{0,24},{4,28},{8,16},{12,20},{16,8},{20,12},{24,0},{28,4},{1,25},{... | collective-permute-start | bytes 1572872 | tf_op jit(solution)/shard_map/ppermute | solution.py:106
  112.3 24.5 %collective-permute-start.3 = (bf16[512,512]{1,0:T(8,128)(2,1)S(1)}, bf16[512,512]{1,0:T(8,128)(2,1)S(1)}, u32[]{:S(2)}, u32[]{:S(2)}) collective-permute-start(bf16[512,512]{1,0:T(8,128)(2,1)S(1)} %collective-permute-done.1), channel_id=1, source_target_pairs={{0,4},{4,0},{8,12},{12,8},{16,20},{20,16},{24,28},{28,24},{1,5},{5... | collective-permute-start | bytes 1572872 | tf_op jit(solution)/shard_map/ppermute | solution.py:106
  112.8 27.3 %collective-permute-start.11 = (bf16[512,512]{1,0:T(8,128)(2,1)S(1)}, bf16[512,512]{1,0:T(8,128)(2,1)S(1)}, u32[]{:S(2)}, u32[]{:S(2)}) collective-permute-start(bf16[512,512]{1,0:T(8,128)(2,1)S(1)} %get-tuple-element.33), channel_id=1, source_target_pairs={{0,16},{4,20},{8,24},{12,28},{16,0},{20,4},{24,8},{28,12},{1,17},{... | collective-permute-start | bytes 1572872 | tf_op jit(solution)/shard_map/ppermute | solution.py:106
  112.8 28.9 %collective-permute-start.13 = (bf16[512,512]{1,0:T(8,128)(2,1)S(1)}, bf16[512,512]{1,0:T(8,128)(2,1)S(1)}, u32[]{:S(2)}, u32[]{:S(2)}) collective-permute-start(bf16[512,512]{1,0:T(8,128)(2,1)S(1)} %get-tuple-element.41), channel_id=1, source_target_pairs={{0,8},{4,12},{8,0},{12,4},{16,24},{20,28},{24,16},{28,20},{1,9},{5... | collective-permute-start | bytes 1572872 | tf_op jit(solution)/shard_map/ppermute | solution.py:106
  125.7 22.4 %collective-permute-start.10 = (bf16[512,512]{1,0:T(8,128)(2,1)S(1)}, bf16[512,512]{1,0:T(8,128)(2,1)S(1)}, u32[]{:S(2)}, u32[]{:S(2)}) collective-permute-start(bf16[512,512]{1,0:T(8,128)(2,1)S(1)} %collective-permute-done.5), channel_id=1, source_target_pairs={{0,4},{4,0},{8,12},{12,8},{16,20},{20,16},{24,28},{28,24},{1,5},{5... | collective-permute-start | bytes 1572872 | tf_op jit(solution)/shard_map/ppermute | solution.py:106
  137.6 21.7 %collective-permute-start.4 = (bf16[512,512]{1,0:T(8,128)(2,1)S(1)}, bf16[512,512]{1,0:T(8,128)(2,1)S(1)}, u32[]{:S(2)}, u32[]{:S(2)}) collective-permute-start(bf16[512,512]{1,0:T(8,128)(2,1)S(1)} %get-tuple-element.33), channel_id=1, source_target_pairs={{0,4},{4,0},{8,12},{12,8},{16,20},{20,16},{24,28},{28,24},{1,5},{5... | collective-permute-start | bytes 1572872 | tf_op jit(solution)/shard_map/ppermute | solution.py:106
  140.1 20.8 %collective-permute-start.16 = (bf16[512,512]{1,0:T(8,128)(2,1)}, bf16[512,512]{1,0:T(8,128)(2,1)}, u32[]{:S(2)}, u32[]{:S(2)}) collective-permute-start(bf16[512,512]{1,0:T(8,128)(2,1)} %get-tuple-element.48), channel_id=1, source_target_pairs={{0,24},{4,28},{8,16},{12,20},{16,8},{20,12},{24,0},{28,4},{1,25},{... | collective-permute-start | bytes 1572872 | tf_op jit(solution)/shard_map/ppermute | solution.py:106
  148.0 24.9 %collective-permute-start.14 = (bf16[512,512]{1,0:T(8,128)(2,1)S(1)}, bf16[512,512]{1,0:T(8,128)(2,1)S(1)}, u32[]{:S(2)}, u32[]{:S(2)}) collective-permute-start(bf16[512,512]{1,0:T(8,128)(2,1)S(1)} %collective-permute-done.13), channel_id=1, source_target_pairs={{0,4},{4,0},{8,12},{12,8},{16,20},{20,16},{24,28},{28,24},{1,5},{5... | collective-permute-start | bytes 1572872 | tf_op jit(solution)/shard_map/ppermute | solution.py:106
  159.3 22.6 %collective-permute-start.12 = (bf16[512,512]{1,0:T(8,128)(2,1)S(1)}, bf16[512,512]{1,0:T(8,128)(2,1)}, u32[]{:S(2)}, u32[]{:S(2)}) collective-permute-start(bf16[512,512]{1,0:T(8,128)(2,1)S(1)} %collective-permute-done.11), channel_id=1, source_target_pairs={{0,4},{4,0},{8,12},{12,8},{16,20},{20,16},{24,28},{28,24},{1,5},{5... | collective-permute-start | bytes 1572872 | tf_op jit(solution)/shard_map/ppermute | solution.py:106
  160.8 23.9 %collective-permute-start.18 = (bf16[512,512]{1,0:T(8,128)(2,1)S(1)}, bf16[512,512]{1,0:T(8,128)(2,1)}, u32[]{:S(2)}, u32[]{:S(2)}) collective-permute-start(bf16[512,512]{1,0:T(8,128)(2,1)S(1)} %get-tuple-element.43), channel_id=1, source_target_pairs={{0,16},{4,20},{8,24},{12,28},{16,0},{20,4},{24,8},{28,12},{1,17},{... | collective-permute-start | bytes 1572872 | tf_op jit(solution)/shard_map/ppermute | solution.py:106
  160.9 40.0 %collective-permute-start.20 = (bf16[512,512]{1,0:T(8,128)(2,1)}, bf16[512,512]{1,0:T(8,128)(2,1)}, u32[]{:S(2)}, u32[]{:S(2)}) collective-permute-start(bf16[512,512]{1,0:T(8,128)(2,1)} %get-tuple-element.48), channel_id=1, source_target_pairs={{0,8},{4,12},{8,0},{12,4},{16,24},{20,28},{24,16},{28,20},{1,9},{5... | collective-permute-start | bytes 1572872 | tf_op jit(solution)/shard_map/ppermute | solution.py:106
  173.7 27.1 %collective-permute-start.17 = (bf16[512,512]{1,0:T(8,128)(2,1)}, bf16[512,512]{1,0:T(8,128)(2,1)}, u32[]{:S(2)}, u32[]{:S(2)}) collective-permute-start(bf16[512,512]{1,0:T(8,128)(2,1)} %collective-permute-done.16), channel_id=1, source_target_pairs={{0,4},{4,0},{8,12},{12,8},{16,20},{20,16},{24,28},{28,24},{1,5},{5... | collective-permute-start | bytes 1572872 | tf_op jit(solution)/shard_map/ppermute | solution.py:106
  181.8 22.4 %collective-permute-start.15 = (bf16[512,512]{1,0:T(8,128)(2,1)S(1)}, bf16[512,512]{1,0:T(8,128)(2,1)S(1)}, u32[]{:S(2)}, u32[]{:S(2)}) collective-permute-start(bf16[512,512]{1,0:T(8,128)(2,1)S(1)} %get-tuple-element.43), channel_id=1, source_target_pairs={{0,4},{4,0},{8,12},{12,8},{16,20},{20,16},{24,28},{28,24},{1,5},{5... | collective-permute-start | bytes 1572872 | tf_op jit(solution)/shard_map/ppermute | solution.py:106
  184.7 21.1 %collective-permute-start.23 = (bf16[512,512]{1,0:T(8,128)(2,1)S(1)}, bf16[512,512]{1,0:T(8,128)(2,1)S(1)}, u32[]{:S(2)}, u32[]{:S(2)}) collective-permute-start(bf16[512,512]{1,0:T(8,128)(2,1)S(1)} %get-tuple-element.52), channel_id=1, source_target_pairs={{0,24},{4,28},{8,16},{12,20},{16,8},{20,12},{24,0},{28,4},{1,25},{... | collective-permute-start | bytes 1572872 | tf_op jit(solution)/shard_map/ppermute | solution.py:106
  201.6 49.3 %collective-permute-start.32 = (s32[1,640]{1,0:T(1,128)S(1)}, s32[1,640]{1,0:T(1,128)S(1)}, u32[]{:S(2)}, u32[]{:S(2)}) collective-permute-start(s32[1,640]{1,0:T(1,128)S(1)} %copy-done.10), channel_id=1, source_target_pairs={{0,8},{4,12},{8,0},{12,4},{16,24},{20,28},{24,16},{28,20},{1,9},{5... | collective-permute-start | bytes 7688 | tf_op jit(solution)/shard_map/ppermute | solution.py:106
  204.2 23.0 %collective-permute-start.19 = (bf16[512,512]{1,0:T(8,128)(2,1)}, bf16[512,512]{1,0:T(8,128)(2,1)S(1)}, u32[]{:S(2)}, u32[]{:S(2)}) collective-permute-start(bf16[512,512]{1,0:T(8,128)(2,1)} %collective-permute-done.18), channel_id=1, source_target_pairs={{0,4},{4,0},{8,12},{12,8},{16,20},{20,16},{24,28},{28,24},{1,5},{5... | collective-permute-start | bytes 1572872 | tf_op jit(solution)/shard_map/ppermute | solution.py:106
  205.8 22.5 %collective-permute-start.24 = (bf16[512,512]{1,0:T(8,128)(2,1)S(1)}, bf16[512,512]{1,0:T(8,128)(2,1)}, u32[]{:S(2)}, u32[]{:S(2)}) collective-permute-start(bf16[512,512]{1,0:T(8,128)(2,1)S(1)} %get-tuple-element.52), channel_id=1, source_target_pairs={{0,8},{4,12},{8,0},{12,4},{16,24},{20,28},{24,16},{28,20},{1,9},{5... | collective-permute-start | bytes 1572872 | tf_op jit(solution)/shard_map/ppermute | solution.py:106
  216.0 22.5 %collective-permute-start.25 = (bf16[512,512]{1,0:T(8,128)(2,1)S(1)}, bf16[512,512]{1,0:T(8,128)(2,1)S(1)}, u32[]{:S(2)}, u32[]{:S(2)}) collective-permute-start(bf16[512,512]{1,0:T(8,128)(2,1)S(1)} %collective-permute-done.23), channel_id=1, source_target_pairs={{0,4},{4,0},{8,12},{12,8},{16,20},{20,16},{24,28},{28,24},{1,5},{5... | collective-permute-start | bytes 1572872 | tf_op jit(solution)/shard_map/ppermute | solution.py:106
  219.7 29.5 %collective-permute-start.27 = (bf16[512,512]{1,0:T(8,128)(2,1)}, bf16[512,512]{1,0:T(8,128)(2,1)}, u32[]{:S(2)}, u32[]{:S(2)}) collective-permute-start(bf16[512,512]{1,0:T(8,128)(2,1)} %get-tuple-element.55), channel_id=1, source_target_pairs={{0,16},{4,20},{8,24},{12,28},{16,0},{20,4},{24,8},{28,12},{1,17},{... | collective-permute-start | bytes 1572872 | tf_op jit(solution)/shard_map/ppermute | solution.py:106
  227.2 22.6 %collective-permute-start.22 = (bf16[512,512]{1,0:T(8,128)(2,1)}, bf16[512,512]{1,0:T(8,128)(2,1)}, u32[]{:S(2)}, u32[]{:S(2)}) collective-permute-start(bf16[512,512]{1,0:T(8,128)(2,1)} %get-tuple-element.55), channel_id=1, source_target_pairs={{0,4},{4,0},{8,12},{12,8},{16,20},{20,16},{24,28},{28,24},{1,5},{5... | collective-permute-start | bytes 1572872 | tf_op jit(solution)/shard_map/ppermute | solution.py:106
  238.4 22.6 %collective-permute-start.26 = (bf16[512,512]{1,0:T(8,128)(2,1)}, bf16[512,512]{1,0:T(8,128)(2,1)}, u32[]{:S(2)}, u32[]{:S(2)}) collective-permute-start(bf16[512,512]{1,0:T(8,128)(2,1)} %collective-permute-done.24), channel_id=1, source_target_pairs={{0,4},{4,0},{8,12},{12,8},{16,20},{20,16},{24,28},{28,24},{1,5},{5... | collective-permute-start | bytes 1572872 | tf_op jit(solution)/shard_map/ppermute | solution.py:106
  363.8 31.9 %collective-permute-start.35 = (bf16[640,1024]{1,0:T(8,128)(2,1)}, bf16[640,1024]{1,0:T(8,128)(2,1)}, u32[]{:S(2)}, u32[]{:S(2)}) collective-permute-start(bf16[640,1024]{1,0:T(8,128)(2,1)} %add_convert_fusion.2), channel_id=1, source_target_pairs={{0,2},{1,3},{2,0},{3,1},{4,6},{5,7},{6,4},{7,5},{8,10},{9,11},{10,... | collective-permute-start | bytes 3932168 | tf_op jit(solution)/shard_map/ppermute | solution.py:106
  367.9 31.3 %collective-permute-start.29 = (bf16[640,1024]{1,0:T(8,128)(2,1)S(1)}, bf16[640,1024]{1,0:T(8,128)(2,1)S(1)}, u32[]{:S(2)}, u32[]{:S(2)}) collective-permute-start(bf16[640,1024]{1,0:T(8,128)(2,1)S(1)} %convolution_convert_fusion.3), channel_id=1, source_target_pairs={{0,1},{1,0},{2,3},{3,2},{4,5},{5,4},{6,7},{7,6},{8,9},{9,8},{10,11... | collective-permute-start | bytes 3932168 | tf_op jit(solution)/shard_map/ppermute | solution.py:106
  371.2 52.1 %collective-permute-start.31 = (bf16[640,1024]{1,0:T(8,128)(2,1)S(1)}, bf16[640,1024]{1,0:T(8,128)(2,1)S(1)}, u32[]{:S(2)}, u32[]{:S(2)}) collective-permute-start(bf16[640,1024]{1,0:T(8,128)(2,1)S(1)} %add_convert_fusion.3), channel_id=1, source_target_pairs={{0,2},{1,3},{2,0},{3,1},{4,6},{5,7},{6,4},{7,5},{8,10},{9,11},{10,... | collective-permute-start | bytes 3932168 | tf_op jit(solution)/shard_map/ppermute | solution.py:106
  398.2 30.0 %collective-permute-start.36 = (bf16[640,1024]{1,0:T(8,128)(2,1)S(1)}, bf16[640,1024]{1,0:T(8,128)(2,1)S(1)}, u32[]{:S(2)}, u32[]{:S(2)}) collective-permute-start(bf16[640,1024]{1,0:T(8,128)(2,1)S(1)} %add_convert_fusion.1), channel_id=1, source_target_pairs={{0,8},{4,12},{8,0},{12,4},{16,24},{20,28},{24,16},{28,20},{1,9},{5... | collective-permute-start | bytes 3932168 | tf_op jit(solution)/shard_map/ppermute | solution.py:106
  (66 other events, 1573.9 us)
Sparse Core Ops, SparseCore 0:
  8.9 43.1 all-gather.2
  53.7 40.4 all-gather.4

commit v2 on v1

--- a/solution.py
+++ b/solution.py
@@ -105,55 +105,73 @@
         count = n_batch if axis == "batch" else n_hidden
         return lax.ppermute(value, axis, [(i, i ^ step) for i in range(count)])
 
+    def halves(weight, axis):
+        size = weight.shape[axis] // 2
+        return [
+            lax.dynamic_slice_in_dim(weight, side * size, size, axis)
+            for side in (parity, 1 - parity)
+        ]
+
+    far_steps = list(range(n_batch - 2, 2, -2))
+    far_line, near_line = [], []
+
+    def paced(value, step, line, *earlier):
+        waits = tuple(line[-2:-1]) + earlier
+        if waits:
+            value = after(value, waits)
+        received = swap(value, step)
+        line.append(received)
+        return received
+
+    def along_z(parts, earlier):
+        pieces = {0: parts[0]}
+        for step in far_steps:
+            pieces[step] = paced(parts[(step >> 1) & 1], step, far_line, *earlier.get(step, ()))
+        pieces[2] = swap(after(parts[1], far_line[-2:-1]), 2)
+        return pieces
+
+    def along_x(pieces, steps, earlier):
+        for step in steps:
+            pieces[step ^ 1] = paced(pieces[step], 1, near_line, *earlier.get(step, ()))
+
     peer_tokens = swap(tokens, 2)
     peer_ids = swap(segments, 2)
-    gathered = [
-        lax.all_gather(part, "hidden", axis=1, tiled=True) for part in (tokens, peer_tokens)
-    ]
-
-    history_far, history_near = [peer_tokens, peer_tokens], []
-
-    def paced(value, step, history):
-        if len(history) >= 2:
-            value = after(value, history[-2])
-        received = swap(value, step)
-        history.append(received)
-        return received
-
-    def collect(weight, axis):
-        halves = [
-            lax.dynamic_slice_in_dim(weight, side * (weight.shape[axis] // 2), weight.shape[axis] // 2, axis)
-            for side in (parity, 1 - parity)
-        ]
-        pieces = {0: halves[0]}
-        far = list(range(n_batch - 2, 0, -2))
-        for step in far:
-            pieces[step] = paced(halves[(step >> 1) & 1], step, history_far)
-        for step in [0] + far:
-            pieces[step ^ 1] = paced(pieces[step], 1, history_near)
-        return pieces
-
-    key_pieces = collect(w_key, 1)
-    query_pieces = collect(w_query, 1)
-    value_pieces = collect(w_value, 1)
-    out_pieces = collect(w_out, 0)
+
+    def all_features(part):
+        across = swap(part, 2, "hidden")
+        return [part, swap(part, 1, "hidden"), across, swap(across, 1, "hidden")]
+
+    gathered = [all_features(part) for part in (tokens, peer_tokens)]
+
+    key_pieces = along_z(halves(w_key, 1), {})
+    query_parts = halves(w_query, 1)
+    query_pieces = along_z(query_parts, {})
+    value_parts = halves(w_value, 1)
+    others = far_steps + [2]
+    along_x(key_pieces, [0], {})
+    along_x(query_pieces, [0], {})
+    along_x(key_pieces, others, {})
+    along_x(query_pieces, others, {})
 
     table = lax.dynamic_slice_in_dim(rel_bias, parity * heads, heads, 1)
     bias = bias_tiles(table)
 
-    both = jnp.concatenate(gathered, axis=0).astype(jnp.float32)
-    scale = lax.rsqrt(jnp.mean(both * both, axis=1, keepdims=True) + norm_epsilon)
+    both = jnp.concatenate([jnp.concatenate(parts, axis=1) for parts in gathered], axis=0)
+    wide = both.astype(jnp.float32)
+    scale = lax.rsqrt(jnp.mean(wide * wide, axis=1, keepdims=True) + norm_epsilon)
     depth = w_query.shape[0]
+    per_block = own_width // depth
 
     def normed_part(step):
-        start = (place ^ step) * depth
+        source = place ^ step
+        where = ((source // per_block) ^ column) * own_width + (source % per_block) * depth
         return (
-            lax.dynamic_slice_in_dim(both, start, depth, 1)
+            lax.dynamic_slice_in_dim(both, where, depth, 1).astype(jnp.float32)
             * scale
-            * lax.dynamic_slice_in_dim(ln_gain, start, depth, 0)
+            * lax.dynamic_slice_in_dim(ln_gain, source * depth, depth, 0)
         ).astype(jnp.bfloat16)
 
-    order = [s for e in [0] + list(range(n_batch - 2, 0, -2)) for s in (e, e ^ 1)]
+    order = [s for e in [0] + others for s in (e, e ^ 1)]
     rounds = [order[: n_batch // 2], order[n_batch // 2 :]]
     normed = [jnp.concatenate([normed_part(step) for step in steps], axis=1) for steps in rounds]
 
@@ -167,32 +185,50 @@
 
     keys = project(key_pieces, "td,df->tf")
     queries = project(query_pieces, "td,df->ft")
+    last = far_steps[-1]
+    value_pieces = along_z(value_parts, {last: (normed[0], normed[1])})
+    along_x(value_pieces, [0] + others, {})
     values = project(value_pieces, "td,df->ft")
 
-    out_width = w_out.shape[1]
-    w_out_here = jnp.zeros((half, out_width * n_batch), jnp.bfloat16)
-    for step in range(n_batch):
-        w_out_here = lax.dynamic_update_slice_in_dim(
-            w_out_here, out_pieces[step], (place ^ step) * out_width, 1
-        )
-
-    def partial_sums(attended):
+    out_pieces = along_z(halves(w_out, 0), {far_steps[0]: (keys,), last: (queries,)})
+    along_x(out_pieces, [0], {})
+    attended = [attend(queries, keys, values, peer_ids[0], bias, 1, width)]
+    along_x(out_pieces, [2] + far_steps, {last: (attended[0],)})
+    attended.insert(0, attend(queries, keys, values, segments[0], bias, 0, width))
+    attended = jnp.concatenate(attended, axis=1)
+
+    side = place & 1
+    stripes = own_width // (2 * w_out.shape[1])
+
+    def sums(parity_step):
+        rows = jnp.concatenate([out_pieces[e ^ parity_step] for e in range(0, n_batch, 2)], axis=0)
+
         def block(step):
-            rows = lax.dynamic_slice_in_dim(w_out_here, (column ^ step) * own_width, own_width, 1)
-            return jnp.einsum("ft,fc->tc", attended, rows, preferred_element_type=jnp.float32)
-
-        def rounded(value):
-            return value.astype(jnp.bfloat16)
-
-        far = swap(rounded(block(3)), 1, "hidden")
-        near = swap(rounded(block(1)), 1, "hidden")
-        across = swap(rounded(block(2) + far.astype(jnp.float32)), 2, "hidden")
-        return block(0) + near.astype(jnp.float32) + across.astype(jnp.float32)
-
-    peer = partial_sums(attend(queries, keys, values, peer_ids[0], bias, 1, width))
-    from_peer = swap(peer.astype(jnp.bfloat16), 2)
-    own = partial_sums(attend(queries, keys, values, segments[0], bias, 0, width))
-    return (tokens.astype(jnp.float32) + own + from_peer.astype(jnp.float32)).astype(jnp.bfloat16)
+            first = (column ^ step) * stripes
+            chosen = [
+                lax.dynamic_slice_in_dim(rows, ((place >> 1) ^ (first + j)) * half, half, 0)
+                for j in range(stripes)
+            ]
+            chosen = chosen[0] if stripes == 1 else jnp.concatenate(chosen, axis=1)
+            return jnp.einsum("ft,fc->tc", attended, chosen, preferred_element_type=jnp.float32)
+
+        far = send(block(3), 1, "hidden")
+        near = send(block(1), 1, "hidden")
+        return block(0) + near, block(2) + far
+
+    def send(value, step, axis="batch"):
+        return swap(value.astype(jnp.bfloat16), step, axis).astype(jnp.float32)
+
+    here, there = sums(0)
+    first = here + send(there, 2, "hidden")
+    first = first[:length] + send(first[length:], 2)
+    here, there = sums(1)
+    there = there[:length] + send(there[length:], 2)
+    second = here[:length] + send(here[length:], 2) + send(there, 2, "hidden")
+
+    parts = [v.reshape(length, stripes, w_out.shape[1]) for v in (first, second)]
+    combined = jnp.where(side == 0, jnp.stack(parts, 2), jnp.stack(parts[::-1], 2))
+    return (tokens.astype(jnp.float32) + combined.reshape(length, own_width)).astype(jnp.bfloat16)
 
 
 def solution(mesh):

time: 442 us -> 411 us (0.930)
  between operations: 14.4 us -> 1.33 us
  waiting for transfers between devices: 221 us -> 209 us
  local copies, waits for them, and re-layouts: 22 us -> 12.8 us
  starting transfers between devices: 72.6 us -> 80 us
    convert_element_type x4 -> x3, other arithmetic: 27.7 us -> 7.78 us  [the longest x1 4.03 us: normed_part(): return (lax.dynamic_slice_in_dim(both, where, depth, 1).astype(jnp.float3...]
    dynamic_update_slice x8 -> x0, local copies, waits for them, and re-layouts: 12.3 us -> none  [per_device(): lax.dynamic_update_slice_in_dim(w_out_here, out_pieces[step], (place ^ st...]
    reduce_sum x1, other arithmetic: 6.61 us -> 18.8 us  [per_device(): jnp.mean(wide * wide, axis=1, keepdims=True) + norm_epsilon]
    ppermute x37 -> x45, waiting for transfers between devices: 220 us -> 209 us  [swap(): return lax.ppermute(value, axis, [(i, i ^ step) for i in range(count)])]
    ppermute x37 -> x45, starting transfers between devices: 72.5 us -> 80 us  [swap(): return lax.ppermute(value, axis, [(i, i ^ step) for i in range(count)])]
  transfers between devices with their start and end apart: 39 -> 45, of which waited for: 21 -> 17; matrix products, arithmetic and copies ran while one was open for 10% -> 21% of each run, Pallas kernels for 3% -> 5%
where the time goes in v2:
time: 411 us; the launch traced here: 408 us
  waiting for transfers between devices  209 us (51%)
  starting transfers between devices  80 us (19%)
  other arithmetic  43.3 us (11%)
  matrix products  39.5 us (10%)
  Pallas kernels  22 us (5%)
  local copies, waits for them, and re-layouts  12.8 us (3%)
    ppermute x45, waiting for transfers between devices, swap(): return lax.ppermute(value, axis, [(i, i ^ step) for i in range(count)])  209 us
    ppermute x45, starting transfers between devices, swap(): return lax.ppermute(value, axis, [(i, i ^ step) for i in range(count)])  80 us
    pallas_call x2, Pallas kernels, attend(): pl.pallas_call(functools.partial(attention_kernel, width), grid=(features...  22 us
    dot_general x6, matrix products, project(): term = jnp.einsum(form, part, rows, preferred_element_type=jnp.float32)  20.9 us
    reduce_sum x1, other arithmetic, per_device(): jnp.mean(wide * wide, axis=1, keepdims=True) + norm_epsilon  18.8 us
    dot_general x8, matrix products, block(): jnp.einsum('ft,fc->tc', attended, chosen, preferred_element_type=jnp.floa...  18.6 us
    select_n x1, other arithmetic, bias_tiles(): tiles = jnp.where(buckets == level, table[level][:, None, None], tiles)  9.65 us
  transfers between devices with their start and end apart: 45, of which 17 were waited for; matrix products, arithmetic and copies ran while one was open for 21% of the time, Pallas kernels for 5%

profile of v2, /device:TPU:0, one launch (start us, length us, event | category | flops | bytes accessed | tf_op | source)
XLA Modules:
  0.0 407.8 jit_solution(6489420992288559632)
XLA Ops:
  0.0 3.1 collective-permute-start.9
  9.3 34.4 %collective-permute-done.3 = bf16[512,512]{1,0:T(8,128)(2,1)S(1)} collective-permute-done((bf16[512,512]{1,0:T(8,128)(2,1)S(1)}, bf16[512,512]{1,0:T(8,128)(2,1)S(1)}, u32[]{:S(2)}, u32[]{:S(2)}) %collective-permute-start.3) | collective-permute-done | bytes 524320 | tf_op jit(solution)/shard_map/ppermute | solution.py:106
  45.2 11.6 %collective-permute-done.1 = bf16[512,512]{1,0:T(8,128)(2,1)S(1)} collective-permute-done((bf16[512,512]{1,0:T(8,128)(2,1)S(1)}, bf16[512,512]{1,0:T(8,128)(2,1)S(1)}, u32[]{:S(2)}, u32[]{:S(2)}) %collective-permute-start.1) | collective-permute-done | bytes 524320 | tf_op jit(solution)/shard_map/ppermute | solution.py:106
  59.8 3.0 collective-permute-start.13
  62.7 10.8 %collective-permute-done.2 = bf16[512,512]{1,0:T(8,128)(2,1)S(1)} collective-permute-done((bf16[512,512]{1,0:T(8,128)(2,1)S(1)}, bf16[512,512]{1,0:T(8,128)(2,1)S(1)}, u32[]{:S(2)}, u32[]{:S(2)}) %collective-permute-start.2) | collective-permute-done | bytes 524320 | tf_op jit(solution)/shard_map/ppermute | solution.py:106
  75.0 6.4 %collective-permute-start.19 = (bf16[512,512]{1,0:T(8,128)(2,1)S(1)}, bf16[512,512]{1,0:T(8,128)(2,1)}, u32[]{:S(2)}, u32[]{:S(2)}) collective-permute-start(bf16[512,512]{1,0:T(8,128)(2,1)S(1)} %get-tuple-element.37), channel_id=1, source_target_pairs={{0,8},{4,12},{8,0},{12,4},{16,24},{20,28},{24,16},{28,20},{1,9},{5... | collective-permute-start | bytes 1572872 | tf_op jit(solution)/shard_map/ppermute | solution.py:106
  81.4 5.0 %collective-permute-done.14 = bf16[512,512]{1,0:T(8,128)(2,1)S(1)} collective-permute-done((bf16[512,512]{1,0:T(8,128)(2,1)S(1)}, bf16[512,512]{1,0:T(8,128)(2,1)S(1)}, u32[]{:S(2)}, u32[]{:S(2)}) %collective-permute-start.14) | collective-permute-done | bytes 524320 | tf_op jit(solution)/shard_map/ppermute | solution.py:106
  91.0 16.3 %collective-permute-done.19 = bf16[512,512]{1,0:T(8,128)(2,1)} collective-permute-done((bf16[512,512]{1,0:T(8,128)(2,1)S(1)}, bf16[512,512]{1,0:T(8,128)(2,1)}, u32[]{:S(2)}, u32[]{:S(2)}) %collective-permute-start.19) | collective-permute-done | bytes 524320 | tf_op jit(solution)/shard_map/ppermute | solution.py:106
  110.9 5.7 %collective-permute-done.22 = bf16[512,512]{1,0:T(8,128)(2,1)S(1)} collective-permute-done((bf16[512,512]{1,0:T(8,128)(2,1)S(1)}, bf16[512,512]{1,0:T(8,128)(2,1)S(1)}, u32[]{:S(2)}, u32[]{:S(2)}) %collective-permute-start.22) | collective-permute-done | bytes 524320 | tf_op jit(solution)/shard_map/ppermute | solution.py:106
  116.6 8.2 %collective-permute-start.24 = (bf16[512,512]{1,0:T(8,128)(2,1)S(1)}, bf16[512,512]{1,0:T(8,128)(2,1)}, u32[]{:S(2)}, u32[]{:S(2)}) collective-permute-start(bf16[512,512]{1,0:T(8,128)(2,1)S(1)} %get-tuple-element.39), channel_id=1, source_target_pairs={{0,16},{4,20},{8,24},{12,28},{16,0},{20,4},{24,8},{28,12},{1,17},{... | collective-permute-start | bytes 1572872 | tf_op jit(solution)/shard_map/ppermute | solution.py:106
  125.6 8.3 %collective-permute-done.18 = bf16[512,512]{1,0:T(8,128)(2,1)} collective-permute-done((bf16[512,512]{1,0:T(8,128)(2,1)}, bf16[512,512]{1,0:T(8,128)(2,1)}, u32[]{:S(2)}, u32[]{:S(2)}) %collective-permute-start.18) | collective-permute-done | bytes 524320 | tf_op jit(solution)/shard_map/ppermute | solution.py:106
  134.2 14.2 %collective-permute-done.24 = bf16[512,512]{1,0:T(8,128)(2,1)} collective-permute-done((bf16[512,512]{1,0:T(8,128)(2,1)S(1)}, bf16[512,512]{1,0:T(8,128)(2,1)}, u32[]{:S(2)}, u32[]{:S(2)}) %collective-permute-start.24) | collective-permute-done | bytes 524320 | tf_op jit(solution)/shard_map/ppermute | solution.py:106
  152.5 9.3 %collective-permute-done.21 = bf16[512,512]{1,0:T(8,128)(2,1)S(1)} collective-permute-done((bf16[512,512]{1,0:T(8,128)(2,1)S(1)}, bf16[512,512]{1,0:T(8,128)(2,1)S(1)}, u32[]{:S(2)}, u32[]{:S(2)}) %collective-permute-start.21) | collective-permute-done | bytes 524320 | tf_op jit(solution)/shard_map/ppermute | solution.py:106
  163.0 3.2 collective-permute-done.28.q_ids
  169.1 9.7 %select_select_fusion.bias = f32[8,640,128]{2,1,0:T(8,128)S(1)} fusion(f32[8]{0:T(128)S(1)} %get-tuple-element.54, f32[8]{0:T(128)S(1)} %get-tuple-element.55, f32[8]{0:T(128)S(1)} %get-tuple-element.56, f32[8]{0:T(128)S(1)} %get-tuple-element.57, f32[8]{0:T(128)S(1)} %get-tuple-element.58, f32[8]{0:T(128)S(1)} %get-tuple-element.59, ...), kind=kLoop, calls=%fused_computation.30 | loop fusion | flops 20971520 | bytes 5243904 | tf_op jit(solution)/shard_map/jit(_where)/select_n | solution.py:35
  183.7 18.8 %multiply_reduce_fusion = (f32[1280]{0:T(1024)S(1)}, bf16[1280,4096]{1,0:T(8,128)(2,1)S(1)}) fusion(bf16[640,1024]{1,0:T(8,128)(2,1)} %collective-permute-done.12, bf16[640,1024]{1,0:T(8,128)(2,1)} %collective-permute-done.11, bf16[640,1024]{1,0:T(8,128)(2,1)} %collective-permute-done.10, bf16[640,1024]{1,0:T(8,128)(2,1)} %collective-permute-done.9, ...), kind=kLoop, calls=%fused_computation | loop fusion | flops 99613440 | bytes 20976640 | tf_op jit(solution)/shard_map/reduce_sum | solution.py:161
  202.5 4.0 multiply_convert_fusion.7
  206.6 4.6 %fusion.12 = f32[512,1280]{1,0:T(8,128)S(1)} fusion(bf16[512,512]{1,0:T(8,128)(2,1)} %collective-permute-done.20, bf16[512,512]{1,0:T(8,128)(2,1)} %collective-permute-done.19, bf16[512,512]{1,0:T(8,128)(2,1)} %collective-permute-done.18, bf16[512,512]{1,0:T(8,128)(2,1)} %collective-permute-done.13, bf16[1280,512]{1,0:T(8,128)(2,1)S(1)} %get-tuple-element.94, ...), kind=kOutput, calls=%fused_computation.38 | convolution fusion | flops 2713714688 | bytes 9961472 | tf_op jit(solution)/shard_map/td,df->ft/dot_general | solution.py:182
  218.3 3.0 fusion.2.keys
  222.9 4.5 %fusion.42 = f32[512,1280]{1,0:T(8,128)S(1)} fusion(bf16[512,512]{1,0:T(8,128)(2,1)S(1)} %collective-permute-done.27, bf16[512,512]{1,0:T(8,128)(2,1)} %collective-permute-done.26, bf16[512,512]{1,0:T(8,128)(2,1)} %collective-permute-done.25, bf16[512,512]{1,0:T(8,128)(2,1)} %collective-permute-done.24, bf16[1280,512]{1,0:T(8,128)(2,1)S(1)} %get-tuple-element.94, ...), kind=kOutput, calls=%fused_computation.68 | convolution fusion | flops 2713714688 | bytes 9961472 | tf_op jit(solution)/shard_map/td,df->ft/dot_general | solution.py:182
  227.5 12.7 %collective-permute-done.29 = bf16[512,512]{1,0:T(8,128)(2,1)} collective-permute-done((bf16[512,512]{1,0:T(8,128)(2,1)S(1)}, bf16[512,512]{1,0:T(8,128)(2,1)}, u32[]{:S(2)}, u32[]{:S(2)}) %collective-permute-start.29) | collective-permute-done | bytes 524320 | tf_op jit(solution)/shard_map/ppermute | solution.py:106
  240.2 22.9 %collective-permute-start.30 = (bf16[512,512]{1,0:T(8,128)(2,1)S(1)}, bf16[512,512]{1,0:T(8,128)(2,1)S(1)}, u32[]{:S(2)}, u32[]{:S(2)}) collective-permute-start(bf16[512,512]{1,0:T(8,128)(2,1)S(1)} %copy-done.17), channel_id=1, source_target_pairs={{0,8},{4,12},{8,0},{12,4},{16,24},{20,28},{24,16},{28,20},{1,9},{5... | collective-permute-start | bytes 1572872 | tf_op jit(solution)/shard_map/ppermute | solution.py:106
  266.2 10.9 %shard_map.82 = bf16[512,640]{1,0:T(8,128)(2,1)S(1)} custom-call(s32[1,640]{1,0:T(1,128)S(1)} %copy-done.4, s32[640,128]{1,0:T(8,128)S(1)} %broadcast_in_dim.424.k_ids, f32[8,640,128]{2,1,0:T(8,128)S(1)} %select_select_fusion.bias, bf16[512,1280]{1,0:T(8,128)(2,1)S(1)} %fusion.1.queries, bf16[1280,512]{1,0:T(8,128)(2,1)S(1)} %fusion.2.keys, ...), custom_call_target="tpu_custom_call" | custom-call | flops 1677721600 | bytes 5242880 | tf_op jit(solution)/shard_map/pallas_call | solution.py:69
  277.2 11.1 %shard_map.83 = bf16[512,640]{1,0:T(8,128)(2,1)S(1)} custom-call(s32[1,640]{1,0:T(1,128)S(1)} %collective-permute-done.28.q_ids, s32[640,128]{1,0:T(8,128)S(1)} %broadcast_in_dim.523.k_ids, f32[8,640,128]{2,1,0:T(8,128)S(1)} %select_select_fusion.bias, bf16[512,1280]{1,0:T(8,128)(2,1)S(1)} %fusion.1.queries, bf16[1280,512]{1,0:T(8,128)(2,1)S(1)} %fusion.2.keys, ...), custom_call_target="tpu_custom_call" | custom-call | flops 1677721600 | bytes 5242880 | tf_op jit(solution)/shard_map/pallas_call | solution.py:69
  292.7 9.3 %collective-permute-done.37 = bf16[512,512]{1,0:T(8,128)(2,1)S(1)} collective-permute-done((bf16[512,512]{1,0:T(8,128)(2,1)S(1)}, bf16[512,512]{1,0:T(8,128)(2,1)S(1)}, u32[]{:S(2)}, u32[]{:S(2)}) %collective-permute-start.37) | collective-permute-done | bytes 524320 | tf_op jit(solution)/shard_map/ppermute | solution.py:106
  305.2 11.9 %collective-permute-done.38 = bf16[512,512]{1,0:T(8,128)(2,1)S(1)} collective-permute-done((bf16[512,512]{1,0:T(8,128)(2,1)}, bf16[512,512]{1,0:T(8,128)(2,1)S(1)}, u32[]{:S(2)}, u32[]{:S(2)}) %collective-permute-start.38) | collective-permute-done | bytes 524320 | tf_op jit(solution)/shard_map/ppermute | solution.py:106
  317.1 9.0 %collective-permute-done.39 = bf16[512,512]{1,0:T(8,128)(2,1)S(1)} collective-permute-done((bf16[512,512]{1,0:T(8,128)(2,1)}, bf16[512,512]{1,0:T(8,128)(2,1)S(1)}, u32[]{:S(2)}, u32[]{:S(2)}) %collective-permute-start.39) | collective-permute-done | bytes 524320 | tf_op jit(solution)/shard_map/ppermute | solution.py:106
  331.0 3.4 fusion.4
  341.2 24.6 %collective-permute-done.34 = bf16[1280,512]{0,1:T(8,128)(2,1)} collective-permute-done((bf16[1280,512]{0,1:T(8,128)(2,1)}, bf16[1280,512]{0,1:T(8,128)(2,1)}, u32[]{:S(2)}, u32[]{:S(2)}) %collective-permute-start.34) | collective-permute-done | bytes 1310752 | tf_op jit(solution)/shard_map/ppermute | solution.py:106
  376.6 10.8 %collective-permute-done.35 = bf16[640,512]{0,1:T(8,128)(2,1)} collective-permute-done((bf16[640,512]{0,1:T(8,128)(2,1)}, bf16[640,512]{0,1:T(8,128)(2,1)}, u32[]{:S(2)}, u32[]{:S(2)}) %collective-permute-start.35) | collective-permute-done | bytes 655392 | tf_op jit(solution)/shard_map/ppermute | solution.py:106
  388.6 11.6 %collective-permute-done.41 = bf16[640,512]{0,1:T(8,128)(2,1)} collective-permute-done((bf16[640,512]{0,1:T(8,128)(2,1)}, bf16[640,512]{0,1:T(8,128)(2,1)}, u32[]{:S(2)}, u32[]{:S(2)}) %collective-permute-start.41) | collective-permute-done | bytes 655392 | tf_op jit(solution)/shard_map/ppermute | solution.py:106
  403.9 3.6 add_convert_fusion
  (198 shorter events, 80.5 us)
Async XLA Ops:
  0.0 88.0 %collective-permute-start.9 = (bf16[640,1024]{1,0:T(8,128)(2,1)}, bf16[640,1024]{1,0:T(8,128)(2,1)}, u32[]{:S(2)}, u32[]{:S(2)}) collective-permute-start(bf16[640,1024]{1,0:T(8,128)(2,1)} %param.8), channel_id=1, source_target_pairs={{0,8},{4,12},{8,0},{12,4},{16,24},{20,28},{24,16},{28,20},{1,9},{5... | collective-permute-start | bytes 3932168 | tf_op jit(solution)/shard_map/ppermute | solution.py:106
  4.4 39.4 %collective-permute-start.3 = (bf16[512,512]{1,0:T(8,128)(2,1)S(1)}, bf16[512,512]{1,0:T(8,128)(2,1)S(1)}, u32[]{:S(2)}, u32[]{:S(2)}) collective-permute-start(bf16[512,512]{1,0:T(8,128)(2,1)S(1)} %get-tuple-element.102), channel_id=1, source_target_pairs={{0,16},{4,20},{8,24},{12,28},{16,0},{20,4},{24,8},{28,12},{1,17},{... | collective-permute-start | bytes 1572872 | tf_op jit(solution)/shard_map/ppermute | solution.py:106
  7.2 36.6 %collective-permute-start = (bf16[512,512]{1,0:T(8,128)(2,1)S(1)}, bf16[512,512]{1,0:T(8,128)(2,1)S(1)}, u32[]{:S(2)}, u32[]{:S(2)}) collective-permute-start(bf16[512,512]{1,0:T(8,128)(2,1)S(1)} %get-tuple-element.32), channel_id=1, source_target_pairs={{0,4},{4,0},{8,12},{12,8},{16,20},{20,16},{24,28},{28,24},{1,5},{5... | collective-permute-start | bytes 1572872 | tf_op jit(solution)/shard_map/ppermute | solution.py:106
  8.7 48.1 %collective-permute-start.1 = (bf16[512,512]{1,0:T(8,128)(2,1)S(1)}, bf16[512,512]{1,0:T(8,128)(2,1)S(1)}, u32[]{:S(2)}, u32[]{:S(2)}) collective-permute-start(bf16[512,512]{1,0:T(8,128)(2,1)S(1)} %get-tuple-element.33), channel_id=1, source_target_pairs={{0,24},{4,28},{8,16},{12,20},{16,8},{20,12},{24,0},{28,4},{1,25},{... | collective-permute-start | bytes 1572872 | tf_op jit(solution)/shard_map/ppermute | solution.py:106
  9.1 49.2 %collective-permute-start.15 = (bf16[512,512]{1,0:T(8,128)(2,1)S(1)}, bf16[512,512]{1,0:T(8,128)(2,1)S(1)}, u32[]{:S(2)}, u32[]{:S(2)}) collective-permute-start(bf16[512,512]{1,0:T(8,128)(2,1)S(1)} %get-tuple-element.102), channel_id=1, source_target_pairs={{0,4},{4,0},{8,12},{12,8},{16,20},{20,16},{24,28},{28,24},{1,5},{5... | collective-permute-start | bytes 1572872 | tf_op jit(solution)/shard_map/ppermute | solution.py:106
  58.3 16.7 %collective-permute-start.16 = (bf16[512,512]{1,0:T(8,128)(2,1)S(1)}, bf16[512,512]{1,0:T(8,128)(2,1)S(1)}, u32[]{:S(2)}, u32[]{:S(2)}) collective-permute-start(bf16[512,512]{1,0:T(8,128)(2,1)S(1)} %collective-permute-done.1), channel_id=1, source_target_pairs={{0,4},{4,0},{8,12},{12,8},{16,20},{20,16},{24,28},{28,24},{1,5},{5... | collective-permute-start | bytes 1572872 | tf_op jit(solution)/shard_map/ppermute | solution.py:106
  59.8 26.6 %collective-permute-start.14 = (bf16[512,512]{1,0:T(8,128)(2,1)S(1)}, bf16[512,512]{1,0:T(8,128)(2,1)S(1)}, u32[]{:S(2)}, u32[]{:S(2)}) collective-permute-start(bf16[512,512]{1,0:T(8,128)(2,1)S(1)} %get-tuple-element.33), channel_id=1, source_target_pairs={{0,8},{4,12},{8,0},{12,4},{16,24},{20,28},{24,16},{28,20},{1,9},{5... | collective-permute-start | bytes 1572872 | tf_op jit(solution)/shard_map/ppermute | solution.py:106
  59.8 49.1 %collective-permute-start.13 = (bf16[512,512]{1,0:T(8,128)(2,1)S(1)}, bf16[512,512]{1,0:T(8,128)(2,1)}, u32[]{:S(2)}, u32[]{:S(2)}) collective-permute-start(bf16[512,512]{1,0:T(8,128)(2,1)S(1)} %get-tuple-element.32), channel_id=1, source_target_pairs={{0,16},{4,20},{8,24},{12,28},{16,0},{20,4},{24,8},{28,12},{1,17},{... | collective-permute-start | bytes 1572872 | tf_op jit(solution)/shard_map/ppermute | solution.py:106
  75.0 32.3 %collective-permute-start.19 = (bf16[512,512]{1,0:T(8,128)(2,1)S(1)}, bf16[512,512]{1,0:T(8,128)(2,1)}, u32[]{:S(2)}, u32[]{:S(2)}) collective-permute-start(bf16[512,512]{1,0:T(8,128)(2,1)S(1)} %get-tuple-element.37), channel_id=1, source_target_pairs={{0,8},{4,12},{8,0},{12,4},{16,24},{20,28},{24,16},{28,20},{1,9},{5... | collective-permute-start | bytes 1572872 | tf_op jit(solution)/shard_map/ppermute | solution.py:106
  86.4 23.0 %collective-permute-start.17 = (bf16[512,512]{1,0:T(8,128)(2,1)S(1)}, bf16[512,512]{1,0:T(8,128)(2,1)S(1)}, u32[]{:S(2)}, u32[]{:S(2)}) collective-permute-start(bf16[512,512]{1,0:T(8,128)(2,1)S(1)} %collective-permute-done.14), channel_id=1, source_target_pairs={{0,4},{4,0},{8,12},{12,8},{16,20},{20,16},{24,28},{28,24},{1,5},{5... | collective-permute-start | bytes 1572872 | tf_op jit(solution)/shard_map/ppermute | solution.py:106
  88.1 28.5 %collective-permute-start.22 = (bf16[512,512]{1,0:T(8,128)(2,1)S(1)}, bf16[512,512]{1,0:T(8,128)(2,1)S(1)}, u32[]{:S(2)}, u32[]{:S(2)}) collective-permute-start(bf16[512,512]{1,0:T(8,128)(2,1)S(1)} %get-tuple-element.44), channel_id=1, source_target_pairs={{0,24},{4,28},{8,16},{12,20},{16,8},{20,12},{24,0},{28,4},{1,25},{... | collective-permute-start | bytes 1572872 | tf_op jit(solution)/shard_map/ppermute | solution.py:106
  89.5 76.7 %collective-permute-start.7 = (bf16[640,1024]{1,0:T(8,128)(2,1)}, bf16[640,1024]{1,0:T(8,128)(2,1)}, u32[]{:S(2)}, u32[]{:S(2)}) collective-permute-start(bf16[640,1024]{1,0:T(8,128)(2,1)} %param.8), channel_id=1, source_target_pairs={{0,2},{1,3},{2,0},{3,1},{4,6},{5,7},{6,4},{7,5},{8,10},{9,11},{10,... | collective-permute-start | bytes 3932168 | tf_op jit(solution)/shard_map/ppermute | solution.py:106
  107.3 59.5 %collective-permute-start.11 = (bf16[640,1024]{1,0:T(8,128)(2,1)}, bf16[640,1024]{1,0:T(8,128)(2,1)}, u32[]{:S(2)}, u32[]{:S(2)}) collective-permute-start(bf16[640,1024]{1,0:T(8,128)(2,1)} %collective-permute-done.9), channel_id=1, source_target_pairs={{0,2},{1,3},{2,0},{3,1},{4,6},{5,7},{6,4},{7,5},{8,10},{9,11},{10,... | collective-permute-start | bytes 3932168 | tf_op jit(solution)/shard_map/ppermute | solution.py:106
  109.4 24.5 %collective-permute-start.18 = (bf16[512,512]{1,0:T(8,128)(2,1)}, bf16[512,512]{1,0:T(8,128)(2,1)}, u32[]{:S(2)}, u32[]{:S(2)}) collective-permute-start(bf16[512,512]{1,0:T(8,128)(2,1)} %collective-permute-done.13), channel_id=1, source_target_pairs={{0,4},{4,0},{8,12},{12,8},{16,20},{20,16},{24,28},{28,24},{1,5},{5... | collective-permute-start | bytes 1572872 | tf_op jit(solution)/shard_map/ppermute | solution.py:106
  116.6 31.8 %collective-permute-start.24 = (bf16[512,512]{1,0:T(8,128)(2,1)S(1)}, bf16[512,512]{1,0:T(8,128)(2,1)}, u32[]{:S(2)}, u32[]{:S(2)}) collective-permute-start(bf16[512,512]{1,0:T(8,128)(2,1)S(1)} %get-tuple-element.39), channel_id=1, source_target_pairs={{0,16},{4,20},{8,24},{12,28},{16,0},{20,4},{24,8},{28,12},{1,17},{... | collective-permute-start | bytes 1572872 | tf_op jit(solution)/shard_map/ppermute | solution.py:106
  125.4 41.4 %collective-permute-start.26 = (bf16[512,512]{1,0:T(8,128)(2,1)S(1)}, bf16[512,512]{1,0:T(8,128)(2,1)}, u32[]{:S(2)}, u32[]{:S(2)}) collective-permute-start(bf16[512,512]{1,0:T(8,128)(2,1)S(1)} %get-tuple-element.44), channel_id=1, source_target_pairs={{0,8},{4,12},{8,0},{12,4},{16,24},{20,28},{24,16},{28,20},{1,9},{5... | collective-permute-start | bytes 1572872 | tf_op jit(solution)/shard_map/ppermute | solution.py:106
  133.9 34.4 %collective-permute-start.23 = (bf16[512,512]{1,0:T(8,128)(2,1)S(1)}, bf16[512,512]{1,0:T(8,128)(2,1)S(1)}, u32[]{:S(2)}, u32[]{:S(2)}) collective-permute-start(bf16[512,512]{1,0:T(8,128)(2,1)S(1)} %collective-permute-done.22), channel_id=1, source_target_pairs={{0,4},{4,0},{8,12},{12,8},{16,20},{20,16},{24,28},{28,24},{1,5},{5... | collective-permute-start | bytes 1572872 | tf_op jit(solution)/shard_map/ppermute | solution.py:106
  166.2 17.4 %collective-permute-start.10 = (bf16[640,1024]{1,0:T(8,128)(2,1)}, bf16[640,1024]{1,0:T(8,128)(2,1)}, u32[]{:S(2)}, u32[]{:S(2)}) collective-permute-start(bf16[640,1024]{1,0:T(8,128)(2,1)} %collective-permute-done.9), channel_id=1, source_target_pairs={{0,1},{1,0},{2,3},{3,2},{4,5},{5,4},{6,7},{7,6},{8,9},{9,8},{10,11... | collective-permute-start | bytes 3932168 | tf_op jit(solution)/shard_map/ppermute | solution.py:106
  166.8 16.9 %collective-permute-start.8 = (bf16[640,1024]{1,0:T(8,128)(2,1)}, bf16[640,1024]{1,0:T(8,128)(2,1)}, u32[]{:S(2)}, u32[]{:S(2)}) collective-permute-start(bf16[640,1024]{1,0:T(8,128)(2,1)} %collective-permute-done.7), channel_id=1, source_target_pairs={{0,1},{1,0},{2,3},{3,2},{4,5},{5,4},{6,7},{7,6},{8,9},{9,8},{10,11... | collective-permute-start | bytes 3932168 | tf_op jit(solution)/shard_map/ppermute | solution.py:106
  181.6 41.3 %collective-permute-start.27 = (bf16[512,512]{1,0:T(8,128)(2,1)}, bf16[512,512]{1,0:T(8,128)(2,1)S(1)}, u32[]{:S(2)}, u32[]{:S(2)}) collective-permute-start(bf16[512,512]{1,0:T(8,128)(2,1)} %collective-permute-done.26), channel_id=1, source_target_pairs={{0,4},{4,0},{8,12},{12,8},{16,20},{20,16},{24,28},{28,24},{1,5},{5... | collective-permute-start | bytes 1572872 | tf_op jit(solution)/shard_map/ppermute | solution.py:106
  182.9 119.9 %collective-permute-start.36 = (bf16[512,512]{1,0:T(8,128)(2,1)}, bf16[512,512]{1,0:T(8,128)(2,1)}, u32[]{:S(2)}, u32[]{:S(2)}) collective-permute-start(bf16[512,512]{1,0:T(8,128)(2,1)} %get-tuple-element.48), channel_id=1, source_target_pairs={{0,4},{4,0},{8,12},{12,8},{16,20},{20,16},{24,28},{28,24},{1,5},{5... | collective-permute-start | bytes 1572872 | tf_op jit(solution)/shard_map/ppermute | solution.py:106
  214.2 74.9 %collective-permute-start.31 = (bf16[512,512]{1,0:T(8,128)(2,1)}, bf16[512,512]{1,0:T(8,128)(2,1)}, u32[]{:S(2)}, u32[]{:S(2)}) collective-permute-start(bf16[512,512]{1,0:T(8,128)(2,1)} %get-tuple-element.48), channel_id=1, source_target_pairs={{0,16},{4,20},{8,24},{12,28},{16,0},{20,4},{24,8},{28,12},{1,17},{... | collective-permute-start | bytes 1572872 | tf_op jit(solution)/shard_map/ppermute | solution.py:106
  221.4 18.8 %collective-permute-start.29 = (bf16[512,512]{1,0:T(8,128)(2,1)S(1)}, bf16[512,512]{1,0:T(8,128)(2,1)}, u32[]{:S(2)}, u32[]{:S(2)}) collective-permute-start(bf16[512,512]{1,0:T(8,128)(2,1)S(1)} %copy-done.17), channel_id=1, source_target_pairs={{0,24},{4,28},{8,16},{12,20},{16,8},{20,12},{24,0},{28,4},{1,25},{... | collective-permute-start | bytes 1572872 | tf_op jit(solution)/shard_map/ppermute | solution.py:106
  240.2 48.2 %collective-permute-start.30 = (bf16[512,512]{1,0:T(8,128)(2,1)S(1)}, bf16[512,512]{1,0:T(8,128)(2,1)S(1)}, u32[]{:S(2)}, u32[]{:S(2)}) collective-permute-start(bf16[512,512]{1,0:T(8,128)(2,1)S(1)} %copy-done.17), channel_id=1, source_target_pairs={{0,8},{4,12},{8,0},{12,4},{16,24},{20,28},{24,16},{28,20},{1,9},{5... | collective-permute-start | bytes 1572872 | tf_op jit(solution)/shard_map/ppermute | solution.py:106
  292.7 38.3 %collective-permute-start.33 = (bf16[1280,512]{0,1:T(8,128)(2,1)}, bf16[1280,512]{0,1:T(8,128)(2,1)}, u32[]{:S(2)}, u32[]{:S(2)}) collective-permute-start(bf16[1280,512]{0,1:T(8,128)(2,1)} %convolution_convert_fusion.2), channel_id=1, source_target_pairs={{0,1},{1,0},{2,3},{3,2},{4,5},{5,4},{6,7},{7,6},{8,9},{9,8},{10,11... | collective-permute-start | bytes 3932168 | tf_op jit(solution)/shard_map/ppermute | solution.py:106
  302.7 23.4 %collective-permute-start.39 = (bf16[512,512]{1,0:T(8,128)(2,1)}, bf16[512,512]{1,0:T(8,128)(2,1)S(1)}, u32[]{:S(2)}, u32[]{:S(2)}) collective-permute-start(bf16[512,512]{1,0:T(8,128)(2,1)} %collective-permute-done.29), channel_id=1, source_target_pairs={{0,4},{4,0},{8,12},{12,8},{16,20},{20,16},{24,28},{28,24},{1,5},{5... | collective-permute-start | bytes 1572872 | tf_op jit(solution)/shard_map/ppermute | solution.py:106
  334.3 31.5 %collective-permute-start.34 = (bf16[1280,512]{0,1:T(8,128)(2,1)}, bf16[1280,512]{0,1:T(8,128)(2,1)}, u32[]{:S(2)}, u32[]{:S(2)}) collective-permute-start(bf16[1280,512]{0,1:T(8,128)(2,1)} %fusion.4), channel_id=1, source_target_pairs={{0,2},{1,3},{2,0},{3,1},{4,6},{5,7},{6,4},{7,5},{8,10},{9,11},{10,... | collective-permute-start | bytes 3932168 | tf_op jit(solution)/shard_map/ppermute | solution.py:106
  337.8 32.2 %collective-permute-start.40 = (bf16[1280,512]{0,1:T(8,128)(2,1)}, bf16[1280,512]{0,1:T(8,128)(2,1)}, u32[]{:S(2)}, u32[]{:S(2)}) collective-permute-start(bf16[1280,512]{0,1:T(8,128)(2,1)} %convolution_convert_fusion.1), channel_id=1, source_target_pairs={{0,1},{1,0},{2,3},{3,2},{4,5},{5,4},{6,7},{7,6},{8,9},{9,8},{10,11... | collective-permute-start | bytes 3932168 | tf_op jit(solution)/shard_map/ppermute | solution.py:106
  340.5 34.3 %collective-permute-start.43 = (bf16[640,512]{0,1:T(8,128)(2,1)S(1)}, bf16[640,512]{0,1:T(8,128)(2,1)S(1)}, u32[]{:S(2)}, u32[]{:S(2)}) collective-permute-start(bf16[640,512]{0,1:T(8,128)(2,1)S(1)} %slice.207), channel_id=1, source_target_pairs={{0,8},{4,12},{8,0},{12,4},{16,24},{20,28},{24,16},{28,20},{1,9},{5... | collective-permute-start | bytes 1966088 | tf_op jit(solution)/shard_map/ppermute | solution.py:106
  369.4 18.0 %collective-permute-start.35 = (bf16[640,512]{0,1:T(8,128)(2,1)}, bf16[640,512]{0,1:T(8,128)(2,1)}, u32[]{:S(2)}, u32[]{:S(2)}) collective-permute-start(bf16[640,512]{0,1:T(8,128)(2,1)} %slice.209), channel_id=1, source_target_pairs={{0,8},{4,12},{8,0},{12,4},{16,24},{20,28},{24,16},{28,20},{1,9},{5... | collective-permute-start | bytes 1966088 | tf_op jit(solution)/shard_map/ppermute | solution.py:106
  373.5 26.7 %collective-permute-start.41 = (bf16[640,512]{0,1:T(8,128)(2,1)}, bf16[640,512]{0,1:T(8,128)(2,1)}, u32[]{:S(2)}, u32[]{:S(2)}) collective-permute-start(bf16[640,512]{0,1:T(8,128)(2,1)} %slice.208), channel_id=1, source_target_pairs={{0,8},{4,12},{8,0},{12,4},{16,24},{20,28},{24,16},{28,20},{1,9},{5... | collective-permute-start | bytes 1966088 | tf_op jit(solution)/shard_map/ppermute | solution.py:106
  375.0 25.1 %collective-permute-start.44 = (bf16[640,512]{0,1:T(8,128)(2,1)S(1)}, bf16[640,512]{0,1:T(8,128)(2,1)}, u32[]{:S(2)}, u32[]{:S(2)}) collective-permute-start(bf16[640,512]{0,1:T(8,128)(2,1)S(1)} %fusion.50), channel_id=1, source_target_pairs={{0,2},{1,3},{2,0},{3,1},{4,6},{5,7},{6,4},{7,5},{8,10},{9,11},{10,... | collective-permute-start | bytes 1966088 | tf_op jit(solution)/shard_map/ppermute | solution.py:106
  (59 other events, 1496.5 us)

commit v3 on v2

--- a/solution.py
+++ b/solution.py
@@ -105,108 +105,120 @@
         count = n_batch if axis == "batch" else n_hidden
         return lax.ppermute(value, axis, [(i, i ^ step) for i in range(count)])
 
-    def halves(weight, axis):
+    planes = n_batch // 4
+    plane = place >> 2
+    near_line = []
+
+    def paired(weight, axis, *earlier):
         size = weight.shape[axis] // 2
-        return [
+        kept, given = [
             lax.dynamic_slice_in_dim(weight, side * size, size, axis)
             for side in (parity, 1 - parity)
         ]
-
-    far_steps = list(range(n_batch - 2, 2, -2))
-    far_line, near_line = [], []
-
-    def paced(value, step, line, *earlier):
-        waits = tuple(line[-2:-1]) + earlier
+        if earlier:
+            given = after(given, earlier)
+        return jnp.concatenate([kept, swap(given, 2)], axis=0)
+
+    def along_z(pair):
+        groups = [[r + 4 * i for i in range(planes)] for r in range(4)]
+        return lax.all_gather(pair, "batch", axis=0, tiled=True, axis_index_groups=groups)
+
+    def along_x(value, *earlier):
+        waits = tuple(near_line[-2:-1]) + earlier
         if waits:
             value = after(value, waits)
-        received = swap(value, step)
-        line.append(received)
+        received = swap(value, 1)
+        near_line.append(received)
         return received
 
-    def along_z(parts, earlier):
-        pieces = {0: parts[0]}
-        for step in far_steps:
-            pieces[step] = paced(parts[(step >> 1) & 1], step, far_line, *earlier.get(step, ()))
-        pieces[2] = swap(after(parts[1], far_line[-2:-1]), 2)
-        return pieces
-
-    def along_x(pieces, steps, earlier):
-        for step in steps:
-            pieces[step ^ 1] = paced(pieces[step], 1, near_line, *earlier.get(step, ()))
+    def others(whole):
+        size = whole.shape[0] // planes
+        rest = [
+            lax.dynamic_slice_in_dim(whole, (plane ^ k) * size, size, 0) for k in range(1, planes)
+        ]
+        return rest[0] if len(rest) == 1 else jnp.concatenate(rest, axis=0)
+
+    key_pair = paired(w_key, 1)
 
     peer_tokens = swap(tokens, 2)
     peer_ids = swap(segments, 2)
-
-    def all_features(part):
-        across = swap(part, 2, "hidden")
-        return [part, swap(part, 1, "hidden"), across, swap(across, 1, "hidden")]
-
-    gathered = [all_features(part) for part in (tokens, peer_tokens)]
-
-    key_pieces = along_z(halves(w_key, 1), {})
-    query_parts = halves(w_query, 1)
-    query_pieces = along_z(query_parts, {})
-    value_parts = halves(w_value, 1)
-    others = far_steps + [2]
-    along_x(key_pieces, [0], {})
-    along_x(query_pieces, [0], {})
-    along_x(key_pieces, others, {})
-    along_x(query_pieces, others, {})
+    across = jnp.concatenate([swap(tokens, 2, "hidden"), swap(peer_tokens, 2, "hidden")], axis=0)
+    held = jnp.concatenate([jnp.concatenate([tokens, peer_tokens], axis=0), across], axis=1)
+    other = swap(held, 1, "hidden")
+
+    query_pair = paired(w_query, 1, key_pair)
+    value_pair = paired(w_value, 1, query_pair)
+    out_pair = paired(w_out, 0, value_pair)
+    key_whole = along_z(key_pair)
+    query_whole = along_z(after(query_pair, key_pair))
+    value_whole = along_z(after(value_pair, query_pair))
+    out_whole = along_z(after(out_pair, value_pair))
+
+    key_near = along_x(key_pair)
+    query_near = along_x(query_pair)
+    key_rest = along_x(others(key_whole))
+    value_near = along_x(value_pair)
+    query_rest = along_x(others(query_whole))
 
     table = lax.dynamic_slice_in_dim(rel_bias, parity * heads, heads, 1)
     bias = bias_tiles(table)
 
-    both = jnp.concatenate([jnp.concatenate(parts, axis=1) for parts in gathered], axis=0)
-    wide = both.astype(jnp.float32)
-    scale = lax.rsqrt(jnp.mean(wide * wide, axis=1, keepdims=True) + norm_epsilon)
     depth = w_query.shape[0]
     per_block = own_width // depth
 
-    def normed_part(step):
-        source = place ^ step
-        where = ((source // per_block) ^ column) * own_width + (source % per_block) * depth
-        return (
-            lax.dynamic_slice_in_dim(both, where, depth, 1).astype(jnp.float32)
-            * scale
-            * lax.dynamic_slice_in_dim(ln_gain, source * depth, depth, 0)
-        ).astype(jnp.bfloat16)
-
-    order = [s for e in [0] + others for s in (e, e ^ 1)]
-    rounds = [order[: n_batch // 2], order[n_batch // 2 :]]
-    normed = [jnp.concatenate([normed_part(step) for step in steps], axis=1) for steps in rounds]
-
-    def project(pieces, form):
+    def squares(value):
+        value = value.astype(jnp.float32)
+        return jnp.sum(value * value, axis=1, keepdims=True)
+
+    scale = lax.rsqrt((squares(held) + squares(other)) / (2 * held.shape[1]) + norm_epsilon)
+
+    def normed_part(source):
+        block = (source // per_block) ^ column
+        where = (block >> 1) * own_width + (source % per_block) * depth
+        chosen = jnp.where(
+            (block & 1) == 0,
+            lax.dynamic_slice_in_dim(held, where, depth, 1),
+            lax.dynamic_slice_in_dim(other, where, depth, 1),
+        )
+        gain = lax.dynamic_slice_in_dim(ln_gain, source * depth, depth, 0)
+        return (chosen.astype(jnp.float32) * scale * gain).astype(jnp.bfloat16)
+
+    def normed_parts(sources):
+        return jnp.concatenate([normed_part(source) for source in sources], axis=1)
+
+    normed_near = normed_parts([place ^ (2 * j + 1) for j in range(2)])
+    normed_whole = normed_parts(
+        [4 * i + ((place & 3) ^ (2 * j)) for i in range(planes) for j in range(2)]
+    )
+    normed_rest = normed_parts(
+        [place ^ (4 * k + 2 * j + 1) for k in range(1, planes) for j in range(2)]
+    )
+
+    def project(near, whole, rest, form):
         total = None
-        for part, steps in zip(normed, rounds):
-            rows = jnp.concatenate([pieces[step] for step in steps], axis=0)
+        for part, rows in ((normed_near, near), (normed_whole, whole), (normed_rest, rest)):
             term = jnp.einsum(form, part, rows, preferred_element_type=jnp.float32)
             total = term if total is None else total + term
         return total.astype(jnp.bfloat16)
 
-    keys = project(key_pieces, "td,df->tf")
-    queries = project(query_pieces, "td,df->ft")
-    last = far_steps[-1]
-    value_pieces = along_z(value_parts, {last: (normed[0], normed[1])})
-    along_x(value_pieces, [0] + others, {})
-    values = project(value_pieces, "td,df->ft")
-
-    out_pieces = along_z(halves(w_out, 0), {far_steps[0]: (keys,), last: (queries,)})
-    along_x(out_pieces, [0], {})
+    keys = project(key_near, key_whole, key_rest, "td,df->tf")
+    queries = project(query_near, query_whole, query_rest, "td,df->ft")
+    value_rest = along_x(others(value_whole), keys)
+    values = project(value_near, value_whole, value_rest, "td,df->ft")
+    out_near = along_x(out_pair)
     attended = [attend(queries, keys, values, peer_ids[0], bias, 1, width)]
-    along_x(out_pieces, [2] + far_steps, {last: (attended[0],)})
+    out_rest = along_x(others(out_whole), attended[0])
     attended.insert(0, attend(queries, keys, values, segments[0], bias, 0, width))
     attended = jnp.concatenate(attended, axis=1)
 
     side = place & 1
     stripes = own_width // (2 * w_out.shape[1])
 
-    def sums(parity_step):
-        rows = jnp.concatenate([out_pieces[e ^ parity_step] for e in range(0, n_batch, 2)], axis=0)
-
+    def sums(rows, mine):
         def block(step):
             first = (column ^ step) * stripes
             chosen = [
-                lax.dynamic_slice_in_dim(rows, ((place >> 1) ^ (first + j)) * half, half, 0)
+                lax.dynamic_slice_in_dim(rows, (mine ^ (first + j)) * half, half, 0)
                 for j in range(stripes)
             ]
             chosen = chosen[0] if stripes == 1 else jnp.concatenate(chosen, axis=1)
@@ -219,10 +231,10 @@
     def send(value, step, axis="batch"):
         return swap(value.astype(jnp.bfloat16), step, axis).astype(jnp.float32)
 
-    here, there = sums(0)
+    here, there = sums(out_whole, parity)
     first = here + send(there, 2, "hidden")
     first = first[:length] + send(first[length:], 2)
-    here, there = sums(1)
+    here, there = sums(jnp.concatenate([out_near, out_rest], axis=0), place >> 1)
     there = there[:length] + send(there[length:], 2)
     second = here[:length] + send(here[length:], 2) + send(there, 2, "hidden")
 

time: 411 us -> 451 us (1.097)
  waiting for transfers between devices: 209 us -> 262 us
  starting transfers between devices: 80 us -> 27.6 us
  between operations: 1.33 us -> 14.3 us
  other arithmetic: 43.3 us -> 52.6 us
  local copies, waits for them, and re-layouts: 12.8 us -> 21.8 us
  matrix products: 39.5 us -> 44.7 us
    ppermute x45 -> x26, starting transfers between devices: 80 us -> 27.5 us  [swap(): return lax.ppermute(value, axis, [(i, i ^ step) for i in range(count)])]
    all_gather x0 -> x4, waiting for transfers between devices: none -> 38.6 us  [along_z(): lax.all_gather(pair, 'batch', axis=0, tiled=True, axis_index_groups=groups)]
    ppermute x45 -> x26, waiting for transfers between devices: 209 us -> 223 us  [swap(): return lax.ppermute(value, axis, [(i, i ^ step) for i in range(count)])]
    dynamic_slice x5 -> x9, local copies, waits for them, and re-layouts: 3.82 us -> 11.7 us  [the longest x4 8.18 us: others(): lax.dynamic_slice_in_dim(whole, (plane ^ k) * size, size, 0)]
    convert_element_type x1 -> x2, other arithmetic: 4.03 us -> 10.9 us  [normed_part(): return (chosen.astype(jnp.float32) * scale * gain).astype(jnp.bfloat16)]
    reduce_sum x1 -> x2, other arithmetic: 18.8 us -> 15.8 us  [squares(): return jnp.sum(value * value, axis=1, keepdims=True)]
    dot_general x6 -> x9, matrix products: 20.9 us -> 23.8 us  [project(): term = jnp.einsum(form, part, rows, preferred_element_type=jnp.float32)]
  transfers between devices with their start and end apart: 45 -> 30, of which waited for: 17 -> 14; matrix products, arithmetic and copies ran while one was open for 21% -> 24% of each run, Pallas kernels for 5% -> 5%
where the time goes in v3:
time: 451 us; the launch traced here: 445 us
  waiting for transfers between devices  262 us (58%)
  other arithmetic  52.6 us (12%)
  matrix products  44.7 us (10%)
  starting transfers between devices  27.6 us (6%)
  Pallas kernels  22.1 us (5%)
  local copies, waits for them, and re-layouts  21.8 us (5%)
  between operations  14.3 us (3%)
    ppermute x26, waiting for transfers between devices, swap(): return lax.ppermute(value, axis, [(i, i ^ step) for i in range(count)])  223 us
    all_gather x4, waiting for transfers between devices, along_z(): lax.all_gather(pair, 'batch', axis=0, tiled=True, axis_index_groups=groups)  38.6 us
    ppermute x26, starting transfers between devices, swap(): return lax.ppermute(value, axis, [(i, i ^ step) for i in range(count)])  27.5 us
    dot_general x9, matrix products, project(): term = jnp.einsum(form, part, rows, preferred_element_type=jnp.float32)  23.8 us
    pallas_call x2, Pallas kernels, attend(): pl.pallas_call(functools.partial(attention_kernel, width), grid=(features...  22.1 us
    dot_general x8, matrix products, block(): jnp.einsum('ft,fc->tc', attended, chosen, preferred_element_type=jnp.floa...  20.9 us
    reduce_sum x2, other arithmetic, squares(): return jnp.sum(value * value, axis=1, keepdims=True)  15.8 us
    convert_element_type x2, other arithmetic, normed_part(): return (chosen.astype(jnp.float32) * scale * gain).astype(jnp.bfloat16)  10.9 us
  transfers between devices with their start and end apart: 30, of which 14 were waited for; matrix products, arithmetic and copies ran while one was open for 24% of the time, Pallas kernels for 5%

profile of v3, /device:TPU:0, one launch (start us, length us, event | category | flops | bytes accessed | tf_op | source)
XLA Modules:
  0.0 445.0 jit_solution(114575278143465495)
XLA Ops:
  7.9 3.1 collective-permute-start
  11.0 11.9 %collective-permute-done = bf16[512,512]{1,0:T(8,128)(2,1)S(1)} collective-permute-done((bf16[512,512]{1,0:T(8,128)(2,1)S(1)}, bf16[512,512]{1,0:T(8,128)(2,1)S(1)}, u32[]{:S(2)}, u32[]{:S(2)}) %collective-permute-start) | collective-permute-done | bytes 524320 | tf_op jit(solution)/shard_map/ppermute | solution.py:106
  29.2 47.1 %collective-permute-done.3 = bf16[640,1024]{1,0:T(8,128)(2,1)S(1)} collective-permute-done((bf16[640,1024]{1,0:T(8,128)(2,1)S(1)}, bf16[640,1024]{1,0:T(8,128)(2,1)S(1)}, u32[]{:S(2)}, u32[]{:S(2)}) %collective-permute-start.3) | collective-permute-done | bytes 1310752 | tf_op jit(solution)/shard_map/ppermute | solution.py:106
  77.6 10.2 %collective-permute-done.1 = bf16[512,512]{1,0:T(8,128)(2,1)S(1)} collective-permute-done((bf16[512,512]{1,0:T(8,128)(2,1)S(1)}, bf16[512,512]{1,0:T(8,128)(2,1)S(1)}, u32[]{:S(2)}, u32[]{:S(2)}) %collective-permute-start.1) | collective-permute-done | bytes 524320 | tf_op jit(solution)/shard_map/ppermute | solution.py:106
  88.9 10.8 %collective-permute-done.5 = bf16[640,1024]{1,0:T(8,128)(2,1)} collective-permute-done((bf16[640,1024]{1,0:T(8,128)(2,1)S(1)}, bf16[640,1024]{1,0:T(8,128)(2,1)}, u32[]{:S(2)}, u32[]{:S(2)}) %collective-permute-start.5) | collective-permute-done | bytes 1310752 | tf_op jit(solution)/shard_map/ppermute | solution.py:106
  99.7 12.2 %multiply_reduce_fusion.1 = (f32[1280]{0:T(1024)S(1)}, bf16[1280,2048]{1,0:T(8,128)(2,1)}) fusion(bf16[640,1024]{1,0:T(8,128)(2,1)} %collective-permute-done.5, bf16[640,1024]{1,0:T(8,128)(2,1)} %collective-permute-done.4, bf16[640,1024]{1,0:T(8,128)(2,1)S(1)} %collective-permute-done.3, bf16[640,1024]{1,0:T(8,128)(2,1)S(1)} %copy-done.5), kind=kLoop, calls=%fused_computation.1 | loop fusion | flops 28834560 | bytes 10490880 | tf_op jit(solution)/shard_map/reduce_sum | solution.py:171
  114.0 34.0 %collective-permute-done.10 = bf16[512,512]{1,0:T(8,128)(2,1)S(1)} collective-permute-done((bf16[512,512]{1,0:T(8,128)(2,1)S(1)}, bf16[512,512]{1,0:T(8,128)(2,1)S(1)}, u32[]{:S(2)}, u32[]{:S(2)}) %collective-permute-start.10) | collective-permute-done | bytes 524320 | tf_op jit(solution)/shard_map/ppermute | solution.py:106
  155.7 18.4 %collective-permute-done.7 = bf16[1024,512]{1,0:T(8,128)(2,1)} collective-permute-done((bf16[1024,512]{1,0:T(8,128)(2,1)S(1)}, bf16[1024,512]{1,0:T(8,128)(2,1)}, u32[]{:S(2)}, u32[]{:S(2)}) %collective-permute-start.7) | collective-permute-done | bytes 1048608 | tf_op jit(solution)/shard_map/ppermute | solution.py:106
  178.8 3.4 broadcast_compare_fusion.26
  185.1 15.1 %collective-permute-done.8 = bf16[1024,512]{1,0:T(8,128)(2,1)S(1)} collective-permute-done((bf16[1024,512]{1,0:T(8,128)(2,1)S(1)}, bf16[1024,512]{1,0:T(8,128)(2,1)S(1)}, u32[]{:S(2)}, u32[]{:S(2)}) %collective-permute-start.8) | collective-permute-done | bytes 1048608 | tf_op jit(solution)/shard_map/ppermute | solution.py:106
  201.7 10.7 %select_select_fusion.bias = f32[8,640,128]{2,1,0:T(8,128)S(1)} fusion(f32[8]{0:T(128)} %get-tuple-element.30, f32[8]{0:T(128)} %get-tuple-element.31, f32[8]{0:T(128)} %get-tuple-element.32, f32[8]{0:T(128)} %get-tuple-element.33, f32[8]{0:T(128)} %get-tuple-element.34, f32[8]{0:T(128)} %get-tuple-element.35, f32[8]{0:T(128)} %get-tuple-element.36, ...), kind=kLoop, calls=%fused_computation.35 | loop fusion | flops 20971520 | bytes 5243904 | tf_op jit(solution)/shard_map/jit(_where)/select_n | solution.py:35
  212.5 10.2 %collective-permute-done.2 = bf16[1024,512]{1,0:T(8,128)(2,1)} collective-permute-done((bf16[1024,512]{1,0:T(8,128)(2,1)}, bf16[1024,512]{1,0:T(8,128)(2,1)}, u32[]{:S(2)}, u32[]{:S(2)}) %collective-permute-start.2) | collective-permute-done | bytes 1048608 | tf_op jit(solution)/shard_map/ppermute | solution.py:106
  226.5 38.6 %all-gather.11.cloned.1.call-done = bf16[2048,512]{1,0:T(8,128)(2,1)} async-done(((bf16[1024,512]{1,0:T(8,128)(2,1)}), bf16[2048,512]{1,0:T(8,128)(2,1)}) %all-gather.11.cloned.1.call-update) | async-done | bytes 2097168 | tf_op jit(solution)/shard_map/all_gather | solution.py:124
  269.0 3.6 multiply_reduce_fusion
  272.6 4.2 multiply_convert_fusion.2
  276.9 6.6 %multiply_convert_fusion.7 = (bf16[1280,512]{1,0:T(8,128)(2,1)S(1)}, bf16[1280,512]{1,0:T(8,128)(2,1)S(1)}, bf16[1280,512]{1,0:T(8,128)(2,1)S(1)}, bf16[1280,512]{1,0:T(8,128)(2,1)S(1)}, bf16[1280,512]{1,0:T(8,128)(2,1)S(1)}) fusion(f32[512]{0:T(512)S(1)} %get-tuple-element.79, f32[1280]{0:T(1024)S(1)} %add_rsqrt_fusion, ...), kind=kLoop, calls=%fused_computation.34 | loop fusion | flops 16384000 | bytes 19676184 | tf_op jit(solution)/shard_map/convert_element_type | solution.py:184
  283.6 2.9 fusion.48
  288.1 3.1 fusion.5.keys
  291.9 2.9 fusion.49
  297.7 3.0 fusion.6.queries
  300.7 3.2 fusion.47
  303.9 11.9 %collective-permute-done.12 = bf16[1024,512]{1,0:T(8,128)(2,1)S(1)} collective-permute-done((bf16[1024,512]{1,0:T(8,128)(2,1)S(1)}, bf16[1024,512]{1,0:T(8,128)(2,1)S(1)}, u32[]{:S(2)}, u32[]{:S(2)}) %collective-permute-start.12) | collective-permute-done | bytes 1048608 | tf_op jit(solution)/shard_map/ppermute | solution.py:106
  320.3 10.9 %shard_map.83 = bf16[512,640]{1,0:T(8,128)(2,1)S(1)} custom-call(s32[1,640]{1,0:T(1,128)S(1)} %collective-permute-done.13.q_ids, s32[640,128]{1,0:T(8,128)S(1)} %broadcast_in_dim.524.k_ids, f32[8,640,128]{2,1,0:T(8,128)S(1)} %select_select_fusion.bias, bf16[512,1280]{1,0:T(8,128)(2,1)S(1)} %fusion.6.queries, bf16[1280,512]{1,0:T(8,128)(2,1)S(1)} %fusion.5.keys, ...), custom_call_target="tpu_custom_call" | custom-call | flops 1677721600 | bytes 5242880 | tf_op jit(solution)/shard_map/pallas_call | solution.py:69
  332.2 11.2 %shard_map.82 = bf16[512,640]{1,0:T(8,128)(2,1)S(1)} custom-call(s32[1,640]{1,0:T(1,128)S(1)} %copy-done.4, s32[640,128]{1,0:T(8,128)S(1)} %broadcast_in_dim.425.k_ids, f32[8,640,128]{2,1,0:T(8,128)S(1)} %select_select_fusion.bias, bf16[512,1280]{1,0:T(8,128)(2,1)S(1)} %fusion.6.queries, bf16[1280,512]{1,0:T(8,128)(2,1)S(1)} %fusion.5.keys, ...), custom_call_target="tpu_custom_call" | custom-call | flops 1677721600 | bytes 5242880 | tf_op jit(solution)/shard_map/pallas_call | solution.py:69
  343.4 3.2 convolution_convert_fusion.2
  348.0 7.3 %collective-permute-done.20 = bf16[1024,512]{1,0:T(8,128)(2,1)} collective-permute-done((bf16[1024,512]{1,0:T(8,128)(2,1)}, bf16[1024,512]{1,0:T(8,128)(2,1)}, u32[]{:S(2)}, u32[]{:S(2)}) %collective-permute-start.20) | collective-permute-done | bytes 1048608 | tf_op jit(solution)/shard_map/ppermute | solution.py:106
  361.5 3.3 fusion.7
  366.5 3.0 convolution_convert_fusion.1
  372.3 24.0 %collective-permute-done.17 = bf16[1280,512]{0,1:T(8,128)(2,1)} collective-permute-done((bf16[1280,512]{0,1:T(8,128)(2,1)}, bf16[1280,512]{0,1:T(8,128)(2,1)}, u32[]{:S(2)}, u32[]{:S(2)}) %collective-permute-start.17) | collective-permute-done | bytes 1310752 | tf_op jit(solution)/shard_map/ppermute | solution.py:106
  407.2 10.6 %collective-permute-done.18 = bf16[640,512]{0,1:T(8,128)(2,1)} collective-permute-done((bf16[640,512]{0,1:T(8,128)(2,1)}, bf16[640,512]{0,1:T(8,128)(2,1)}, u32[]{:S(2)}, u32[]{:S(2)}) %collective-permute-start.18) | collective-permute-done | bytes 655392 | tf_op jit(solution)/shard_map/ppermute | solution.py:106
  419.0 11.6 %collective-permute-done.22 = bf16[640,512]{0,1:T(8,128)(2,1)} collective-permute-done((bf16[640,512]{0,1:T(8,128)(2,1)}, bf16[640,512]{0,1:T(8,128)(2,1)}, u32[]{:S(2)}, u32[]{:S(2)}) %collective-permute-start.22) | collective-permute-done | bytes 655392 | tf_op jit(solution)/shard_map/ppermute | solution.py:106
  434.4 3.6 add_convert_fusion
  (148 shorter events, 74.8 us)
Async XLA Ops:
  6.5 146.8 %copy-start = (f32[32,16]{0,1:T(8,128)S(1)}, f32[32,16]{0,1:T(8,128)}, u32[]{:S(2)}) copy-start(f32[32,16]{0,1:T(8,128)} %param.10) | copy-start | bytes 6148
  6.5 147.8 %all-gather.7.cloned.1.call-start = ((), (), s32[]{:S(2)}) async-start(), calls=%async_computation.1 | async-start | bytes 3145728 | tf_op jit(solution)/shard_map/all_gather | solution.py:124
  7.9 15.0 %collective-permute-start = (bf16[512,512]{1,0:T(8,128)(2,1)S(1)}, bf16[512,512]{1,0:T(8,128)(2,1)S(1)}, u32[]{:S(2)}, u32[]{:S(2)}) collective-permute-start(bf16[512,512]{1,0:T(8,128)(2,1)S(1)} %get-tuple-element.78), channel_id=1, source_target_pairs={{0,8},{4,12},{8,0},{12,4},{16,24},{20,28},{24,16},{28,20},{1,9},{5... | collective-permute-start | bytes 1572872 | tf_op jit(solution)/shard_map/ppermute | solution.py:106
  24.0 158.7 %all-gather.5.cloned.1.call-start = ((), (), s32[]{:S(2)}) async-start(), calls=%async_computation | async-start | bytes 3145728 | tf_op jit(solution)/shard_map/all_gather | solution.py:124
  24.1 52.2 %collective-permute-start.3 = (bf16[640,1024]{1,0:T(8,128)(2,1)S(1)}, bf16[640,1024]{1,0:T(8,128)(2,1)S(1)}, u32[]{:S(2)}, u32[]{:S(2)}) collective-permute-start(bf16[640,1024]{1,0:T(8,128)(2,1)S(1)} %copy-done.5), channel_id=1, source_target_pairs={{0,8},{4,12},{8,0},{12,4},{16,24},{20,28},{24,16},{28,20},{1,9},{5... | collective-permute-start | bytes 3932168 | tf_op jit(solution)/shard_map/ppermute | solution.py:106
  27.2 60.7 %collective-permute-start.1 = (bf16[512,512]{1,0:T(8,128)(2,1)S(1)}, bf16[512,512]{1,0:T(8,128)(2,1)S(1)}, u32[]{:S(2)}, u32[]{:S(2)}) collective-permute-start(bf16[512,512]{1,0:T(8,128)(2,1)S(1)} %get-tuple-element.17), channel_id=1, source_target_pairs={{0,8},{4,12},{8,0},{12,4},{16,24},{20,28},{24,16},{28,20},{1,9},{5... | collective-permute-start | bytes 1572872 | tf_op jit(solution)/shard_map/ppermute | solution.py:106
  27.5 61.4 %collective-permute-start.4 = (bf16[640,1024]{1,0:T(8,128)(2,1)S(1)}, bf16[640,1024]{1,0:T(8,128)(2,1)}, u32[]{:S(2)}, u32[]{:S(2)}) collective-permute-start(bf16[640,1024]{1,0:T(8,128)(2,1)S(1)} %copy-done.5), channel_id=1, source_target_pairs={{0,2},{1,3},{2,0},{3,1},{4,6},{5,7},{6,4},{7,5},{8,10},{9,11},{10,... | collective-permute-start | bytes 3932168 | tf_op jit(solution)/shard_map/ppermute | solution.py:106
  76.3 23.5 %collective-permute-start.5 = (bf16[640,1024]{1,0:T(8,128)(2,1)S(1)}, bf16[640,1024]{1,0:T(8,128)(2,1)}, u32[]{:S(2)}, u32[]{:S(2)}) collective-permute-start(bf16[640,1024]{1,0:T(8,128)(2,1)S(1)} %collective-permute-done.3), channel_id=1, source_target_pairs={{0,2},{1,3},{2,0},{3,1},{4,6},{5,7},{6,4},{7,5},{8,10},{9,11},{10,... | collective-permute-start | bytes 3932168 | tf_op jit(solution)/shard_map/ppermute | solution.py:106
  88.9 135.4 %all-gather.9.cloned.1.call-start = ((), (), s32[]{:S(2)}) async-start(), calls=%async_computation.2 | async-start | bytes 3145728 | tf_op jit(solution)/shard_map/all_gather | solution.py:124
  112.0 39.2 %copy-start.13 = (bf16[1024,512]{1,0:T(8,128)(2,1)S(1)}, bf16[1024,512]{1,0:T(8,128)(2,1)}, u32[]{:S(2)}) copy-start(bf16[1024,512]{1,0:T(8,128)(2,1)} %param.15) | copy-start | bytes 3145732
  112.0 157.0 %collective-permute-start.6 = (bf16[1280,2048]{1,0:T(8,128)(2,1)}, bf16[1280,2048]{1,0:T(8,128)(2,1)}, u32[]{:S(2)}, u32[]{:S(2)}) collective-permute-start(bf16[1280,2048]{1,0:T(8,128)(2,1)} %get-tuple-element.62), channel_id=1, source_target_pairs={{0,1},{1,0},{2,3},{3,2},{4,5},{5,4},{6,7},{7,6},{8,9},{9,8},{10,11... | collective-permute-start | bytes 15728648 | tf_op jit(solution)/shard_map/ppermute | solution.py:106
  112.2 35.8 %collective-permute-start.10 = (bf16[512,512]{1,0:T(8,128)(2,1)S(1)}, bf16[512,512]{1,0:T(8,128)(2,1)S(1)}, u32[]{:S(2)}, u32[]{:S(2)}) collective-permute-start(bf16[512,512]{1,0:T(8,128)(2,1)S(1)} %get-tuple-element.21), channel_id=1, source_target_pairs={{0,8},{4,12},{8,0},{12,4},{16,24},{20,28},{24,16},{28,20},{1,9},{5... | collective-permute-start | bytes 1572872 | tf_op jit(solution)/shard_map/ppermute | solution.py:106
  149.1 116.1 %all-gather.11.cloned.1.call-start = ((), (), s32[]{:S(2)}) async-start(), calls=%async_computation.3 | async-start | bytes 3145728 | tf_op jit(solution)/shard_map/all_gather | solution.py:124
  149.2 24.9 %collective-permute-start.7 = (bf16[1024,512]{1,0:T(8,128)(2,1)S(1)}, bf16[1024,512]{1,0:T(8,128)(2,1)}, u32[]{:S(2)}, u32[]{:S(2)}) collective-permute-start(bf16[1024,512]{1,0:T(8,128)(2,1)S(1)} %copy-done.6), channel_id=1, source_target_pairs={{0,4},{4,0},{8,12},{12,8},{16,20},{20,16},{24,28},{28,24},{1,5},{5... | collective-permute-start | bytes 3145736 | tf_op jit(solution)/shard_map/ppermute | solution.py:106
  150.5 62.0 %collective-permute-start.13 = (s32[1,640]{1,0:T(1,128)S(1)}, s32[1,640]{1,0:T(1,128)S(1)}, u32[]{:S(2)}, u32[]{:S(2)}) collective-permute-start(s32[1,640]{1,0:T(1,128)S(1)} %copy-done.4), channel_id=1, source_target_pairs={{0,8},{4,12},{8,0},{12,4},{16,24},{20,28},{24,16},{28,20},{1,9},{5... | collective-permute-start | bytes 7688 | tf_op jit(solution)/shard_map/ppermute | solution.py:106
  151.3 25.4 %collective-permute-start.14 = (bf16[512,512]{1,0:T(8,128)(2,1)S(1)}, bf16[512,512]{1,0:T(8,128)(2,1)}, u32[]{:S(2)}, u32[]{:S(2)}) collective-permute-start(bf16[512,512]{1,0:T(8,128)(2,1)S(1)} %get-tuple-element.25), channel_id=1, source_target_pairs={{0,8},{4,12},{8,0},{12,4},{16,24},{20,28},{24,16},{28,20},{1,9},{5... | collective-permute-start | bytes 1572872 | tf_op jit(solution)/shard_map/ppermute | solution.py:106
  174.1 26.1 %collective-permute-start.8 = (bf16[1024,512]{1,0:T(8,128)(2,1)S(1)}, bf16[1024,512]{1,0:T(8,128)(2,1)S(1)}, u32[]{:S(2)}, u32[]{:S(2)}) collective-permute-start(bf16[1024,512]{1,0:T(8,128)(2,1)S(1)} %constant_dynamic-slice_fusion.6), channel_id=1, source_target_pairs={{0,4},{4,0},{8,12},{12,8},{16,20},{20,16},{24,28},{28,24},{1,5},{5... | collective-permute-start | bytes 3145736 | tf_op jit(solution)/shard_map/ppermute | solution.py:106
  182.2 40.6 %collective-permute-start.2 = (bf16[1024,512]{1,0:T(8,128)(2,1)}, bf16[1024,512]{1,0:T(8,128)(2,1)}, u32[]{:S(2)}, u32[]{:S(2)}) collective-permute-start(bf16[1024,512]{1,0:T(8,128)(2,1)} %pad_maximum_fusion.5), channel_id=1, source_target_pairs={{0,4},{4,0},{8,12},{12,8},{16,20},{20,16},{24,28},{28,24},{1,5},{5... | collective-permute-start | bytes 3145736 | tf_op jit(solution)/shard_map/ppermute | solution.py:106
  200.2 67.2 %collective-permute-start.9 = (bf16[1024,512]{1,0:T(8,128)(2,1)}, bf16[1024,512]{1,0:T(8,128)(2,1)}, u32[]{:S(2)}, u32[]{:S(2)}) collective-permute-start(bf16[1024,512]{1,0:T(8,128)(2,1)} %constant_dynamic-slice_fusion.7), channel_id=1, source_target_pairs={{0,4},{4,0},{8,12},{12,8},{16,20},{20,16},{24,28},{28,24},{1,5},{5... | collective-permute-start | bytes 3145736 | tf_op jit(solution)/shard_map/ppermute | solution.py:106
  222.8 68.4 %collective-permute-start.11 = (bf16[1024,512]{1,0:T(8,128)(2,1)}, bf16[1024,512]{1,0:T(8,128)(2,1)}, u32[]{:S(2)}, u32[]{:S(2)}) collective-permute-start(bf16[1024,512]{1,0:T(8,128)(2,1)} %pad_maximum_fusion.6), channel_id=1, source_target_pairs={{0,4},{4,0},{8,12},{12,8},{16,20},{20,16},{24,28},{28,24},{1,5},{5... | collective-permute-start | bytes 3145736 | tf_op jit(solution)/shard_map/ppermute | solution.py:106
  267.4 79.2 %collective-permute-start.19 = (bf16[1024,512]{1,0:T(8,128)(2,1)}, bf16[1024,512]{1,0:T(8,128)(2,1)}, u32[]{:S(2)}, u32[]{:S(2)}) collective-permute-start(bf16[1024,512]{1,0:T(8,128)(2,1)} %pad_maximum_fusion.7), channel_id=1, source_target_pairs={{0,4},{4,0},{8,12},{12,8},{16,20},{20,16},{24,28},{28,24},{1,5},{5... | collective-permute-start | bytes 3145736 | tf_op jit(solution)/shard_map/ppermute | solution.py:106
  291.1 24.7 %collective-permute-start.12 = (bf16[1024,512]{1,0:T(8,128)(2,1)S(1)}, bf16[1024,512]{1,0:T(8,128)(2,1)S(1)}, u32[]{:S(2)}, u32[]{:S(2)}) collective-permute-start(bf16[1024,512]{1,0:T(8,128)(2,1)S(1)} %copy-done.11), channel_id=1, source_target_pairs={{0,4},{4,0},{8,12},{12,8},{16,20},{20,16},{24,28},{28,24},{1,5},{5... | collective-permute-start | bytes 3145736 | tf_op jit(solution)/shard_map/ppermute | solution.py:106
  331.3 24.1 %collective-permute-start.20 = (bf16[1024,512]{1,0:T(8,128)(2,1)}, bf16[1024,512]{1,0:T(8,128)(2,1)}, u32[]{:S(2)}, u32[]{:S(2)}) collective-permute-start(bf16[1024,512]{1,0:T(8,128)(2,1)} %constant_dynamic-slice_fusion), channel_id=1, source_target_pairs={{0,4},{4,0},{8,12},{12,8},{16,20},{20,16},{24,28},{28,24},{1,5},{5... | collective-permute-start | bytes 3145736 | tf_op jit(solution)/shard_map/ppermute | solution.py:106
  346.6 14.9 %collective-permute-start.16 = (bf16[1280,512]{0,1:T(8,128)(2,1)}, bf16[1280,512]{0,1:T(8,128)(2,1)}, u32[]{:S(2)}, u32[]{:S(2)}) collective-permute-start(bf16[1280,512]{0,1:T(8,128)(2,1)} %convolution_convert_fusion.2), channel_id=1, source_target_pairs={{0,1},{1,0},{2,3},{3,2},{4,5},{5,4},{6,7},{7,6},{8,9},{9,8},{10,11... | collective-permute-start | bytes 3932168 | tf_op jit(solution)/shard_map/ppermute | solution.py:106
  358.6 11.1 %collective-permute-start.23 = (bf16[1280,512]{0,1:T(8,128)(2,1)}, bf16[1280,512]{0,1:T(8,128)(2,1)}, u32[]{:S(2)}, u32[]{:S(2)}) collective-permute-start(bf16[1280,512]{0,1:T(8,128)(2,1)} %convolution_convert_fusion), channel_id=1, source_target_pairs={{0,1},{1,0},{2,3},{3,2},{4,5},{5,4},{6,7},{7,6},{8,9},{9,8},{10,11... | collective-permute-start | bytes 3932168 | tf_op jit(solution)/shard_map/ppermute | solution.py:106
  361.5 10.8 %collective-permute-start.15 = (bf16[1280,512]{0,1:T(8,128)(2,1)}, bf16[1280,512]{0,1:T(8,128)(2,1)S(1)}, u32[]{:S(2)}, u32[]{:S(2)}) collective-permute-start(bf16[1280,512]{0,1:T(8,128)(2,1)} %convolution_convert_fusion.3), channel_id=1, source_target_pairs={{0,1},{1,0},{2,3},{3,2},{4,5},{5,4},{6,7},{7,6},{8,9},{9,8},{10,11... | collective-permute-start | bytes 3932168 | tf_op jit(solution)/shard_map/ppermute | solution.py:106
  364.8 31.5 %collective-permute-start.17 = (bf16[1280,512]{0,1:T(8,128)(2,1)}, bf16[1280,512]{0,1:T(8,128)(2,1)}, u32[]{:S(2)}, u32[]{:S(2)}) collective-permute-start(bf16[1280,512]{0,1:T(8,128)(2,1)} %fusion.7), channel_id=1, source_target_pairs={{0,2},{1,3},{2,0},{3,1},{4,6},{5,7},{6,4},{7,5},{8,10},{9,11},{10,... | collective-permute-start | bytes 3932168 | tf_op jit(solution)/shard_map/ppermute | solution.py:106
  369.5 30.4 %collective-permute-start.21 = (bf16[1280,512]{0,1:T(8,128)(2,1)}, bf16[1280,512]{0,1:T(8,128)(2,1)}, u32[]{:S(2)}, u32[]{:S(2)}) collective-permute-start(bf16[1280,512]{0,1:T(8,128)(2,1)} %convolution_convert_fusion.1), channel_id=1, source_target_pairs={{0,1},{1,0},{2,3},{3,2},{4,5},{5,4},{6,7},{7,6},{8,9},{9,8},{10,11... | collective-permute-start | bytes 3932168 | tf_op jit(solution)/shard_map/ppermute | solution.py:106
  372.2 33.1 %collective-permute-start.24 = (bf16[640,512]{0,1:T(8,128)(2,1)S(1)}, bf16[640,512]{0,1:T(8,128)(2,1)S(1)}, u32[]{:S(2)}, u32[]{:S(2)}) collective-permute-start(bf16[640,512]{0,1:T(8,128)(2,1)S(1)} %slice.207), channel_id=1, source_target_pairs={{0,8},{4,12},{8,0},{12,4},{16,24},{20,28},{24,16},{28,20},{1,9},{5... | collective-permute-start | bytes 1966088 | tf_op jit(solution)/shard_map/ppermute | solution.py:106
  399.9 18.0 %collective-permute-start.18 = (bf16[640,512]{0,1:T(8,128)(2,1)}, bf16[640,512]{0,1:T(8,128)(2,1)}, u32[]{:S(2)}, u32[]{:S(2)}) collective-permute-start(bf16[640,512]{0,1:T(8,128)(2,1)} %slice.209), channel_id=1, source_target_pairs={{0,8},{4,12},{8,0},{12,4},{16,24},{20,28},{24,16},{28,20},{1,9},{5... | collective-permute-start | bytes 1966088 | tf_op jit(solution)/shard_map/ppermute | solution.py:106
  403.4 27.2 %collective-permute-start.22 = (bf16[640,512]{0,1:T(8,128)(2,1)}, bf16[640,512]{0,1:T(8,128)(2,1)}, u32[]{:S(2)}, u32[]{:S(2)}) collective-permute-start(bf16[640,512]{0,1:T(8,128)(2,1)} %slice.208), channel_id=1, source_target_pairs={{0,8},{4,12},{8,0},{12,4},{16,24},{20,28},{24,16},{28,20},{1,9},{5... | collective-permute-start | bytes 1966088 | tf_op jit(solution)/shard_map/ppermute | solution.py:106
  405.5 25.1 %collective-permute-start.25 = (bf16[640,512]{0,1:T(8,128)(2,1)S(1)}, bf16[640,512]{0,1:T(8,128)(2,1)}, u32[]{:S(2)}, u32[]{:S(2)}) collective-permute-start(bf16[640,512]{0,1:T(8,128)(2,1)S(1)} %fusion.8), channel_id=1, source_target_pairs={{0,2},{1,3},{2,0},{3,1},{4,6},{5,7},{6,4},{7,5},{8,10},{9,11},{10,... | collective-permute-start | bytes 1966088 | tf_op jit(solution)/shard_map/ppermute | solution.py:106
  (27 other events, 276.8 us)
Sparse Core Ops, SparseCore 0:
  24.1 56.9 all-gather.6
  89.0 57.6 all-gather.4
  149.2 58.9 all-gather.8
  209.6 55.4 all-gather.10

commit v4 on v3

--- a/solution.py
+++ b/solution.py
@@ -95,7 +95,7 @@
 def per_device(n_batch, n_hidden, tokens, segments, rel_bias, ln_gain, w_query, w_key, w_value, w_out):
     place = lax.axis_index("batch")
     column = lax.axis_index("hidden")
-    parity = (place >> 1) & 1
+    parity = place & 1
     length, own_width = tokens.shape
     heads = rel_bias.shape[1] // 2
     half = w_query.shape[1] // 2
@@ -105,11 +105,7 @@
         count = n_batch if axis == "batch" else n_hidden
         return lax.ppermute(value, axis, [(i, i ^ step) for i in range(count)])
 
-    planes = n_batch // 4
-    plane = place >> 2
-    near_line = []
-
-    def paired(weight, axis, *earlier):
+    def swapped(weight, axis, *earlier):
         size = weight.shape[axis] // 2
         kept, given = [
             lax.dynamic_slice_in_dim(weight, side * size, size, axis)
@@ -117,54 +113,27 @@
         ]
         if earlier:
             given = after(given, earlier)
-        return jnp.concatenate([kept, swap(given, 2)], axis=0)
-
-    def along_z(pair):
-        groups = [[r + 4 * i for i in range(planes)] for r in range(4)]
-        return lax.all_gather(pair, "batch", axis=0, tiled=True, axis_index_groups=groups)
-
-    def along_x(value, *earlier):
-        waits = tuple(near_line[-2:-1]) + earlier
-        if waits:
-            value = after(value, waits)
-        received = swap(value, 1)
-        near_line.append(received)
-        return received
-
-    def others(whole):
-        size = whole.shape[0] // planes
-        rest = [
-            lax.dynamic_slice_in_dim(whole, (plane ^ k) * size, size, 0) for k in range(1, planes)
-        ]
-        return rest[0] if len(rest) == 1 else jnp.concatenate(rest, axis=0)
-
-    key_pair = paired(w_key, 1)
-
-    peer_tokens = swap(tokens, 2)
-    peer_ids = swap(segments, 2)
+        taken = swap(given, 1)
+        return jnp.where(parity == 0, kept, taken), jnp.where(parity == 0, taken, kept)
+
+    def over_pairs(piece):
+        groups = [[r + 2 * i for i in range(n_batch // 2)] for r in range(2)]
+        return lax.all_gather(piece, "batch", axis=0, tiled=True, axis_index_groups=groups)
+
+    key_pair = jnp.concatenate(swapped(w_key, 1), axis=0)
+
+    peer_tokens = swap(after(tokens, key_pair), 1)
+    peer_ids = swap(segments, 1)
     across = jnp.concatenate([swap(tokens, 2, "hidden"), swap(peer_tokens, 2, "hidden")], axis=0)
     held = jnp.concatenate([jnp.concatenate([tokens, peer_tokens], axis=0), across], axis=1)
     other = swap(held, 1, "hidden")
 
-    query_pair = paired(w_query, 1, key_pair)
-    value_pair = paired(w_value, 1, query_pair)
-    out_pair = paired(w_out, 0, value_pair)
-    key_whole = along_z(key_pair)
-    query_whole = along_z(after(query_pair, key_pair))
-    value_whole = along_z(after(value_pair, query_pair))
-    out_whole = along_z(after(out_pair, value_pair))
-
-    key_near = along_x(key_pair)
-    query_near = along_x(query_pair)
-    key_rest = along_x(others(key_whole))
-    value_near = along_x(value_pair)
-    query_rest = along_x(others(query_whole))
+    query_pair = jnp.concatenate(swapped(w_query, 1, peer_tokens), axis=0)
+    value_pair = jnp.concatenate(swapped(w_value, 1, query_pair), axis=0)
+    out_pair = swapped(w_out, 0, value_pair)
 
     table = lax.dynamic_slice_in_dim(rel_bias, parity * heads, heads, 1)
     bias = bias_tiles(table)
-
-    depth = w_query.shape[0]
-    per_block = own_width // depth
 
     def squares(value):
         value = value.astype(jnp.float32)
@@ -172,54 +141,43 @@
 
     scale = lax.rsqrt((squares(held) + squares(other)) / (2 * held.shape[1]) + norm_epsilon)
 
-    def normed_part(source):
-        block = (source // per_block) ^ column
-        where = (block >> 1) * own_width + (source % per_block) * depth
+    def normed_part(block):
+        step = block ^ column
+        where = (step >> 1) * own_width
         chosen = jnp.where(
-            (block & 1) == 0,
-            lax.dynamic_slice_in_dim(held, where, depth, 1),
-            lax.dynamic_slice_in_dim(other, where, depth, 1),
+            (step & 1) == 0,
+            lax.dynamic_slice_in_dim(held, where, own_width, 1),
+            lax.dynamic_slice_in_dim(other, where, own_width, 1),
         )
-        gain = lax.dynamic_slice_in_dim(ln_gain, source * depth, depth, 0)
+        gain = ln_gain[block * own_width : (block + 1) * own_width]
         return (chosen.astype(jnp.float32) * scale * gain).astype(jnp.bfloat16)
 
-    def normed_parts(sources):
-        return jnp.concatenate([normed_part(source) for source in sources], axis=1)
-
-    normed_near = normed_parts([place ^ (2 * j + 1) for j in range(2)])
-    normed_whole = normed_parts(
-        [4 * i + ((place & 3) ^ (2 * j)) for i in range(planes) for j in range(2)]
-    )
-    normed_rest = normed_parts(
-        [place ^ (4 * k + 2 * j + 1) for k in range(1, planes) for j in range(2)]
-    )
-
-    def project(near, whole, rest, form):
-        total = None
-        for part, rows in ((normed_near, near), (normed_whole, whole), (normed_rest, rest)):
-            term = jnp.einsum(form, part, rows, preferred_element_type=jnp.float32)
-            total = term if total is None else total + term
+    normed = jnp.concatenate([normed_part(block) for block in range(n_hidden)], axis=1)
+
+    def project(pair, form):
+        total = jnp.einsum(form, normed, over_pairs(pair), preferred_element_type=jnp.float32)
         return total.astype(jnp.bfloat16)
 
-    keys = project(key_near, key_whole, key_rest, "td,df->tf")
-    queries = project(query_near, query_whole, query_rest, "td,df->ft")
-    value_rest = along_x(others(value_whole), keys)
-    values = project(value_near, value_whole, value_rest, "td,df->ft")
-    out_near = along_x(out_pair)
-    attended = [attend(queries, keys, values, peer_ids[0], bias, 1, width)]
-    out_rest = along_x(others(out_whole), attended[0])
-    attended.insert(0, attend(queries, keys, values, segments[0], bias, 0, width))
-    attended = jnp.concatenate(attended, axis=1)
-
-    side = place & 1
+    keys = project(key_pair, "td,df->tf")
+    queries = project(query_pair, "td,df->ft")
+    values = project(value_pair, "td,df->ft")
+    w_out_even = over_pairs(after(out_pair[0], keys))
+    w_out_odd = over_pairs(after(out_pair[1], queries))
+    attended = jnp.concatenate(
+        [
+            attend(queries, keys, values, ids[0], bias, group, width)
+            for group, ids in enumerate((segments, peer_ids))
+        ],
+        axis=1,
+    )
+
     stripes = own_width // (2 * w_out.shape[1])
 
-    def sums(rows, mine):
+    def sums(rows):
         def block(step):
-            first = (column ^ step) * stripes
+            first = (column ^ step) * stripes * half
             chosen = [
-                lax.dynamic_slice_in_dim(rows, (mine ^ (first + j)) * half, half, 0)
-                for j in range(stripes)
+                lax.dynamic_slice_in_dim(rows, first + j * half, half, 0) for j in range(stripes)
             ]
             chosen = chosen[0] if stripes == 1 else jnp.concatenate(chosen, axis=1)
             return jnp.einsum("ft,fc->tc", attended, chosen, preferred_element_type=jnp.float32)
@@ -231,15 +189,15 @@
     def send(value, step, axis="batch"):
         return swap(value.astype(jnp.bfloat16), step, axis).astype(jnp.float32)
 
-    here, there = sums(out_whole, parity)
+    here, there = sums(w_out_even)
     first = here + send(there, 2, "hidden")
-    first = first[:length] + send(first[length:], 2)
-    here, there = sums(jnp.concatenate([out_near, out_rest], axis=0), place >> 1)
-    there = there[:length] + send(there[length:], 2)
-    second = here[:length] + send(here[length:], 2) + send(there, 2, "hidden")
+    first = first[:length] + send(first[length:], 1)
+    here, there = sums(w_out_odd)
+    there = there[:length] + send(there[length:], 1)
+    second = here[:length] + send(here[length:], 1) + send(there, 2, "hidden")
 
     parts = [v.reshape(length, stripes, w_out.shape[1]) for v in (first, second)]
-    combined = jnp.where(side == 0, jnp.stack(parts, 2), jnp.stack(parts[::-1], 2))
+    combined = jnp.stack(parts, 2)
     return (tokens.astype(jnp.float32) + combined.reshape(length, own_width)).astype(jnp.bfloat16)
 
 

time: 451 us -> 443 us (0.982)
  local copies, waits for them, and re-layouts: 21.8 us -> 9.32 us
  matrix products: 44.7 us -> 56.5 us
  starting transfers between devices: 27.6 us -> 17.7 us
  other arithmetic: 52.6 us -> 62.2 us
  waiting for transfers between devices: 262 us -> 255 us
    ppermute x26 -> x18, waiting for transfers between devices: 223 us -> 166 us  [swap(): return lax.ppermute(value, axis, [(i, i ^ step) for i in range(count)])]
    all_gather x4 -> x5, waiting for transfers between devices: 38.6 us -> 89.3 us  [over_pairs(): lax.all_gather(piece, 'batch', axis=0, tiled=True, axis_index_groups=groups)]
    ppermute x26 -> x18, starting transfers between devices: 27.5 us -> 17.1 us  [swap(): return lax.ppermute(value, axis, [(i, i ^ step) for i in range(count)])]
    dot_general x9 -> x3, matrix products: 23.8 us -> 34 us  [project(): jnp.einsum(form, normed, over_pairs(pair), preferred_element_type=jnp.flo...]
    dynamic_slice x9 -> x3, local copies, waits for them, and re-layouts: 11.7 us -> 2.26 us  [swapped(): lax.dynamic_slice_in_dim(weight, side * size, size, axis)]
    reduce_sum x2, other arithmetic: 15.8 us -> 24.8 us  [squares(): return jnp.sum(value * value, axis=1, keepdims=True)]
    convert_element_type x2 -> x1, other arithmetic: 10.9 us -> 12.1 us  [normed_part(): return (chosen.astype(jnp.float32) * scale * gain).astype(jnp.bfloat16)]
  transfers between devices with their start and end apart: 30 -> 23, of which waited for: 14 -> 15; matrix products, arithmetic and copies ran while one was open for 24% -> 27% of each run, Pallas kernels for 5% -> 5%
where the time goes in v4:
time: 443 us; the launch traced here: 437 us
  waiting for transfers between devices  255 us (58%)
  other arithmetic  62.2 us (14%)
  matrix products  56.5 us (13%)
  Pallas kernels  22 us (5%)
  starting transfers between devices  17.7 us (4%)
  between operations  13.7 us (3%)
  local copies, waits for them, and re-layouts  9.32 us (2%)
    ppermute x18, waiting for transfers between devices, swap(): return lax.ppermute(value, axis, [(i, i ^ step) for i in range(count)])  166 us
    all_gather x5, waiting for transfers between devices, over_pairs(): lax.all_gather(piece, 'batch', axis=0, tiled=True, axis_index_groups=groups)  89.3 us
    dot_general x3, matrix products, project(): jnp.einsum(form, normed, over_pairs(pair), preferred_element_type=jnp.flo...  34 us
    reduce_sum x2, other arithmetic, squares(): return jnp.sum(value * value, axis=1, keepdims=True)  24.8 us
    dot_general x8, matrix products, block(): jnp.einsum('ft,fc->tc', attended, chosen, preferred_element_type=jnp.floa...  22.6 us
    pallas_call x2, Pallas kernels, attend(): pl.pallas_call(functools.partial(attention_kernel, width), grid=(features...  22 us
    ppermute x18, starting transfers between devices, swap(): return lax.ppermute(value, axis, [(i, i ^ step) for i in range(count)])  17.1 us
    convert_element_type x1, other arithmetic, normed_part(): return (chosen.astype(jnp.float32) * scale * gain).astype(jnp.bfloat16)  12.1 us
  transfers between devices with their start and end apart: 23, of which 15 were waited for; matrix products, arithmetic and copies ran while one was open for 27% of the time, Pallas kernels for 5%

profile of v4, /device:TPU:0, one launch (start us, length us, event | category | flops | bytes accessed | tf_op | source)
XLA Modules:
  0.0 436.9 jit_solution(15509976225614043968)
XLA Ops:
  7.6 3.0 collective-permute-start
  10.6 11.9 %collective-permute-done = bf16[512,512]{1,0:T(8,128)(2,1)S(1)} collective-permute-done((bf16[512,512]{1,0:T(8,128)(2,1)S(1)}, bf16[512,512]{1,0:T(8,128)(2,1)S(1)}, u32[]{:S(2)}, u32[]{:S(2)}) %collective-permute-start) | collective-permute-done | bytes 524320 | tf_op jit(solution)/shard_map/ppermute | solution.py:106
  27.8 27.1 %collective-permute-done.1 = bf16[640,1024]{1,0:T(8,128)(2,1)S(1)} collective-permute-done((bf16[640,1024]{1,0:T(8,128)(2,1)S(1)}, bf16[640,1024]{1,0:T(8,128)(2,1)S(1)}, u32[]{:S(2)}, u32[]{:S(2)}) %collective-permute-start.1) | collective-permute-done | bytes 1310752 | tf_op jit(solution)/shard_map/ppermute | solution.py:106
  56.4 10.9 %collective-permute-done.2 = bf16[512,512]{1,0:T(8,128)(2,1)S(1)} collective-permute-done((bf16[512,512]{1,0:T(8,128)(2,1)S(1)}, bf16[512,512]{1,0:T(8,128)(2,1)S(1)}, u32[]{:S(2)}, u32[]{:S(2)}) %collective-permute-start.2) | collective-permute-done | bytes 524320 | tf_op jit(solution)/shard_map/ppermute | solution.py:106
  71.7 29.7 %collective-permute-done.3 = bf16[640,1024]{1,0:T(8,128)(2,1)S(1)} collective-permute-done((bf16[640,1024]{1,0:T(8,128)(2,1)S(1)}, bf16[640,1024]{1,0:T(8,128)(2,1)S(1)}, u32[]{:S(2)}, u32[]{:S(2)}) %collective-permute-start.3) | collective-permute-done | bytes 1310752 | tf_op jit(solution)/shard_map/ppermute | solution.py:106
  101.4 24.7 %collective-permute-done.4 = bf16[640,1024]{1,0:T(8,128)(2,1)S(1)} collective-permute-done((bf16[640,1024]{1,0:T(8,128)(2,1)S(1)}, bf16[640,1024]{1,0:T(8,128)(2,1)S(1)}, u32[]{:S(2)}, u32[]{:S(2)}) %collective-permute-start.4) | collective-permute-done | bytes 1310752 | tf_op jit(solution)/shard_map/ppermute | solution.py:106
  126.1 21.2 %multiply_reduce_fusion.1 = (f32[1280]{0:T(1024)S(1)}, bf16[1280,2048]{1,0:T(8,128)(2,1)}) fusion(bf16[640,1024]{1,0:T(8,128)(2,1)S(1)} %collective-permute-done.4, bf16[640,1024]{1,0:T(8,128)(2,1)S(1)} %collective-permute-done.3, bf16[640,1024]{1,0:T(8,128)(2,1)S(1)} %collective-permute-done.1, bf16[640,1024]{1,0:T(8,128)(2,1)S(1)} %copy-done.7), kind=kLoop, calls=%fused_computation.2 | loop fusion | flops 28834560 | bytes 10490880 | tf_op jit(solution)/shard_map/reduce_sum | solution.py:140
  148.4 13.5 %collective-permute-done.6 = bf16[512,512]{1,0:T(8,128)(2,1)S(1)} collective-permute-done((bf16[512,512]{1,0:T(8,128)(2,1)S(1)}, bf16[512,512]{1,0:T(8,128)(2,1)S(1)}, u32[]{:S(2)}, u32[]{:S(2)}) %collective-permute-start.6) | collective-permute-done | bytes 524320 | tf_op jit(solution)/shard_map/ppermute | solution.py:106
  164.6 12.9 %collective-permute-done.8 = bf16[512,512]{1,0:T(8,128)(2,1)S(1)} collective-permute-done((bf16[512,512]{1,0:T(8,128)(2,1)S(1)}, bf16[512,512]{1,0:T(8,128)(2,1)S(1)}, u32[]{:S(2)}, u32[]{:S(2)}) %collective-permute-start.8) | collective-permute-done | bytes 524320 | tf_op jit(solution)/shard_map/ppermute | solution.py:106
  178.7 3.6 multiply_reduce_fusion
  182.3 12.1 %multiply_convert_fusion.3 = (bf16[1280,1024]{1,0:T(8,128)(2,1)S(1)}, bf16[1280,1024]{1,0:T(8,128)(2,1)}, bf16[1280,1024]{1,0:T(8,128)(2,1)}, bf16[1280,1024]{1,0:T(8,128)(2,1)}) fusion(f32[1024]{0:T(1024)S(1)} %get-tuple-element.63, f32[1280]{0:T(1024)S(1)} %add_rsqrt_fusion, bf16[1280,2048]{1,0:T(8,128)(2,1)} %collective-permute-done.5, s32[]{:T(128)S(6)} %select_n.575, ...), kind=kLoop, calls=%fused_computation.7 | loop fusion | flops 26214400 | bytes 31478804 | tf_op jit(solution)/shard_map/convert_element_type | solution.py:153
  194.4 11.5 %convolution_convert_fusion.6.keys = bf16[1280,512]{1,0:T(8,128)(2,1)} fusion(bf16[4096,512]{1,0:T(8,128)(2,1)} %all-gather.8.cloned.1.call-done, bf16[1280,1024]{1,0:T(8,128)(2,1)} %get-tuple-element.54, bf16[1280,1024]{1,0:T(8,128)(2,1)} %get-tuple-element.53, bf16[1280,1024]{1,0:T(8,128)(2,1)} %get-tuple-element.52, ...), kind=kOutput, calls=%fused_computation.20 | convolution fusion | flops 5411307520 | bytes 15990784 | tf_op jit(solution)/shard_map/td,df->tf/dot_general | solution.py:158
  208.9 3.0 broadcast_compare_fusion.26
  212.0 11.4 %convolution_convert_fusion.1.queries = bf16[512,1280]{1,0:T(8,128)(2,1)} fusion(bf16[4096,512]{1,0:T(8,128)(2,1)} %all-gather.6.cloned.1.call-done, bf16[1280,1024]{1,0:T(8,128)(2,1)} %get-tuple-element.54, bf16[1280,1024]{1,0:T(8,128)(2,1)} %get-tuple-element.53, bf16[1280,1024]{1,0:T(8,128)(2,1)} %get-tuple-element.52, ...), kind=kOutput, calls=%fused_computation.14 | convolution fusion | flops 5411307520 | bytes 15990784 | tf_op jit(solution)/shard_map/td,df->ft/dot_general | solution.py:158
  223.4 10.8 %select_select_fusion.bias = f32[8,640,128]{2,1,0:T(8,128)S(1)} fusion(f32[8]{0:T(128)} %get-tuple-element.18, f32[8]{0:T(128)} %get-tuple-element.19, f32[8]{0:T(128)} %get-tuple-element.20, f32[8]{0:T(128)} %get-tuple-element.21, f32[8]{0:T(128)} %get-tuple-element.22, f32[8]{0:T(128)} %get-tuple-element.23, f32[8]{0:T(128)} %get-tuple-element.24, ...), kind=kLoop, calls=%fused_computation.23 | loop fusion | flops 20971520 | bytes 5243904 | tf_op jit(solution)/shard_map/jit(_where)/select_n | solution.py:35
  234.3 34.8 %all-gather.10.cloned.1.call-done = bf16[4096,512]{1,0:T(8,128)(2,1)} async-done(((bf16[1024,512]{1,0:T(8,128)(2,1)}), bf16[4096,512]{1,0:T(8,128)(2,1)}) %all-gather.10.cloned.1.call-update) | async-done | bytes 4194320 | tf_op jit(solution)/shard_map/all_gather | solution.py:121
  269.1 11.0 %convolution_convert_fusion.values = bf16[512,1280]{1,0:T(8,128)(2,1)S(1)} fusion(bf16[4096,512]{1,0:T(8,128)(2,1)} %all-gather.10.cloned.1.call-done, bf16[1280,1024]{1,0:T(8,128)(2,1)} %get-tuple-element.54, bf16[1280,1024]{1,0:T(8,128)(2,1)} %get-tuple-element.53, bf16[1280,1024]{1,0:T(8,128)(2,1)} %get-tuple-element.52, bf16[1280,1024]{1,0:T(8,128)(2,1)} %copy-done.8), kind=kOutput, calls=%fused_computation.13 | convolution fusion | flops 5411307520 | bytes 15990784 | tf_op jit(solution)/shard_map/td,df->ft/dot_general | solution.py:158
  280.3 10.9 %shard_map.82 = bf16[512,640]{1,0:T(8,128)(2,1)S(1)} custom-call(s32[1,640]{1,0:T(1,128)S(1)} %copy-done.6, s32[640,128]{1,0:T(8,128)S(1)} %broadcast_in_dim.421.k_ids, f32[8,640,128]{2,1,0:T(8,128)S(1)} %select_select_fusion.bias, bf16[512,1280]{1,0:T(8,128)(2,1)S(1)} %copy-done.3, bf16[1280,512]{1,0:T(8,128)(2,1)S(1)} %copy-done.2, ...), custom_call_target="tpu_custom_call" | custom-call | flops 1677721600 | bytes 5242880 | tf_op jit(solution)/shard_map/pallas_call | solution.py:69
  291.4 11.1 %shard_map.83 = bf16[512,640]{1,0:T(8,128)(2,1)S(1)} custom-call(s32[1,640]{1,0:T(1,128)S(1)} %collective-permute-done.7.q_ids, s32[640,128]{1,0:T(8,128)S(1)} %broadcast_in_dim.520.k_ids, f32[8,640,128]{2,1,0:T(8,128)S(1)} %select_select_fusion.bias, bf16[512,1280]{1,0:T(8,128)(2,1)S(1)} %copy-done.3, bf16[1280,512]{1,0:T(8,128)(2,1)S(1)} %copy-done.2, ...), custom_call_target="tpu_custom_call" | custom-call | flops 1677721600 | bytes 5242880 | tf_op jit(solution)/shard_map/pallas_call | solution.py:69
  303.4 11.7 %all-gather.12.cloned.1.call-done = bf16[2048,512]{1,0:T(8,128)(2,1)} async-done(((bf16[512,512]{1,0:T(8,128)(2,1)}), bf16[2048,512]{1,0:T(8,128)(2,1)}) %all-gather.12.cloned.1.call-update) | async-done | bytes 2097168 | tf_op jit(solution)/shard_map/all_gather | solution.py:121
  315.0 3.4 convolution_convert_fusion.4
  318.4 42.7 %all-gather.14.cloned.1.call-done = bf16[2048,512]{1,0:T(8,128)(2,1)} async-done(((bf16[512,512]{1,0:T(8,128)(2,1)}), bf16[2048,512]{1,0:T(8,128)(2,1)}) %all-gather.14.cloned.1.call-update) | async-done | bytes 2097168 | tf_op jit(solution)/shard_map/all_gather | solution.py:121
  361.1 3.0 convolution_convert_fusion.2
  364.1 3.1 convolution_convert_fusion.3
  369.8 3.4 fusion.1
  380.1 2.5 convolution_add_fusion.1
  383.3 12.9 %collective-permute-done.16 = bf16[640,512]{0,1:T(8,128)(2,1)S(1)} collective-permute-done((bf16[640,512]{0,1:T(8,128)(2,1)S(1)}, bf16[640,512]{0,1:T(8,128)(2,1)S(1)}, u32[]{:S(2)}, u32[]{:S(2)}) %collective-permute-start.16) | collective-permute-done | bytes 655392 | tf_op jit(solution)/shard_map/ppermute | solution.py:106
  397.0 8.0 %collective-permute-done.11 = bf16[1280,512]{0,1:T(8,128)(2,1)} collective-permute-done((bf16[1280,512]{0,1:T(8,128)(2,1)}, bf16[1280,512]{0,1:T(8,128)(2,1)}, u32[]{:S(2)}, u32[]{:S(2)}) %collective-permute-start.11) | collective-permute-done | bytes 1310752 | tf_op jit(solution)/shard_map/ppermute | solution.py:106
  405.0 2.9 fusion
  409.6 9.0 %collective-permute-done.17 = bf16[640,512]{0,1:T(8,128)(2,1)S(1)} collective-permute-done((bf16[640,512]{0,1:T(8,128)(2,1)S(1)}, bf16[640,512]{0,1:T(8,128)(2,1)S(1)}, u32[]{:S(2)}, u32[]{:S(2)}) %collective-permute-start.17) | collective-permute-done | bytes 655392 | tf_op jit(solution)/shard_map/ppermute | solution.py:106
  418.8 5.3 %collective-permute-done.12 = bf16[640,512]{0,1:T(8,128)(2,1)S(1)} collective-permute-done((bf16[640,512]{0,1:T(8,128)(2,1)S(1)}, bf16[640,512]{0,1:T(8,128)(2,1)S(1)}, u32[]{:S(2)}, u32[]{:S(2)}) %collective-permute-start.12) | collective-permute-done | bytes 655392 | tf_op jit(solution)/shard_map/ppermute | solution.py:106
  426.5 3.6 add_convert_fusion
  (98 shorter events, 36.4 us)
Async XLA Ops:
  6.5 200.3 %copy-start = (f32[32,16]{0,1:T(8,128)S(1)}, f32[32,16]{0,1:T(8,128)}, u32[]{:S(2)}) copy-start(f32[32,16]{0,1:T(8,128)} %param.10) | copy-start | bytes 6148
  6.5 187.9 %all-gather.8.cloned.1.call-start = ((), (), s32[]{:S(2)}) async-start(), calls=%async_computation.1 | async-start | bytes 5242880 | tf_op jit(solution)/shard_map/all_gather | solution.py:121
  7.6 14.9 %collective-permute-start = (bf16[512,512]{1,0:T(8,128)(2,1)S(1)}, bf16[512,512]{1,0:T(8,128)(2,1)S(1)}, u32[]{:S(2)}, u32[]{:S(2)}) collective-permute-start(bf16[512,512]{1,0:T(8,128)(2,1)S(1)} %constant_dynamic-slice_fusion.2), channel_id=1, source_target_pairs={{0,4},{4,0},{8,12},{12,8},{16,20},{20,16},{24,28},{28,24},{1,5},{5... | collective-permute-start | bytes 1572872 | tf_op jit(solution)/shard_map/ppermute | solution.py:106
  10.6 14.3 %copy-start.7 = (bf16[640,1024]{1,0:T(8,128)(2,1)S(1)}, bf16[640,1024]{1,0:T(8,128)(2,1)}, u32[]{:S(2)}) copy-start(bf16[640,1024]{1,0:T(8,128)(2,1)} %param.8) | copy-start | bytes 3932164
  24.9 187.0 %all-gather.6.cloned.1.call-start = ((), (), s32[]{:S(2)}) async-start(), calls=%async_computation | async-start | bytes 5242880 | tf_op jit(solution)/shard_map/all_gather | solution.py:121
  25.0 30.0 %collective-permute-start.1 = (bf16[640,1024]{1,0:T(8,128)(2,1)S(1)}, bf16[640,1024]{1,0:T(8,128)(2,1)S(1)}, u32[]{:S(2)}, u32[]{:S(2)}) collective-permute-start(bf16[640,1024]{1,0:T(8,128)(2,1)S(1)} %copy-done.7), channel_id=1, source_target_pairs={{0,4},{4,0},{8,12},{12,8},{16,20},{20,16},{24,28},{28,24},{1,5},{5... | collective-permute-start | bytes 3932168 | tf_op jit(solution)/shard_map/ppermute | solution.py:106
  55.0 12.3 %collective-permute-start.2 = (bf16[512,512]{1,0:T(8,128)(2,1)S(1)}, bf16[512,512]{1,0:T(8,128)(2,1)S(1)}, u32[]{:S(2)}, u32[]{:S(2)}) collective-permute-start(bf16[512,512]{1,0:T(8,128)(2,1)S(1)} %constant_dynamic-slice_fusion.3), channel_id=1, source_target_pairs={{0,4},{4,0},{8,12},{12,8},{16,20},{20,16},{24,28},{28,24},{1,5},{5... | collective-permute-start | bytes 1572872 | tf_op jit(solution)/shard_map/ppermute | solution.py:106
  69.6 199.5 %all-gather.10.cloned.1.call-start = ((), (), s32[]{:S(2)}) async-start(), calls=%async_computation.2 | async-start | bytes 5242880 | tf_op jit(solution)/shard_map/all_gather | solution.py:121
  69.6 77.7 %copy-start.11 = (bf16[512,1024]{1,0:T(8,128)(2,1)S(1)}, bf16[512,1024]{1,0:T(8,128)(2,1)}, u32[]{:S(2)}) copy-start(bf16[512,1024]{1,0:T(8,128)(2,1)} %param.14) | copy-start | bytes 3145732
  69.6 77.7 %copy-start.12 = (bf16[1024,512]{1,0:T(8,128)(2,1)S(1)}, bf16[1024,512]{1,0:T(8,128)(2,1)}, u32[]{:S(2)}) copy-start(bf16[1024,512]{1,0:T(8,128)(2,1)} %param.15) | copy-start | bytes 3145732
  69.7 31.8 %collective-permute-start.3 = (bf16[640,1024]{1,0:T(8,128)(2,1)S(1)}, bf16[640,1024]{1,0:T(8,128)(2,1)S(1)}, u32[]{:S(2)}, u32[]{:S(2)}) collective-permute-start(bf16[640,1024]{1,0:T(8,128)(2,1)S(1)} %copy-done.7), channel_id=1, source_target_pairs={{0,2},{1,3},{2,0},{3,1},{4,6},{5,7},{6,4},{7,5},{8,10},{9,11},{10,... | collective-permute-start | bytes 3932168 | tf_op jit(solution)/shard_map/ppermute | solution.py:106
  70.8 55.3 %collective-permute-start.4 = (bf16[640,1024]{1,0:T(8,128)(2,1)S(1)}, bf16[640,1024]{1,0:T(8,128)(2,1)S(1)}, u32[]{:S(2)}, u32[]{:S(2)}) collective-permute-start(bf16[640,1024]{1,0:T(8,128)(2,1)S(1)} %collective-permute-done.1), channel_id=1, source_target_pairs={{0,2},{1,3},{2,0},{3,1},{4,6},{5,7},{6,4},{7,5},{8,10},{9,11},{10,... | collective-permute-start | bytes 3932168 | tf_op jit(solution)/shard_map/ppermute | solution.py:106
  147.4 31.3 %collective-permute-start.5 = (bf16[1280,2048]{1,0:T(8,128)(2,1)}, bf16[1280,2048]{1,0:T(8,128)(2,1)}, u32[]{:S(2)}, u32[]{:S(2)}) collective-permute-start(bf16[1280,2048]{1,0:T(8,128)(2,1)} %get-tuple-element.50), channel_id=1, source_target_pairs={{0,1},{1,0},{2,3},{3,2},{4,5},{5,4},{6,7},{7,6},{8,9},{9,8},{10,11... | collective-permute-start | bytes 15728648 | tf_op jit(solution)/shard_map/ppermute | solution.py:106
  147.5 17.1 %copy-start.14 = (f32[4096]{0:T(1024)S(1)}, f32[4096]{0:T(1024)}, u32[]{:S(2)}) copy-start(f32[4096]{0:T(1024)} %param.11) | copy-start | bytes 49156
  147.5 30.0 %copy-start.13 = (bf16[1024,512]{1,0:T(8,128)(2,1)S(1)}, bf16[1024,512]{1,0:T(8,128)(2,1)}, u32[]{:S(2)}) copy-start(bf16[1024,512]{1,0:T(8,128)(2,1)} %param.15) | copy-start | bytes 3145732
  147.5 14.4 %collective-permute-start.6 = (bf16[512,512]{1,0:T(8,128)(2,1)S(1)}, bf16[512,512]{1,0:T(8,128)(2,1)S(1)}, u32[]{:S(2)}, u32[]{:S(2)}) collective-permute-start(bf16[512,512]{1,0:T(8,128)(2,1)S(1)} %get-tuple-element.13), channel_id=1, source_target_pairs={{0,4},{4,0},{8,12},{12,8},{16,20},{20,16},{24,28},{28,24},{1,5},{5... | collective-permute-start | bytes 1572872 | tf_op jit(solution)/shard_map/ppermute | solution.py:106
  163.2 151.8 %all-gather.12.cloned.1.call-start = ((), (), s32[]{:S(2)}) async-start(), calls=%async_computation.3 | async-start | bytes 2621440 | tf_op jit(solution)/shard_map/all_gather | solution.py:121
  163.8 13.7 %collective-permute-start.8 = (bf16[512,512]{1,0:T(8,128)(2,1)S(1)}, bf16[512,512]{1,0:T(8,128)(2,1)S(1)}, u32[]{:S(2)}, u32[]{:S(2)}) collective-permute-start(bf16[512,512]{1,0:T(8,128)(2,1)S(1)} %get-tuple-element.14), channel_id=1, source_target_pairs={{0,4},{4,0},{8,12},{12,8},{16,20},{20,16},{24,28},{28,24},{1,5},{5... | collective-permute-start | bytes 1572872 | tf_op jit(solution)/shard_map/ppermute | solution.py:106
  194.4 17.6 %copy-start.8 = (bf16[1280,1024]{1,0:T(8,128)(2,1)}, bf16[1280,1024]{1,0:T(8,128)(2,1)S(1)}, u32[]{:S(2)}) copy-start(bf16[1280,1024]{1,0:T(8,128)(2,1)S(1)} %get-tuple-element.51) | copy-start | bytes 7864324
  205.9 155.2 %all-gather.14.cloned.1.call-start = ((), (), s32[]{:S(2)}) async-start(), calls=%async_computation.4 | async-start | bytes 2621440 | tf_op jit(solution)/shard_map/all_gather | solution.py:121
  206.0 28.3 %collective-permute-start.7 = (s32[1,640]{1,0:T(1,128)S(1)}, s32[1,640]{1,0:T(1,128)S(1)}, u32[]{:S(2)}, u32[]{:S(2)}) collective-permute-start(s32[1,640]{1,0:T(1,128)S(1)} %copy-done.6), channel_id=1, source_target_pairs={{0,4},{4,0},{8,12},{12,8},{16,20},{20,16},{24,28},{28,24},{1,5},{5... | collective-permute-start | bytes 7688 | tf_op jit(solution)/shard_map/ppermute | solution.py:106
  315.0 46.1 %copy-start.5 = (bf16[512,640]{1,0:T(8,128)(2,1)S(1)}, bf16[512,640]{1,0:T(8,128)(2,1)}, u32[]{:S(2)}) copy-start(bf16[512,640]{1,0:T(8,128)(2,1)} %copy-done.4) | copy-start | bytes 1966084
  318.4 51.4 %collective-permute-start.10 = (bf16[1280,512]{0,1:T(8,128)(2,1)}, bf16[1280,512]{0,1:T(8,128)(2,1)}, u32[]{:S(2)}, u32[]{:S(2)}) collective-permute-start(bf16[1280,512]{0,1:T(8,128)(2,1)} %convolution_convert_fusion.4), channel_id=1, source_target_pairs={{0,1},{1,0},{2,3},{3,2},{4,5},{5,4},{6,7},{7,6},{8,9},{9,8},{10,11... | collective-permute-start | bytes 3932168 | tf_op jit(solution)/shard_map/ppermute | solution.py:106
  364.1 10.5 %collective-permute-start.15 = (bf16[1280,512]{0,1:T(8,128)(2,1)}, bf16[1280,512]{0,1:T(8,128)(2,1)}, u32[]{:S(2)}, u32[]{:S(2)}) collective-permute-start(bf16[1280,512]{0,1:T(8,128)(2,1)} %convolution_convert_fusion.2), channel_id=1, source_target_pairs={{0,1},{1,0},{2,3},{3,2},{4,5},{5,4},{6,7},{7,6},{8,9},{9,8},{10,11... | collective-permute-start | bytes 3932168 | tf_op jit(solution)/shard_map/ppermute | solution.py:106
  367.3 12.8 %collective-permute-start.13 = (bf16[1280,512]{0,1:T(8,128)(2,1)}, bf16[1280,512]{0,1:T(8,128)(2,1)}, u32[]{:S(2)}, u32[]{:S(2)}) collective-permute-start(bf16[1280,512]{0,1:T(8,128)(2,1)} %convolution_convert_fusion.3), channel_id=1, source_target_pairs={{0,1},{1,0},{2,3},{3,2},{4,5},{5,4},{6,7},{7,6},{8,9},{9,8},{10,11... | collective-permute-start | bytes 3932168 | tf_op jit(solution)/shard_map/ppermute | solution.py:106
  369.8 27.3 %collective-permute-start.9 = (bf16[1280,512]{0,1:T(8,128)(2,1)}, bf16[1280,512]{0,1:T(8,128)(2,1)}, u32[]{:S(2)}, u32[]{:S(2)}) collective-permute-start(bf16[1280,512]{0,1:T(8,128)(2,1)} %convolution_convert_fusion.5), channel_id=1, source_target_pairs={{0,1},{1,0},{2,3},{3,2},{4,5},{5,4},{6,7},{7,6},{8,9},{9,8},{10,11... | collective-permute-start | bytes 3932168 | tf_op jit(solution)/shard_map/ppermute | solution.py:106
  373.1 31.9 %collective-permute-start.11 = (bf16[1280,512]{0,1:T(8,128)(2,1)}, bf16[1280,512]{0,1:T(8,128)(2,1)}, u32[]{:S(2)}, u32[]{:S(2)}) collective-permute-start(bf16[1280,512]{0,1:T(8,128)(2,1)} %fusion.1), channel_id=1, source_target_pairs={{0,2},{1,3},{2,0},{3,1},{4,6},{5,7},{6,4},{7,5},{8,10},{9,11},{10,... | collective-permute-start | bytes 3932168 | tf_op jit(solution)/shard_map/ppermute | solution.py:106
  378.6 17.6 %collective-permute-start.16 = (bf16[640,512]{0,1:T(8,128)(2,1)S(1)}, bf16[640,512]{0,1:T(8,128)(2,1)S(1)}, u32[]{:S(2)}, u32[]{:S(2)}) collective-permute-start(bf16[640,512]{0,1:T(8,128)(2,1)S(1)} %slice.223), channel_id=1, source_target_pairs={{0,4},{4,0},{8,12},{12,8},{16,20},{20,16},{24,28},{28,24},{1,5},{5... | collective-permute-start | bytes 1966088 | tf_op jit(solution)/shard_map/ppermute | solution.py:106
  380.1 16.1 %copy-start.10 = (f32[1280,512]{0,1:T(8,128)S(1)}, f32[1280,512]{0,1:T(8,128)}, u32[]{:S(2)}) copy-start(f32[1280,512]{0,1:T(8,128)} %copy-done.9) | copy-start | bytes 7864324
  382.7 26.9 %collective-permute-start.14 = (bf16[640,512]{0,1:T(8,128)(2,1)S(1)}, bf16[640,512]{0,1:T(8,128)(2,1)S(1)}, u32[]{:S(2)}, u32[]{:S(2)}) collective-permute-start(bf16[640,512]{0,1:T(8,128)(2,1)S(1)} %slice.224), channel_id=1, source_target_pairs={{0,4},{4,0},{8,12},{12,8},{16,20},{20,16},{24,28},{28,24},{1,5},{5... | collective-permute-start | bytes 1966088 | tf_op jit(solution)/shard_map/ppermute | solution.py:106
  396.4 22.2 %collective-permute-start.17 = (bf16[640,512]{0,1:T(8,128)(2,1)S(1)}, bf16[640,512]{0,1:T(8,128)(2,1)S(1)}, u32[]{:S(2)}, u32[]{:S(2)}) collective-permute-start(bf16[640,512]{0,1:T(8,128)(2,1)S(1)} %fusion.2), channel_id=1, source_target_pairs={{0,2},{1,3},{2,0},{3,1},{4,6},{5,7},{6,4},{7,5},{8,10},{9,11},{10,... | collective-permute-start | bytes 1966088 | tf_op jit(solution)/shard_map/ppermute | solution.py:106
  408.0 16.0 %collective-permute-start.12 = (bf16[640,512]{0,1:T(8,128)(2,1)S(1)}, bf16[640,512]{0,1:T(8,128)(2,1)S(1)}, u32[]{:S(2)}, u32[]{:S(2)}) collective-permute-start(bf16[640,512]{0,1:T(8,128)(2,1)S(1)} %slice.225), channel_id=1, source_target_pairs={{0,4},{4,0},{8,12},{12,8},{16,20},{20,16},{24,28},{28,24},{1,5},{5... | collective-permute-start | bytes 1966088 | tf_op jit(solution)/shard_map/ppermute | solution.py:106
  (7 other events, 45.8 us)
Sparse Core Ops, SparseCore 0:
  25.0 82.2 all-gather.7
  108.9 79.2 all-gather.5
  189.8 79.2 all-gather.9
  270.5 44.4 all-gather.11
  316.4 44.6 all-gather.13

commit v5 on v4

--- a/solution.py
+++ b/solution.py
@@ -105,6 +105,9 @@
         count = n_batch if axis == "batch" else n_hidden
         return lax.ppermute(value, axis, [(i, i ^ step) for i in range(count)])
 
+    pairs = n_batch // 2
+    pair = place >> 1
+
     def swapped(weight, axis, *earlier):
         size = weight.shape[axis] // 2
         kept, given = [
@@ -114,55 +117,104 @@
         if earlier:
             given = after(given, earlier)
         taken = swap(given, 1)
-        return jnp.where(parity == 0, kept, taken), jnp.where(parity == 0, taken, kept)
-
-    def over_pairs(piece):
-        groups = [[r + 2 * i for i in range(n_batch // 2)] for r in range(2)]
-        return lax.all_gather(piece, "batch", axis=0, tiled=True, axis_index_groups=groups)
-
-    key_pair = jnp.concatenate(swapped(w_key, 1), axis=0)
-
-    peer_tokens = swap(after(tokens, key_pair), 1)
+        return jnp.where(parity == 0, jnp.concatenate([kept, taken]), jnp.concatenate([taken, kept]))
+
+    def pass_on(value, way):
+        return lax.ppermute(
+            value, "batch", [(i, (i + 2 * way) % n_batch) for i in range(n_batch)]
+        )
+
+    def first_hops(block, *earlier):
+        if earlier:
+            block = after(block, earlier)
+        return [pass_on(block, 1), pass_on(block, -1)]
+
+    def round_ring(block, hops, *earlier):
+        blocks = {0: block, pairs - 1: hops[0], 1: hops[1]}
+        for step in range(2, pairs // 2):
+            hops = [pass_on(hops[0], 1), pass_on(hops[1], -1)]
+            blocks[pairs - step], blocks[step] = hops
+        middle = block.shape[0] // 2
+        ends = [hops[0][:middle], hops[1][middle:]]
+        if earlier:
+            ends = [after(end, wait) for end, wait in zip(ends, earlier)]
+        blocks[pairs // 2] = jnp.concatenate([pass_on(ends[0], 1), pass_on(ends[1], -1)])
+        return blocks
+
+    key_block = swapped(w_key, 1)
+    key_hops = first_hops(key_block)
+    query_block = swapped(w_query, 1, key_block)
+    query_hops = first_hops(query_block)
+
+    peer_tokens = swap(after(tokens, key_block), 1)
     peer_ids = swap(segments, 1)
-    across = jnp.concatenate([swap(tokens, 2, "hidden"), swap(peer_tokens, 2, "hidden")], axis=0)
-    held = jnp.concatenate([jnp.concatenate([tokens, peer_tokens], axis=0), across], axis=1)
-    other = swap(held, 1, "hidden")
-
-    query_pair = jnp.concatenate(swapped(w_query, 1, peer_tokens), axis=0)
-    value_pair = jnp.concatenate(swapped(w_value, 1, query_pair), axis=0)
-    out_pair = swapped(w_out, 0, value_pair)
+    across = swap(tokens, 2, "hidden")
+    value_block = swapped(w_value, 1, peer_tokens)
+    value_hops = first_hops(value_block, *key_hops, across)
+    peer_across = swap(peer_tokens, 2, "hidden")
+    out_block = swapped(w_out, 0, value_block)
+    out_hops = first_hops(out_block, *query_hops, peer_across)
+
+    def all_features(here, there):
+        return [here, swap(here, 1, "hidden"), there, swap(there, 1, "hidden")]
+
+    gathered = [all_features(tokens, across), all_features(peer_tokens, peer_across)]
+
+    key_blocks = round_ring(key_block, key_hops)
+    query_blocks = round_ring(query_block, query_hops)
+    value_blocks = round_ring(value_block, value_hops, gathered[1][3], gathered[1][1])
 
     table = lax.dynamic_slice_in_dim(rel_bias, parity * heads, heads, 1)
     bias = bias_tiles(table)
 
-    def squares(value):
-        value = value.astype(jnp.float32)
-        return jnp.sum(value * value, axis=1, keepdims=True)
-
-    scale = lax.rsqrt((squares(held) + squares(other)) / (2 * held.shape[1]) + norm_epsilon)
-
-    def normed_part(block):
-        step = block ^ column
-        where = (step >> 1) * own_width
-        chosen = jnp.where(
-            (step & 1) == 0,
-            lax.dynamic_slice_in_dim(held, where, own_width, 1),
-            lax.dynamic_slice_in_dim(other, where, own_width, 1),
+    def normalised(parts):
+        def squares(value):
+            value = value.astype(jnp.float32)
+            return jnp.sum(value * value, axis=1, keepdims=True)
+
+        mean = sum(squares(part) for part in parts) / (own_width * len(parts))
+        scale = lax.rsqrt(mean + norm_epsilon)
+        gains = [
+            lax.dynamic_slice_in_dim(ln_gain, (column ^ k) * own_width, own_width, 0)
+            for k in range(len(parts))
+        ]
+        return jnp.concatenate(
+            [
+                (part.astype(jnp.float32) * scale * gain).astype(jnp.bfloat16)
+                for part, gain in zip(parts, gains)
+            ],
+            axis=1,
         )
-        gain = ln_gain[block * own_width : (block + 1) * own_width]
-        return (chosen.astype(jnp.float32) * scale * gain).astype(jnp.bfloat16)
-
-    normed = jnp.concatenate([normed_part(block) for block in range(n_hidden)], axis=1)
-
-    def project(pair, form):
-        total = jnp.einsum(form, normed, over_pairs(pair), preferred_element_type=jnp.float32)
+
+    normed = jnp.concatenate([normalised(parts) for parts in gathered], axis=0)
+    depth = 2 * w_query.shape[0]
+
+    def normed_part(offset):
+        start = (pair + offset) % pairs * depth
+        start = ((start // own_width) ^ column) * own_width + start % own_width
+        return lax.dynamic_slice_in_dim(normed, start, depth, 1)
+
+    arrival = [0] + [r for step in range(1, pairs // 2) for r in (pairs - step, step)] + [pairs // 2]
+    size = max(1, pairs // 4)
+    rounds = [arrival[i : i + size] for i in range(0, pairs, size)]
+
+    def joined(values, axis):
+        return values[0] if len(values) == 1 else jnp.concatenate(values, axis=axis)
+
+    def project(blocks, form):
+        total = None
+        for offsets in rounds:
+            part = joined([normed_part(r) for r in offsets], 1)
+            rows = joined([blocks[r] for r in offsets], 0)
+            term = jnp.einsum(form, part, rows, preferred_element_type=jnp.float32)
+            total = term if total is None else total + term
         return total.astype(jnp.bfloat16)
 
-    keys = project(key_pair, "td,df->tf")
-    queries = project(query_pair, "td,df->ft")
-    values = project(value_pair, "td,df->ft")
-    w_out_even = over_pairs(after(out_pair[0], keys))
-    w_out_odd = over_pairs(after(out_pair[1], queries))
+    keys = project(key_blocks, "td,df->tf")
+    queries = project(query_blocks, "td,df->ft")
+    values = project(value_blocks, "td,df->ft")
+    out_blocks = round_ring(out_block, out_hops, keys, queries)
+    out_rows = jnp.concatenate([out_blocks[r] for r in range(pairs)], axis=0)
     attended = jnp.concatenate(
         [
             attend(queries, keys, values, ids[0], bias, group, width)
@@ -173,13 +225,16 @@
 
     stripes = own_width // (2 * w_out.shape[1])
 
-    def sums(rows):
+    def sums(odd):
         def block(step):
-            first = (column ^ step) * stripes * half
+            first = (column ^ step) * stripes
             chosen = [
-                lax.dynamic_slice_in_dim(rows, first + j * half, half, 0) for j in range(stripes)
+                lax.dynamic_slice_in_dim(
+                    out_rows, ((first + j - pair) % pairs * 2 + odd) * half, half, 0
+                )
+                for j in range(stripes)
             ]
-            chosen = chosen[0] if stripes == 1 else jnp.concatenate(chosen, axis=1)
+            chosen = joined(chosen, 1)
             return jnp.einsum("ft,fc->tc", attended, chosen, preferred_element_type=jnp.float32)
 
         far = send(block(3), 1, "hidden")
@@ -189,10 +244,10 @@
     def send(value, step, axis="batch"):
         return swap(value.astype(jnp.bfloat16), step, axis).astype(jnp.float32)
 
-    here, there = sums(w_out_even)
+    here, there = sums(0)
     first = here + send(there, 2, "hidden")
     first = first[:length] + send(first[length:], 1)
-    here, there = sums(w_out_odd)
+    here, there = sums(1)
     there = there[:length] + send(there[length:], 1)
     second = here[:length] + send(here[length:], 1) + send(there, 2, "hidden")
 

time: 443 us -> 493 us (1.11)
  starting transfers between devices: 17.7 us -> 122 us
  waiting for transfers between devices: 255 us -> 152 us
  other arithmetic: 62.2 us -> 114 us
  between operations: 13.7 us -> 1.18 us
  local copies, waits for them, and re-layouts: 9.32 us -> 20.4 us
    ppermute x0 -> x16, starting transfers between devices: none -> 103 us  [pass_on(): lax.ppermute(value, 'batch', [(i, (i + 2 * way) % n_batch) for i in range...]
    all_gather x5 -> x0, waiting for transfers between devices: 89.3 us -> none  [over_pairs(): lax.all_gather(piece, 'batch', axis=0, tiled=True, axis_index_groups=groups)]
    ppermute x18 -> x21, waiting for transfers between devices: 166 us -> 86.8 us  [swap(): return lax.ppermute(value, axis, [(i, i ^ step) for i in range(count)])]
    concatenate x3 -> x1, other arithmetic: 3.16 us -> 75.1 us  [per_device(): normed = jnp.concatenate([normalised(parts) for parts in gathered], axis=0)]
    ppermute x0 -> x16, waiting for transfers between devices: none -> 65.1 us  [pass_on(): lax.ppermute(value, 'batch', [(i, (i + 2 * way) % n_batch) for i in range...]
    reduce_sum x2 -> x8, other arithmetic: 24.8 us -> 12 us  [squares(): return jnp.sum(value * value, axis=1, keepdims=True)]
    convert_element_type x1, other arithmetic: 12.1 us -> 5.99 us  [normalised(): (part.astype(jnp.float32) * scale * gain).astype(jnp.bfloat16)]
    slice x1 -> x8, local copies, waits for them, and re-layouts: 0.01 us -> 5.36 us  [round_ring(): ends = [hops[0][:middle], hops[1][middle:]]]
  transfers between devices with their start and end apart: 23 -> 37, of which waited for: 15 -> 16; matrix products, arithmetic and copies ran while one was open for 27% -> 36% of each run, Pallas kernels for 5% -> 5%
where the time goes in v5:
time: 493 us; the launch traced here: 489 us
  waiting for transfers between devices  152 us (31%)
  starting transfers between devices  122 us (25%)
  other arithmetic  114 us (23%)
  matrix products  57 us (12%)
  Pallas kernels  22 us (4%)
  local copies, waits for them, and re-layouts  20.4 us (4%)
    ppermute x16, starting transfers between devices, pass_on(): lax.ppermute(value, 'batch', [(i, (i + 2 * way) % n_batch) for i in range...  103 us
    ppermute x21, waiting for transfers between devices, swap(): return lax.ppermute(value, axis, [(i, i ^ step) for i in range(count)])  86.8 us
    concatenate x1, other arithmetic, per_device(): normed = jnp.concatenate([normalised(parts) for parts in gathered], axis=0)  75.1 us
    ppermute x16, waiting for transfers between devices, pass_on(): lax.ppermute(value, 'batch', [(i, (i + 2 * way) % n_batch) for i in range...  65.1 us
    dot_general x12, matrix products, project(): term = jnp.einsum(form, part, rows, preferred_element_type=jnp.float32)  34.4 us
    dot_general x8, matrix products, block(): jnp.einsum('ft,fc->tc', attended, chosen, preferred_element_type=jnp.floa...  22.6 us
    pallas_call x2, Pallas kernels, attend(): pl.pallas_call(functools.partial(attention_kernel, width), grid=(features...  22 us
    ppermute x21, starting transfers between devices, swap(): return lax.ppermute(value, axis, [(i, i ^ step) for i in range(count)])  19 us
  transfers between devices with their start and end apart: 37, of which 16 were waited for; matrix products, arithmetic and copies ran while one was open for 36% of the time, Pallas kernels for 5%

profile of v5, /device:TPU:0, one launch (start us, length us, event | category | flops | bytes accessed | tf_op | source)
XLA Modules:
  0.0 489.1 jit_solution(5325814951424889511)
XLA Ops:
  4.3 11.9 %collective-permute-done = bf16[512,512]{1,0:T(8,128)(2,1)S(1)} collective-permute-done((bf16[512,512]{1,0:T(8,128)(2,1)S(1)}, bf16[512,512]{1,0:T(8,128)(2,1)S(1)}, u32[]{:S(2)}, u32[]{:S(2)}) %collective-permute-start) | collective-permute-done | bytes 524320 | tf_op jit(solution)/shard_map/ppermute | solution.py:106
  22.7 26.0 %collective-permute-done.5 = bf16[640,1024]{1,0:T(8,128)(2,1)} collective-permute-done((bf16[640,1024]{1,0:T(8,128)(2,1)}, bf16[640,1024]{1,0:T(8,128)(2,1)}, u32[]{:S(2)}, u32[]{:S(2)}) %collective-permute-start.5) | collective-permute-done | bytes 1310752 | tf_op jit(solution)/shard_map/ppermute | solution.py:106
  54.8 5.1 %collective-permute-done.1 = bf16[512,512]{1,0:T(8,128)(2,1)S(1)} collective-permute-done((bf16[512,512]{1,0:T(8,128)(2,1)}, bf16[512,512]{1,0:T(8,128)(2,1)S(1)}, u32[]{:S(2)}, u32[]{:S(2)}) %collective-permute-start.1) | collective-permute-done | bytes 524320 | tf_op jit(solution)/shard_map/ppermute | solution.py:106
  65.0 4.4 collective-permute-done.17
  78.9 24.4 %collective-permute-start.10 = (bf16[1024,512]{1,0:T(8,128)(2,1)}, bf16[1024,512]{1,0:T(8,128)(2,1)}, u32[]{:S(2)}, u32[]{:S(2)}) collective-permute-start(bf16[1024,512]{1,0:T(8,128)(2,1)} %maximum_select_fusion.1), channel_id=1, source_target_pairs={{0,24},{4,28},{8,0},{12,4},{16,8},{20,12},{24,16},{28,20},{1,25},{... | collective-permute-start | bytes 3145736 | tf_op jit(solution)/shard_map/ppermute | solution.py:123
  103.3 10.3 %collective-permute-done.14 = bf16[1024,512]{1,0:T(8,128)(2,1)S(1)} collective-permute-done((bf16[1024,512]{1,0:T(8,128)(2,1)S(1)}, bf16[1024,512]{1,0:T(8,128)(2,1)S(1)}, u32[]{:S(2)}, u32[]{:S(2)}) %collective-permute-start.14) | collective-permute-done | bytes 1048608 | tf_op jit(solution)/shard_map/ppermute | solution.py:123
  113.6 10.2 %collective-permute-done.9 = bf16[1024,512]{1,0:T(8,128)(2,1)S(1)} collective-permute-done((bf16[1024,512]{1,0:T(8,128)(2,1)}, bf16[1024,512]{1,0:T(8,128)(2,1)S(1)}, u32[]{:S(2)}, u32[]{:S(2)}) %collective-permute-start.9) | collective-permute-done | bytes 1048608 | tf_op jit(solution)/shard_map/ppermute | solution.py:123
  126.2 9.6 %select_select_fusion.bias = f32[8,640,128]{2,1,0:T(8,128)S(1)} fusion(f32[8]{0:T(128)S(1)} %get-tuple-element.26, f32[8]{0:T(128)S(1)} %get-tuple-element.27, f32[8]{0:T(128)S(1)} %get-tuple-element.28, f32[8]{0:T(128)S(1)} %get-tuple-element.29, f32[8]{0:T(128)S(1)} %get-tuple-element.30, f32[8]{0:T(128)S(1)} %get-tuple-element.31, ...), kind=kLoop, calls=%fused_computation.66 | loop fusion | flops 20971520 | bytes 5243904 | tf_op jit(solution)/shard_map/jit(_where)/select_n | solution.py:35
  141.7 3.4 collective-permute-done.7
  145.1 15.6 %collective-permute-start.19 = (bf16[1024,512]{1,0:T(8,128)(2,1)S(1)}, bf16[1024,512]{1,0:T(8,128)(2,1)S(1)}, u32[]{:S(2)}, u32[]{:S(2)}) collective-permute-start(bf16[1024,512]{1,0:T(8,128)(2,1)S(1)} %copy-done.9), channel_id=1, source_target_pairs={{0,24},{4,28},{8,0},{12,4},{16,8},{20,12},{24,16},{28,20},{1,25},{... | collective-permute-start | bytes 3145736 | tf_op jit(solution)/shard_map/ppermute | solution.py:123
  174.8 18.9 %collective-permute-done.19 = bf16[1024,512]{1,0:T(8,128)(2,1)S(1)} collective-permute-done((bf16[1024,512]{1,0:T(8,128)(2,1)S(1)}, bf16[1024,512]{1,0:T(8,128)(2,1)S(1)}, u32[]{:S(2)}, u32[]{:S(2)}) %collective-permute-start.19) | collective-permute-done | bytes 1048608 | tf_op jit(solution)/shard_map/ppermute | solution.py:123
  193.7 12.7 %collective-permute-start.15 = (bf16[512,512]{1,0:T(8,128)(2,1)}, bf16[512,512]{1,0:T(8,128)(2,1)}, u32[]{:S(2)}, u32[]{:S(2)}) collective-permute-start(bf16[512,512]{1,0:T(8,128)(2,1)} %slice.189), channel_id=1, source_target_pairs={{0,8},{4,12},{8,16},{12,20},{16,24},{20,28},{24,0},{28,4},{1,9},{5... | collective-permute-start | bytes 1572872 | tf_op jit(solution)/shard_map/ppermute | solution.py:123
  206.4 24.7 %collective-permute-start.16 = (bf16[512,512]{1,0:T(8,128)(2,1)S(1)}, bf16[512,512]{1,0:T(8,128)(2,1)}, u32[]{:S(2)}, u32[]{:S(2)}) collective-permute-start(bf16[512,512]{1,0:T(8,128)(2,1)S(1)} %slice.190), channel_id=1, source_target_pairs={{0,24},{4,28},{8,0},{12,4},{16,8},{20,12},{24,16},{28,20},{1,25},{... | collective-permute-start | bytes 1572872 | tf_op jit(solution)/shard_map/ppermute | solution.py:123
  232.0 19.7 %collective-permute-done.25 = bf16[1024,512]{1,0:T(8,128)(2,1)S(1)} collective-permute-done((bf16[1024,512]{1,0:T(8,128)(2,1)S(1)}, bf16[1024,512]{1,0:T(8,128)(2,1)S(1)}, u32[]{:S(2)}, u32[]{:S(2)}) %collective-permute-start.25) | collective-permute-done | bytes 1048608 | tf_op jit(solution)/shard_map/ppermute | solution.py:123
  251.7 13.2 %collective-permute-start.12 = (bf16[512,512]{1,0:T(8,128)(2,1)}, bf16[512,512]{1,0:T(8,128)(2,1)}, u32[]{:S(2)}, u32[]{:S(2)}) collective-permute-start(bf16[512,512]{1,0:T(8,128)(2,1)} %slice.188), channel_id=1, source_target_pairs={{0,24},{4,28},{8,0},{12,4},{16,8},{20,12},{24,16},{28,20},{1,25},{... | collective-permute-start | bytes 1572872 | tf_op jit(solution)/shard_map/ppermute | solution.py:123
  267.7 6.0 %fusion.34 = (bf16[640,1024]{1,0:T(8,128)(2,1)S(1)}, bf16[640,1024]{1,0:T(8,128)(2,1)S(1)}, bf16[640,1024]{1,0:T(8,128)(2,1)S(1)}, bf16[640,1024]{1,0:T(8,128)(2...) fusion(bf16[640,1024]{1,0:T(8,128)(2,1)} %param.8, ...), kind=kLoop, calls=%fused_computation.63 | loop fusion | flops 20971520 | bytes 20993024 | tf_op jit(solution)/shard_map/convert_element_type | solution.py:183
  273.7 75.1 %maximum_maximum_fusion = bf16[1280,4096]{1,0:T(8,128)(2,1)S(1)} fusion(bf16[640,1024]{1,0:T(8,128)(2,1)S(1)} %get-tuple-element.109, bf16[640,1024]{1,0:T(8,128)(2,1)S(1)} %get-tuple-element.107, bf16[640,1024]{1,0:T(8,128)(2,1)S(1)} %get-tuple-element.105, bf16[640,1024]{1,0:T(8,128)(2,1)S(1)} %get-tuple-element.106, ...), kind=kLoop, calls=%fused_computation | loop fusion | flops 83886080 | bytes 20971520 | tf_op jit(solution)/shard_map/concatenate | solution.py:189
  348.8 3.7 fusion.52
  352.5 3.7 fusion.46
  356.9 3.7 fusion.40
  360.5 4.1 fusion.7.queries
  364.6 3.5 collective-permute-start.27
  381.5 3.5 fusion.36
  387.8 4.0 collective-permute-done.26
  392.8 11.1 %shard_map.82 = bf16[512,640]{1,0:T(8,128)(2,1)S(1)} custom-call(s32[1,640]{1,0:T(1,128)S(1)} %copy-done.4, s32[640,128]{1,0:T(8,128)S(1)} %broadcast_in_dim.431.k_ids, f32[8,640,128]{2,1,0:T(8,128)S(1)} %select_select_fusion.bias, bf16[512,1280]{1,0:T(8,128)(2,1)S(1)} %fusion.7.queries, bf16[1280,512]{1,0:T(8,128)(2,1)S(1)} %fusion.8.keys, ...), custom_call_target="tpu_custom_call" | custom-call | flops 1677721600 | bytes 5242880 | tf_op jit(solution)/shard_map/pallas_call | solution.py:69
  404.1 10.9 %shard_map.83 = bf16[512,640]{1,0:T(8,128)(2,1)S(1)} custom-call(s32[1,640]{1,0:T(1,128)S(1)} %collective-permute-done.22.q_ids, s32[640,128]{1,0:T(8,128)S(1)} %broadcast_in_dim.530.k_ids, f32[8,640,128]{2,1,0:T(8,128)S(1)} %select_select_fusion.bias, bf16[512,1280]{1,0:T(8,128)(2,1)S(1)} %fusion.7.queries, bf16[1280,512]{1,0:T(8,128)(2,1)S(1)} %fusion.8.keys, ...), custom_call_target="tpu_custom_call" | custom-call | flops 1677721600 | bytes 5242880 | tf_op jit(solution)/shard_map/pallas_call | solution.py:69
  429.4 3.5 fusion.10
  442.2 12.9 %collective-permute-done.35 = bf16[640,512]{0,1:T(8,128)(2,1)S(1)} collective-permute-done((bf16[640,512]{0,1:T(8,128)(2,1)S(1)}, bf16[640,512]{0,1:T(8,128)(2,1)S(1)}, u32[]{:S(2)}, u32[]{:S(2)}) %collective-permute-start.35) | collective-permute-done | bytes 655392 | tf_op jit(solution)/shard_map/ppermute | solution.py:106
  456.9 8.0 %collective-permute-done.30 = bf16[1280,512]{0,1:T(8,128)(2,1)} collective-permute-done((bf16[1280,512]{0,1:T(8,128)(2,1)}, bf16[1280,512]{0,1:T(8,128)(2,1)}, u32[]{:S(2)}, u32[]{:S(2)}) %collective-permute-start.30) | collective-permute-done | bytes 1310752 | tf_op jit(solution)/shard_map/ppermute | solution.py:106
  468.4 9.5 %collective-permute-done.36 = bf16[640,512]{0,1:T(8,128)(2,1)S(1)} collective-permute-done((bf16[640,512]{0,1:T(8,128)(2,1)S(1)}, bf16[640,512]{0,1:T(8,128)(2,1)S(1)}, u32[]{:S(2)}, u32[]{:S(2)}) %collective-permute-start.36) | collective-permute-done | bytes 655392 | tf_op jit(solution)/shard_map/ppermute | solution.py:106
  478.1 4.8 collective-permute-done.31
  485.2 3.6 fusion.35
  (172 shorter events, 106.3 us)
Async XLA Ops:
  16.7 32.1 %collective-permute-start.5 = (bf16[640,1024]{1,0:T(8,128)(2,1)}, bf16[640,1024]{1,0:T(8,128)(2,1)}, u32[]{:S(2)}, u32[]{:S(2)}) collective-permute-start(bf16[640,1024]{1,0:T(8,128)(2,1)} %param.8), channel_id=1, source_target_pairs={{0,4},{4,0},{8,12},{12,8},{16,20},{20,16},{24,28},{28,24},{1,5},{5... | collective-permute-start | bytes 3932168 | tf_op jit(solution)/shard_map/ppermute | solution.py:106
  19.4 40.5 %collective-permute-start.1 = (bf16[512,512]{1,0:T(8,128)(2,1)}, bf16[512,512]{1,0:T(8,128)(2,1)S(1)}, u32[]{:S(2)}, u32[]{:S(2)}) collective-permute-start(bf16[512,512]{1,0:T(8,128)(2,1)} %get-tuple-element.15), channel_id=1, source_target_pairs={{0,4},{4,0},{8,12},{12,8},{16,20},{20,16},{24,28},{28,24},{1,5},{5... | collective-permute-start | bytes 1572872 | tf_op jit(solution)/shard_map/ppermute | solution.py:106
  19.7 57.2 %collective-permute-start.3 = (bf16[640,1024]{1,0:T(8,128)(2,1)}, bf16[640,1024]{1,0:T(8,128)(2,1)}, u32[]{:S(2)}, u32[]{:S(2)}) collective-permute-start(bf16[640,1024]{1,0:T(8,128)(2,1)} %param.8), channel_id=1, source_target_pairs={{0,2},{1,3},{2,0},{3,1},{4,6},{5,7},{6,4},{7,5},{8,10},{9,11},{10,... | collective-permute-start | bytes 3932168 | tf_op jit(solution)/shard_map/ppermute | solution.py:106
  48.8 20.6 %collective-permute-start.17 = (bf16[512,512]{1,0:T(8,128)(2,1)S(1)}, bf16[512,512]{1,0:T(8,128)(2,1)S(1)}, u32[]{:S(2)}, u32[]{:S(2)}) collective-permute-start(bf16[512,512]{1,0:T(8,128)(2,1)S(1)} %get-tuple-element.17), channel_id=1, source_target_pairs={{0,4},{4,0},{8,12},{12,8},{16,20},{20,16},{24,28},{28,24},{1,5},{5... | collective-permute-start | bytes 1572872 | tf_op jit(solution)/shard_map/ppermute | solution.py:106
  50.9 27.9 %collective-permute-start.13 = (bf16[1024,512]{1,0:T(8,128)(2,1)S(1)}, bf16[1024,512]{1,0:T(8,128)(2,1)S(1)}, u32[]{:S(2)}, u32[]{:S(2)}) collective-permute-start(bf16[1024,512]{1,0:T(8,128)(2,1)S(1)} %maximum_select_fusion), channel_id=1, source_target_pairs={{0,8},{4,12},{8,16},{12,20},{16,24},{20,28},{24,0},{28,4},{1,9},{5... | collective-permute-start | bytes 3145736 | tf_op jit(solution)/shard_map/ppermute | solution.py:123
  52.5 61.1 %collective-permute-start.14 = (bf16[1024,512]{1,0:T(8,128)(2,1)S(1)}, bf16[1024,512]{1,0:T(8,128)(2,1)S(1)}, u32[]{:S(2)}, u32[]{:S(2)}) collective-permute-start(bf16[1024,512]{1,0:T(8,128)(2,1)S(1)} %maximum_select_fusion), channel_id=1, source_target_pairs={{0,24},{4,28},{8,0},{12,4},{16,8},{20,12},{24,16},{28,20},{1,25},{... | collective-permute-start | bytes 3145736 | tf_op jit(solution)/shard_map/ppermute | solution.py:123
  61.3 62.5 %collective-permute-start.9 = (bf16[1024,512]{1,0:T(8,128)(2,1)}, bf16[1024,512]{1,0:T(8,128)(2,1)S(1)}, u32[]{:S(2)}, u32[]{:S(2)}) collective-permute-start(bf16[1024,512]{1,0:T(8,128)(2,1)} %maximum_select_fusion.1), channel_id=1, source_target_pairs={{0,8},{4,12},{8,16},{12,20},{16,24},{20,28},{24,0},{28,4},{1,9},{5... | collective-permute-start | bytes 3145736 | tf_op jit(solution)/shard_map/ppermute | solution.py:123
  73.0 52.4 %collective-permute-start.23 = (bf16[512,512]{1,0:T(8,128)(2,1)S(1)}, bf16[512,512]{1,0:T(8,128)(2,1)S(1)}, u32[]{:S(2)}, u32[]{:S(2)}) collective-permute-start(bf16[512,512]{1,0:T(8,128)(2,1)S(1)} %get-tuple-element.21), channel_id=1, source_target_pairs={{0,4},{4,0},{8,12},{12,8},{16,20},{20,16},{24,28},{28,24},{1,5},{5... | collective-permute-start | bytes 1572872 | tf_op jit(solution)/shard_map/ppermute | solution.py:106
  76.9 83.8 %collective-permute-start.2 = (bf16[640,1024]{1,0:T(8,128)(2,1)}, bf16[640,1024]{1,0:T(8,128)(2,1)}, u32[]{:S(2)}, u32[]{:S(2)}) collective-permute-start(bf16[640,1024]{1,0:T(8,128)(2,1)} %param.8), channel_id=1, source_target_pairs={{0,1},{1,0},{2,3},{3,2},{4,5},{5,4},{6,7},{7,6},{8,9},{9,8},{10,11... | collective-permute-start | bytes 3932168 | tf_op jit(solution)/shard_map/ppermute | solution.py:106
  78.9 62.3 %collective-permute-start.10 = (bf16[1024,512]{1,0:T(8,128)(2,1)}, bf16[1024,512]{1,0:T(8,128)(2,1)}, u32[]{:S(2)}, u32[]{:S(2)}) collective-permute-start(bf16[1024,512]{1,0:T(8,128)(2,1)} %maximum_select_fusion.1), channel_id=1, source_target_pairs={{0,24},{4,28},{8,0},{12,4},{16,8},{20,12},{24,16},{28,20},{1,25},{... | collective-permute-start | bytes 3145736 | tf_op jit(solution)/shard_map/ppermute | solution.py:123
  113.6 48.6 %collective-permute-start.4 = (bf16[640,1024]{1,0:T(8,128)(2,1)}, bf16[640,1024]{1,0:T(8,128)(2,1)}, u32[]{:S(2)}, u32[]{:S(2)}) collective-permute-start(bf16[640,1024]{1,0:T(8,128)(2,1)} %collective-permute-done.3), channel_id=1, source_target_pairs={{0,1},{1,0},{2,3},{3,2},{4,5},{5,4},{6,7},{7,6},{8,9},{9,8},{10,11... | collective-permute-start | bytes 3932168 | tf_op jit(solution)/shard_map/ppermute | solution.py:106
  123.9 21.3 %collective-permute-start.7 = (bf16[640,1024]{1,0:T(8,128)(2,1)}, bf16[640,1024]{1,0:T(8,128)(2,1)}, u32[]{:S(2)}, u32[]{:S(2)}) collective-permute-start(bf16[640,1024]{1,0:T(8,128)(2,1)} %collective-permute-done.5), channel_id=1, source_target_pairs={{0,2},{1,3},{2,0},{3,1},{4,6},{5,7},{6,4},{7,5},{8,10},{9,11},{10,... | collective-permute-start | bytes 3932168 | tf_op jit(solution)/shard_map/ppermute | solution.py:106
  125.4 37.5 %collective-permute-start.6 = (bf16[640,1024]{1,0:T(8,128)(2,1)}, bf16[640,1024]{1,0:T(8,128)(2,1)}, u32[]{:S(2)}, u32[]{:S(2)}) collective-permute-start(bf16[640,1024]{1,0:T(8,128)(2,1)} %collective-permute-done.5), channel_id=1, source_target_pairs={{0,1},{1,0},{2,3},{3,2},{4,5},{5,4},{6,7},{7,6},{8,9},{9,8},{10,11... | collective-permute-start | bytes 3932168 | tf_op jit(solution)/shard_map/ppermute | solution.py:106
  141.2 65.2 %collective-permute-start.18 = (bf16[1024,512]{1,0:T(8,128)(2,1)S(1)}, bf16[1024,512]{1,0:T(8,128)(2,1)S(1)}, u32[]{:S(2)}, u32[]{:S(2)}) collective-permute-start(bf16[1024,512]{1,0:T(8,128)(2,1)S(1)} %copy-done.9), channel_id=1, source_target_pairs={{0,8},{4,12},{8,16},{12,20},{16,24},{20,28},{24,0},{28,4},{1,9},{5... | collective-permute-start | bytes 3145736 | tf_op jit(solution)/shard_map/ppermute | solution.py:123
  145.1 48.6 %collective-permute-start.19 = (bf16[1024,512]{1,0:T(8,128)(2,1)S(1)}, bf16[1024,512]{1,0:T(8,128)(2,1)S(1)}, u32[]{:S(2)}, u32[]{:S(2)}) collective-permute-start(bf16[1024,512]{1,0:T(8,128)(2,1)S(1)} %copy-done.9), channel_id=1, source_target_pairs={{0,24},{4,28},{8,0},{12,4},{16,8},{20,12},{24,16},{28,20},{1,25},{... | collective-permute-start | bytes 3145736 | tf_op jit(solution)/shard_map/ppermute | solution.py:123
  160.7 71.3 %collective-permute-start.24 = (bf16[1024,512]{1,0:T(8,128)(2,1)S(1)}, bf16[1024,512]{1,0:T(8,128)(2,1)S(1)}, u32[]{:S(2)}, u32[]{:S(2)}) collective-permute-start(bf16[1024,512]{1,0:T(8,128)(2,1)S(1)} %get-tuple-element.22), channel_id=1, source_target_pairs={{0,24},{4,28},{8,0},{12,4},{16,8},{20,12},{24,16},{28,20},{1,25},{... | collective-permute-start | bytes 3145736 | tf_op jit(solution)/shard_map/ppermute | solution.py:123
  162.2 89.5 %collective-permute-start.25 = (bf16[1024,512]{1,0:T(8,128)(2,1)S(1)}, bf16[1024,512]{1,0:T(8,128)(2,1)S(1)}, u32[]{:S(2)}, u32[]{:S(2)}) collective-permute-start(bf16[1024,512]{1,0:T(8,128)(2,1)S(1)} %get-tuple-element.22), channel_id=1, source_target_pairs={{0,8},{4,12},{8,16},{12,20},{16,24},{20,28},{24,0},{28,4},{1,9},{5... | collective-permute-start | bytes 3145736 | tf_op jit(solution)/shard_map/ppermute | solution.py:123
  162.9 102.9 %collective-permute-start.8 = (bf16[640,1024]{1,0:T(8,128)(2,1)}, bf16[640,1024]{1,0:T(8,128)(2,1)S(1)}, u32[]{:S(2)}, u32[]{:S(2)}) collective-permute-start(bf16[640,1024]{1,0:T(8,128)(2,1)} %collective-permute-done.7), channel_id=1, source_target_pairs={{0,1},{1,0},{2,3},{3,2},{4,5},{5,4},{6,7},{7,6},{8,9},{9,8},{10,11... | collective-permute-start | bytes 3932168 | tf_op jit(solution)/shard_map/ppermute | solution.py:106
  193.7 177.7 %collective-permute-start.15 = (bf16[512,512]{1,0:T(8,128)(2,1)}, bf16[512,512]{1,0:T(8,128)(2,1)}, u32[]{:S(2)}, u32[]{:S(2)}) collective-permute-start(bf16[512,512]{1,0:T(8,128)(2,1)} %slice.189), channel_id=1, source_target_pairs={{0,8},{4,12},{8,16},{12,20},{16,24},{20,28},{24,0},{28,4},{1,9},{5... | collective-permute-start | bytes 1572872 | tf_op jit(solution)/shard_map/ppermute | solution.py:123
  206.4 164.9 %collective-permute-start.16 = (bf16[512,512]{1,0:T(8,128)(2,1)S(1)}, bf16[512,512]{1,0:T(8,128)(2,1)}, u32[]{:S(2)}, u32[]{:S(2)}) collective-permute-start(bf16[512,512]{1,0:T(8,128)(2,1)S(1)} %slice.190), channel_id=1, source_target_pairs={{0,24},{4,28},{8,0},{12,4},{16,8},{20,12},{24,16},{28,20},{1,25},{... | collective-permute-start | bytes 1572872 | tf_op jit(solution)/shard_map/ppermute | solution.py:123
  232.0 124.3 %collective-permute-start.11 = (bf16[512,512]{1,0:T(8,128)(2,1)}, bf16[512,512]{1,0:T(8,128)(2,1)}, u32[]{:S(2)}, u32[]{:S(2)}) collective-permute-start(bf16[512,512]{1,0:T(8,128)(2,1)} %slice.187), channel_id=1, source_target_pairs={{0,8},{4,12},{8,16},{12,20},{16,24},{20,28},{24,0},{28,4},{1,9},{5... | collective-permute-start | bytes 1572872 | tf_op jit(solution)/shard_map/ppermute | solution.py:123
  251.7 105.1 %collective-permute-start.12 = (bf16[512,512]{1,0:T(8,128)(2,1)}, bf16[512,512]{1,0:T(8,128)(2,1)}, u32[]{:S(2)}, u32[]{:S(2)}) collective-permute-start(bf16[512,512]{1,0:T(8,128)(2,1)} %slice.188), channel_id=1, source_target_pairs={{0,24},{4,28},{8,0},{12,4},{16,8},{20,12},{24,16},{28,20},{1,25},{... | collective-permute-start | bytes 1572872 | tf_op jit(solution)/shard_map/ppermute | solution.py:123
  265.8 115.7 %collective-permute-start.21 = (bf16[512,512]{1,0:T(8,128)(2,1)S(1)}, bf16[512,512]{1,0:T(8,128)(2,1)}, u32[]{:S(2)}, u32[]{:S(2)}) collective-permute-start(bf16[512,512]{1,0:T(8,128)(2,1)S(1)} %slice.192), channel_id=1, source_target_pairs={{0,24},{4,28},{8,0},{12,4},{16,8},{20,12},{24,16},{28,20},{1,25},{... | collective-permute-start | bytes 1572872 | tf_op jit(solution)/shard_map/ppermute | solution.py:123
  356.3 25.3 %collective-permute-start.20 = (bf16[512,512]{1,0:T(8,128)(2,1)S(1)}, bf16[512,512]{1,0:T(8,128)(2,1)S(1)}, u32[]{:S(2)}, u32[]{:S(2)}) collective-permute-start(bf16[512,512]{1,0:T(8,128)(2,1)S(1)} %copy-done.11), channel_id=1, source_target_pairs={{0,8},{4,12},{8,16},{12,20},{16,24},{20,28},{24,0},{28,4},{1,9},{5... | collective-permute-start | bytes 1572872 | tf_op jit(solution)/shard_map/ppermute | solution.py:123
  364.6 50.4 %collective-permute-start.27 = (bf16[512,512]{1,0:T(8,128)(2,1)S(1)}, bf16[512,512]{1,0:T(8,128)(2,1)S(1)}, u32[]{:S(2)}, u32[]{:S(2)}) collective-permute-start(bf16[512,512]{1,0:T(8,128)(2,1)S(1)} %slice.194), channel_id=1, source_target_pairs={{0,24},{4,28},{8,0},{12,4},{16,8},{20,12},{24,16},{28,20},{1,25},{... | collective-permute-start | bytes 1572872 | tf_op jit(solution)/shard_map/ppermute | solution.py:123
  376.3 15.5 %collective-permute-start.26 = (bf16[512,512]{1,0:T(8,128)(2,1)S(1)}, bf16[512,512]{1,0:T(8,128)(2,1)S(1)}, u32[]{:S(2)}, u32[]{:S(2)}) collective-permute-start(bf16[512,512]{1,0:T(8,128)(2,1)S(1)} %copy-done.12), channel_id=1, source_target_pairs={{0,8},{4,12},{8,16},{12,20},{16,24},{20,28},{24,0},{28,4},{1,9},{5... | collective-permute-start | bytes 1572872 | tf_op jit(solution)/shard_map/ppermute | solution.py:123
  428.9 28.0 %collective-permute-start.28 = (bf16[1280,512]{0,1:T(8,128)(2,1)}, bf16[1280,512]{0,1:T(8,128)(2,1)}, u32[]{:S(2)}, u32[]{:S(2)}) collective-permute-start(bf16[1280,512]{0,1:T(8,128)(2,1)} %convolution_convert_fusion.3), channel_id=1, source_target_pairs={{0,1},{1,0},{2,3},{3,2},{4,5},{5,4},{6,7},{7,6},{8,9},{9,8},{10,11... | collective-permute-start | bytes 3932168 | tf_op jit(solution)/shard_map/ppermute | solution.py:106
  432.9 32.0 %collective-permute-start.30 = (bf16[1280,512]{0,1:T(8,128)(2,1)}, bf16[1280,512]{0,1:T(8,128)(2,1)}, u32[]{:S(2)}, u32[]{:S(2)}) collective-permute-start(bf16[1280,512]{0,1:T(8,128)(2,1)} %fusion.10), channel_id=1, source_target_pairs={{0,2},{1,3},{2,0},{3,1},{4,6},{5,7},{6,4},{7,5},{8,10},{9,11},{10,... | collective-permute-start | bytes 3932168 | tf_op jit(solution)/shard_map/ppermute | solution.py:106
  437.4 17.7 %collective-permute-start.35 = (bf16[640,512]{0,1:T(8,128)(2,1)S(1)}, bf16[640,512]{0,1:T(8,128)(2,1)S(1)}, u32[]{:S(2)}, u32[]{:S(2)}) collective-permute-start(bf16[640,512]{0,1:T(8,128)(2,1)S(1)} %slice.247), channel_id=1, source_target_pairs={{0,4},{4,0},{8,12},{12,8},{16,20},{20,16},{24,28},{28,24},{1,5},{5... | collective-permute-start | bytes 1966088 | tf_op jit(solution)/shard_map/ppermute | solution.py:106
  440.6 27.8 %collective-permute-start.33 = (bf16[640,512]{0,1:T(8,128)(2,1)S(1)}, bf16[640,512]{0,1:T(8,128)(2,1)S(1)}, u32[]{:S(2)}, u32[]{:S(2)}) collective-permute-start(bf16[640,512]{0,1:T(8,128)(2,1)S(1)} %slice.248), channel_id=1, source_target_pairs={{0,4},{4,0},{8,12},{12,8},{16,20},{20,16},{24,28},{28,24},{1,5},{5... | collective-permute-start | bytes 1966088 | tf_op jit(solution)/shard_map/ppermute | solution.py:106
  455.3 22.6 %collective-permute-start.36 = (bf16[640,512]{0,1:T(8,128)(2,1)S(1)}, bf16[640,512]{0,1:T(8,128)(2,1)S(1)}, u32[]{:S(2)}, u32[]{:S(2)}) collective-permute-start(bf16[640,512]{0,1:T(8,128)(2,1)S(1)} %fusion.57), channel_id=1, source_target_pairs={{0,2},{1,3},{2,0},{3,1},{4,6},{5,7},{6,4},{7,5},{8,10},{9,11},{10,... | collective-permute-start | bytes 1966088 | tf_op jit(solution)/shard_map/ppermute | solution.py:106
  467.8 15.0 %collective-permute-start.31 = (bf16[640,512]{0,1:T(8,128)(2,1)S(1)}, bf16[640,512]{0,1:T(8,128)(2,1)S(1)}, u32[]{:S(2)}, u32[]{:S(2)}) collective-permute-start(bf16[640,512]{0,1:T(8,128)(2,1)S(1)} %slice.249), channel_id=1, source_target_pairs={{0,4},{4,0},{8,12},{12,8},{16,20},{20,16},{24,28},{28,24},{1,5},{5... | collective-permute-start | bytes 1966088 | tf_op jit(solution)/shard_map/ppermute | solution.py:106
  (33 other events, 522.9 us)

commit v6 on v5

v6 whole, which is shorter than its diff:
```python
import functools

import jax
import jax.numpy as jnp
from jax import lax
from jax.experimental import pallas as pl
from jax.experimental.pallas import tpu as pltpu
from jax.sharding import PartitionSpec as P

PASSAGE = 256
BLOCK = 128

norm_epsilon = 1e-06
bucket_edges = (12, 16, 23, 32, 46, 64, 91)
masked_score = -1e30


def bucket_of(offsets):
    distance = jnp.abs(offsets)
    reached = sum(((distance >= threshold).astype(jnp.int32) for threshold in bucket_edges))
    within = jnp.where(distance < 8, distance, 8 + reached)
    return within + jnp.where(offsets > 0, 16, 0)


def bias_tiles(table):
    rows = 2 * PASSAGE + BLOCK
    offsets = (
        jnp.arange(rows, dtype=jnp.int32)[:, None]
        - PASSAGE
        - jnp.arange(BLOCK, dtype=jnp.int32)[None, :]
    )
    buckets = bucket_of(offsets)[None]
    tiles = jnp.zeros((table.shape[1], rows, BLOCK), jnp.float32)
    for level in range(table.shape[0]):
        tiles = jnp.where(buckets == level, table[level][:, None, None], tiles)
    return tiles


def attention_kernel(width, q_ids, k_ids, bias, queries, keys, values, out):
    length = keys.shape[0]
    blocks = length // BLOCK
    reach = PASSAGE // BLOCK
    heads = keys.shape[1] // width
    turned = jnp.transpose(values[...].astype(jnp.float32)).astype(jnp.bfloat16)
    head_of = lax.broadcasted_iota(jnp.int32, (BLOCK, keys.shape[1]), 1) // width
    for i in range(blocks):
        low, high = max(0, i - reach) * BLOCK, min(blocks, i + reach + 1) * BLOCK
        columns = slice(i * BLOCK, (i + 1) * BLOCK)
        first = low - i * BLOCK + PASSAGE
        same = k_ids[low:high, :] == q_ids[:, columns]
        own = queries[columns, :]
        results = []
        for h in range(heads):
            chosen = jnp.where(head_of == h, own, jnp.zeros_like(own))
            scores = lax.dot_general(
                keys[low:high, :],
                chosen,
                (((1,), (1,)), ((), ())),
                preferred_element_type=jnp.float32,
            )
            scores = jnp.where(same, scores + bias[h, first : first + high - low, :], masked_score)
            raised = jnp.exp(scores - jnp.max(scores, axis=0, keepdims=True)).astype(jnp.bfloat16)
            extended = jnp.concatenate(
                [
                    turned[h * width : (h + 1) * width, low:high],
                    jnp.ones((16, high - low), jnp.bfloat16),
                ],
                axis=0,
            )
            total = jnp.dot(extended, raised, preferred_element_type=jnp.float32)
            results.append(total[:width] / total[width : width + 1])
        out[columns, :] = jnp.transpose(jnp.concatenate(results, axis=0)).astype(jnp.bfloat16)


def attend(queries, keys, values, ids, bias, width):
    groups, length = ids.shape
    features = keys.shape[1]
    heads = 128 // width
    wide_ids = jnp.broadcast_to(ids.reshape(-1)[:, None], (groups * length, BLOCK))
    block = pl.BlockSpec((length, 128), lambda g, p: (g, p))
    return pl.pallas_call(
        functools.partial(attention_kernel, width),
        grid=(groups, features // 128),
        in_specs=[
            pl.BlockSpec((None, 1, length), lambda g, p: (g, 0, 0)),
            pl.BlockSpec((length, BLOCK), lambda g, p: (g, 0)),
            pl.BlockSpec((heads,) + bias.shape[1:], lambda g, p: (p, 0, 0)),
            block,
            block,
            block,
        ],
        out_specs=block,
        out_shape=jax.ShapeDtypeStruct(queries.shape, jnp.bfloat16),
        compiler_params=pltpu.CompilerParams(vmem_limit_bytes=24 * 1024 * 1024),
        cost_estimate=pl.CostEstimate(
            flops=8 * groups * features * length * length,
            bytes_accessed=16 * groups * features * length,
            transcendentals=groups * features // width * length * length,
        ),
    )(ids[:, None, :], wide_ids, bias, queries, keys, values)


def normalise_kernel(count, gains, *refs):
    out = refs[-1]
    for group in range(2):

        @pl.when(pl.program_id(0) == group)
        def _():
            parts = [
                ref[...].astype(jnp.float32) for ref in refs[group * count : (group + 1) * count]
            ]
            size = parts[0].shape[1]
            squares = sum(jnp.sum(part * part, axis=1, keepdims=True) for part in parts)
            scale = lax.rsqrt(squares / (size * count) + norm_epsilon)
            for k, part in enumerate(parts):
                out[:, k * size : (k + 1) * size] = (part * scale * gains[k : k + 1, :]).astype(
                    jnp.bfloat16
                )


def normalise(own, peer, gains):
    length, size = own[0].shape
    count = len(own)
    steps = length // BLOCK
    first = pl.BlockSpec((BLOCK, size), lambda g, i: (jnp.where(g == 0, i, steps - 1), 0))
    second = pl.BlockSpec((BLOCK, size), lambda g, i: (jnp.where(g == 0, 0, i), 0))
    return pl.pallas_call(
        functools.partial(normalise_kernel, count),
        grid=(2, steps),
        in_specs=[pl.BlockSpec(gains.shape, lambda g, i: (0, 0))]
        + [first] * count
        + [second] * count,
        out_specs=pl.BlockSpec((BLOCK, size * count), lambda g, i: (g * steps + i, 0)),
        out_shape=jax.ShapeDtypeStruct((2 * length, size * count), jnp.bfloat16),
        compiler_params=pltpu.CompilerParams(vmem_limit_bytes=24 * 1024 * 1024),
        cost_estimate=pl.CostEstimate(
            flops=16 * length * size * count,
            bytes_accessed=8 * length * size * count,
            transcendentals=2 * length,
        ),
    )(gains, *own, *peer)


def after(value, earlier):
    return lax.optimization_barrier((value, earlier))[0]


def per_device(n_batch, n_hidden, tokens, segments, rel_bias, ln_gain, w_query, w_key, w_value, w_out):
    place = lax.axis_index("batch")
    column = lax.axis_index("hidden")
    parity = place & 1
    length, own_width = tokens.shape
    heads = rel_bias.shape[1] // 2
    half = w_query.shape[1] // 2
    width = half // heads

    def swap(value, step, axis="batch"):
        count = n_batch if axis == "batch" else n_hidden
        return lax.ppermute(value, axis, [(i, i ^ step) for i in range(count)])

    pairs = n_batch // 2
    pair = place >> 1

    def swapped(weight, axis, *earlier):
        size = weight.shape[axis] // 2
        kept, given = [
            lax.dynamic_slice_in_dim(weight, side * size, size, axis)
            for side in (parity, 1 - parity)
        ]
        if earlier:
            given = after(given, earlier)
        taken = swap(given, 1)
        return jnp.where(parity == 0, jnp.concatenate([kept, taken]), jnp.concatenate([taken, kept]))

    def exchange(value, shift):
        def partner(i):
            other = ((i // 2 + shift) ^ 1) - shift
            return other % pairs * 2 + i % 2

        return lax.ppermute(value, "batch", [(i, partner(i)) for i in range(n_batch)])

    def meet(value, *earlier):
        if earlier:
            value = after(value, earlier)
        return [exchange(value, 0), exchange(value, 1)]

    sign = 1 - 2 * (pair & 1)
    steps = [0]
    for step in range(1, pairs // 2):
        steps += [step, -step] if step % 2 else [-step, step]
    steps.append(pairs // 2)

    def round_ring(block, received, *earlier):
        blocks, flows = [block, *received], list(received)
        for step in range(2, pairs // 2):
            flows = [exchange(flows[0], 1 - step % 2), exchange(flows[1], step % 2)]
            blocks += flows
        middle = block.shape[0] // 2
        ends = [flows[0][:middle], flows[1][middle:]]
        if earlier:
            ends = [after(end, wait) for end, wait in zip(ends, earlier)]
        blocks.append(jnp.concatenate([exchange(ends[0], 1), exchange(ends[1], 0)]))
        return blocks

    key_block = swapped(w_key, 1)
    key_hops = meet(key_block)
    query_block = swapped(w_query, 1, key_block)

    across = swap(tokens, 2, "hidden")
    peer_tokens = swap(after(tokens, key_block), 1)
    peer_ids = swap(segments, 1)
    query_hops = meet(query_block, across)
    peer_across = swap(after(peer_tokens, key_hops), 2, "hidden")
    value_block = swapped(w_value, 1, query_block)
    value_hops = meet(value_block, *key_hops)
    out_block = swapped(w_out, 0, value_block)
    out_hops = meet(out_block, *query_hops, peer_across)

    def all_features(here, there):
        return [here, swap(here, 1, "hidden"), there, swap(there, 1, "hidden")]

    gathered = [all_features(tokens, across), all_features(peer_tokens, peer_across)]

    key_blocks = round_ring(key_block, key_hops)
    query_blocks = round_ring(query_block, query_hops)
    value_blocks = round_ring(value_block, value_hops, gathered[1][3], gathered[1][1])

    table = lax.dynamic_slice_in_dim(rel_bias, parity * heads, heads, 1)
    bias = bias_tiles(table)

    gains = jnp.stack(
        [
            lax.dynamic_slice_in_dim(ln_gain, (column ^ k) * own_width, own_width, 0)
            for k in range(n_hidden)
        ]
    )
    normed = normalise(*gathered, gains)
    depth = 2 * w_query.shape[0]

    def normed_part(step):
        start = (pair + sign * step) % pairs * depth
        start = ((start // own_width) ^ column) * own_width + start % own_width
        return lax.dynamic_slice_in_dim(normed, start, depth, 1)

    size = max(1, pairs // 4)
    rounds = [slice(i, i + size) for i in range(0, pairs, size)]

    def joined(values, axis):
        return values[0] if len(values) == 1 else jnp.concatenate(values, axis=axis)

    def project(blocks):
        total = None
        for these in rounds:
            part = joined([normed_part(step) for step in steps[these]], 1)
            term = jnp.dot(part, joined(blocks[these], 0), preferred_element_type=jnp.float32)
            total = term if total is None else total + term
        return total.astype(jnp.bfloat16)

    keys = project(key_blocks)
    queries = project(query_blocks)
    values = project(value_blocks)
    out_blocks = round_ring(out_block, out_hops, keys, queries)
    place_of = {step % pairs: i for i, step in enumerate(steps)}
    out_rows = jnp.concatenate([out_blocks[place_of[e]] for e in range(pairs)], axis=0)
    ids = jnp.concatenate([segments, peer_ids], axis=0)
    attended = attend(queries, keys, values, ids, bias, width)

    stripes = own_width // (2 * w_out.shape[1])

    def sums(odd):
        def block(step):
            first = (column ^ step) * stripes
            chosen = [
                lax.dynamic_slice_in_dim(
                    out_rows, (sign * (first + j - pair) % pairs * 2 + odd) * half, half, 0
                )
                for j in range(stripes)
            ]
            chosen = joined(chosen, 1)
            return jnp.dot(attended, chosen, preferred_element_type=jnp.float32)

        far = send(block(3), 1, "hidden")
        near = send(block(1), 1, "hidden")
        return block(0) + near, block(2) + far

    def send(value, step, axis="batch"):
        return swap(value.astype(jnp.bfloat16), step, axis).astype(jnp.float32)

    here, there = sums(0)
    first = here + send(there, 2, "hidden")
    first = first[:length] + send(first[length:], 1)
    here, there = sums(1)
    there = there[:length] + send(there[length:], 1)
    second = here[:length] + send(here[length:], 1) + send(there, 2, "hidden")

    parts = [v.reshape(length, stripes, w_out.shape[1]) for v in (first, second)]
    combined = jnp.stack(parts, 2)
    return (tokens.astype(jnp.float32) + combined.reshape(length, own_width)).astype(jnp.bfloat16)


def solution(mesh):
    placed = (
        P("batch", "hidden"),
        P("batch", None),
        P(None, "hidden"),
        P(),
        P("batch", "hidden"),
        P("batch", "hidden"),
        P("batch", "hidden"),
        P("hidden", "batch"),
    )
    return jax.shard_map(
        functools.partial(per_device, mesh.shape["batch"], mesh.shape["hidden"]),
        mesh=mesh,
        in_specs=placed,
        out_specs=P("batch", "hidden"),
        check_vma=False,
    )
```

time: 493 us -> 410 us (0.83)
  the two profiles are of different devices: /device:TPU:0 before, /device:TPU:20 now
where the time goes in v6:
time: 410 us; the launch traced here: 405 us
  waiting for transfers between devices  245 us (60%)
  matrix products  52.1 us (13%)
  Pallas kernels  31.6 us (8%)
  other arithmetic  25.6 us (6%)
  starting transfers between devices  24.9 us (6%)
  local copies, waits for them, and re-layouts  24.6 us (6%)
    ppermute x16, waiting for transfers between devices, exchange(): lax.ppermute(value, 'batch', [(i, partner(i)) for i in range(n_batch)])  154 us
    ppermute x21, waiting for transfers between devices, swap(): return lax.ppermute(value, axis, [(i, i ^ step) for i in range(count)])  90.9 us
    dot_general x12, matrix products, project(): jnp.dot(part, joined(blocks[these], 0), preferred_element_type=jnp.float32)  28.7 us
    dot_general x8, matrix products, block(): return jnp.dot(attended, chosen, preferred_element_type=jnp.float32)  23.4 us
    pallas_call x1, Pallas kernels, attend(): pl.pallas_call(functools.partial(attention_kernel, width), grid=(groups,...  22.7 us
    ppermute x21, starting transfers between devices, swap(): return lax.ppermute(value, axis, [(i, i ^ step) for i in range(count)])  16.5 us
    select_n x1, other arithmetic, bias_tiles(): tiles = jnp.where(buckets == level, table[level][:, None, None], tiles)  11 us
    pallas_call x1, Pallas kernels, normalise(): pl.pallas_call(functools.partial(normalise_kernel, count), grid=(2, steps...  8.95 us
  transfers between devices with their start and end apart: 37, of which 19 were waited for; matrix products, arithmetic and copies ran while one was open for 21% of the time, Pallas kernels for 8%

profile of v6, /device:TPU:20, one launch (start us, length us, event | category | flops | bytes accessed | tf_op | source)
XLA Modules:
  0.0 404.7 jit_solution(8447832793790032147)
XLA Ops:
  3.6 11.7 %collective-permute-done.4 = bf16[512,512]{1,0:T(8,128)(2,1)} collective-permute-done((bf16[512,512]{1,0:T(8,128)(2,1)S(1)}, bf16[512,512]{1,0:T(8,128)(2,1)}, u32[]{:S(2)}, u32[]{:S(2)}) %collective-permute-start.4) | collective-permute-done | bytes 524320 | tf_op jit(solution)/shard_map/ppermute | solution.py:159
  20.7 11.1 %collective-permute-done.11 = bf16[512,512]{1,0:T(8,128)(2,1)S(1)} collective-permute-done((bf16[512,512]{1,0:T(8,128)(2,1)S(1)}, bf16[512,512]{1,0:T(8,128)(2,1)S(1)}, u32[]{:S(2)}, u32[]{:S(2)}) %collective-permute-start.11) | collective-permute-done | bytes 524320 | tf_op jit(solution)/shard_map/ppermute | solution.py:159
  35.4 33.6 %collective-permute-done.18 = bf16[512,512]{1,0:T(8,128)(2,1)S(1)} collective-permute-done((bf16[512,512]{1,0:T(8,128)(2,1)S(1)}, bf16[512,512]{1,0:T(8,128)(2,1)S(1)}, u32[]{:S(2)}, u32[]{:S(2)}) %collective-permute-start.18) | collective-permute-done | bytes 524320 | tf_op jit(solution)/shard_map/ppermute | solution.py:159
  72.0 19.8 %collective-permute-done.8 = bf16[1024,512]{1,0:T(8,128)(2,1)} collective-permute-done((bf16[1024,512]{1,0:T(8,128)(2,1)S(1)}, bf16[1024,512]{1,0:T(8,128)(2,1)}, u32[]{:S(2)}, u32[]{:S(2)}) %collective-permute-start.8) | collective-permute-done | bytes 1048608 | tf_op jit(solution)/shard_map/ppermute | solution.py:180
  92.5 21.7 %collective-permute-done.13 = bf16[1024,512]{1,0:T(8,128)(2,1)} collective-permute-done((bf16[1024,512]{1,0:T(8,128)(2,1)S(1)}, bf16[1024,512]{1,0:T(8,128)(2,1)}, u32[]{:S(2)}, u32[]{:S(2)}) %collective-permute-start.13) | collective-permute-done | bytes 1048608 | tf_op jit(solution)/shard_map/ppermute | solution.py:180
  120.0 2.9 constant_dynamic-update-slice_fusion.4
  123.4 32.9 %collective-permute-done.20 = bf16[1024,512]{1,0:T(8,128)(2,1)} collective-permute-done((bf16[1024,512]{1,0:T(8,128)(2,1)}, bf16[1024,512]{1,0:T(8,128)(2,1)}, u32[]{:S(2)}, u32[]{:S(2)}) %collective-permute-start.20) | collective-permute-done | bytes 1048608 | tf_op jit(solution)/shard_map/ppermute | solution.py:180
  156.3 7.1 %collective-permute-done.19 = bf16[1024,512]{1,0:T(8,128)(2,1)} collective-permute-done((bf16[1024,512]{1,0:T(8,128)(2,1)}, bf16[1024,512]{1,0:T(8,128)(2,1)}, u32[]{:S(2)}, u32[]{:S(2)}) %collective-permute-start.19) | collective-permute-done | bytes 1048608 | tf_op jit(solution)/shard_map/ppermute | solution.py:180
  163.5 11.0 %select_select_fusion.bias = f32[8,640,128]{2,1,0:T(8,128)} fusion(f32[8]{0:T(128)S(1)} %get-tuple-element.30, f32[8]{0:T(128)S(1)} %get-tuple-element.31, f32[8]{0:T(128)S(1)} %get-tuple-element.32, f32[8]{0:T(128)S(1)} %get-tuple-element.33, f32[8]{0:T(128)S(1)} %get-tuple-element.34, f32[8]{0:T(128)S(1)} %get-tuple-element.35, ...), kind=kLoop, calls=%fused_computation.24 | loop fusion | flops 20971520 | bytes 5243904 | tf_op jit(solution)/shard_map/jit(_where)/select_n | solution.py:35
  181.0 4.9 %collective-permute-done.24 = bf16[1024,512]{1,0:T(8,128)(2,1)} collective-permute-done((bf16[1024,512]{1,0:T(8,128)(2,1)}, bf16[1024,512]{1,0:T(8,128)(2,1)}, u32[]{:S(2)}, u32[]{:S(2)}) %collective-permute-start.24) | collective-permute-done | bytes 1048608 | tf_op jit(solution)/shard_map/ppermute | solution.py:180
  187.0 23.6 %collective-permute-done.26 = bf16[1024,512]{1,0:T(8,128)(2,1)} collective-permute-done((bf16[1024,512]{1,0:T(8,128)(2,1)}, bf16[1024,512]{1,0:T(8,128)(2,1)}, u32[]{:S(2)}, u32[]{:S(2)}) %collective-permute-start.26) | collective-permute-done | bytes 1048608 | tf_op jit(solution)/shard_map/ppermute | solution.py:180
  216.2 2.9 collective-permute-start.22
  219.0 8.9 %shard_map.82 = bf16[1280,4096]{1,0:T(8,128)(2,1)S(1)} custom-call(f32[4,1024]{1,0:T(4,128)S(1)} %pad_maximum_fusion.1.gains, bf16[640,1024]{1,0:T(8,128)(2,1)S(1)} %copy-done.2, bf16[640,1024]{1,0:T(8,128)(2,1)S(1)} %collective-permute-done.1.refs_1_, bf16[640,1024]{1,0:T(8,128)(2,1)} %collective-permute-done.2.refs_2_, ...), custom_call_target="tpu_custom_call" | custom-call | flops 41943040 | bytes 20971520 | tf_op jit(solution)/shard_map/pallas_call | solution.py:127
  230.8 2.9 fusion.19
  242.1 2.9 fusion.21
  246.7 12.6 %collective-permute-done.14 = bf16[512,512]{1,0:T(8,128)(2,1)S(1)} collective-permute-done((bf16[512,512]{1,0:T(8,128)(2,1)S(1)}, bf16[512,512]{1,0:T(8,128)(2,1)S(1)}, u32[]{:S(2)}, u32[]{:S(2)}) %collective-permute-start.14) | collective-permute-done | bytes 524320 | tf_op jit(solution)/shard_map/ppermute | solution.py:180
  267.1 2.9 fusion.3
  270.0 23.0 %collective-permute-done.21 = bf16[512,512]{1,0:T(8,128)(2,1)S(1)} collective-permute-done((bf16[512,512]{1,0:T(8,128)(2,1)S(1)}, bf16[512,512]{1,0:T(8,128)(2,1)S(1)}, u32[]{:S(2)}, u32[]{:S(2)}) %collective-permute-start.21) | collective-permute-done | bytes 524320 | tf_op jit(solution)/shard_map/ppermute | solution.py:180
  294.6 7.0 %collective-permute-done.25 = bf16[512,512]{1,0:T(8,128)(2,1)S(1)} collective-permute-done((bf16[512,512]{1,0:T(8,128)(2,1)S(1)}, bf16[512,512]{1,0:T(8,128)(2,1)S(1)}, u32[]{:S(2)}, u32[]{:S(2)}) %collective-permute-start.25) | collective-permute-done | bytes 524320 | tf_op jit(solution)/shard_map/ppermute | solution.py:180
  302.6 22.7 %shard_map.83 = bf16[1280,512]{1,0:T(8,128)(2,1)S(1)} custom-call(s32[2,1,640]{2,1,0:T(1,128)S(1)} %broadcast_in_dim.410.q_ids, s32[1280,128]{1,0:T(8,128)S(1)} %broadcast_in_dim.412.k_ids, f32[8,640,128]{2,1,0:T(8,128)S(1)} %copy-done.3, bf16[1280,512]{1,0:T(8,128)(2,1)S(1)} %fusion.4.queries, bf16[1280,512]{1,0:T(8,128)(2,1)S(1)} %fusion.5.keys, ...), custom_call_target="tpu_custom_call" | custom-call | flops 3355443200 | bytes 10485760 | tf_op jit(solution)/shard_map/pallas_call | solution.py:81
  328.5 3.1 convolution_convert_fusion.2
  331.5 3.0 convolution_convert_fusion
  335.0 3.0 convolution_convert_fusion.1
  338.0 3.1 convolution_convert_fusion.3
  341.6 3.5 fusion.7
  356.2 13.2 %collective-permute-done.35 = bf16[640,512]{0,1:T(8,128)(2,1)S(1)} collective-permute-done((bf16[640,512]{0,1:T(8,128)(2,1)}, bf16[640,512]{0,1:T(8,128)(2,1)S(1)}, u32[]{:S(2)}, u32[]{:S(2)}) %collective-permute-start.35) | collective-permute-done | bytes 655392 | tf_op jit(solution)/shard_map/ppermute | solution.py:159
  370.1 7.0 %collective-permute-done.30 = bf16[1280,512]{0,1:T(8,128)(2,1)} collective-permute-done((bf16[1280,512]{0,1:T(8,128)(2,1)}, bf16[1280,512]{0,1:T(8,128)(2,1)}, u32[]{:S(2)}, u32[]{:S(2)}) %collective-permute-start.30) | collective-permute-done | bytes 1310752 | tf_op jit(solution)/shard_map/ppermute | solution.py:159
  377.0 2.9 fusion
  383.3 6.8 %collective-permute-done.36 = bf16[640,512]{0,1:T(8,128)(2,1)S(1)} collective-permute-done((bf16[640,512]{0,1:T(8,128)(2,1)S(1)}, bf16[640,512]{0,1:T(8,128)(2,1)S(1)}, u32[]{:S(2)}, u32[]{:S(2)}) %collective-permute-start.36) | collective-permute-done | bytes 655392 | tf_op jit(solution)/shard_map/ppermute | solution.py:159
  390.2 5.9 %collective-permute-done.31 = bf16[640,512]{0,1:T(8,128)(2,1)S(1)} collective-permute-done((bf16[640,512]{0,1:T(8,128)(2,1)S(1)}, bf16[640,512]{0,1:T(8,128)(2,1)S(1)}, u32[]{:S(2)}, u32[]{:S(2)}) %collective-permute-start.31) | collective-permute-done | bytes 655392 | tf_op jit(solution)/shard_map/ppermute | solution.py:159
  398.0 3.3 copy.15
  401.2 3.3 add_convert_fusion
  (137 shorter events, 80.0 us)
Async XLA Ops:
  2.9 30.9 %collective-permute-start.2 = (bf16[640,1024]{1,0:T(8,128)(2,1)}, bf16[640,1024]{1,0:T(8,128)(2,1)}, u32[]{:S(2)}, u32[]{:S(2)}) collective-permute-start(bf16[640,1024]{1,0:T(8,128)(2,1)} %refs_0_.1), channel_id=1, source_target_pairs={{0,2},{1,3},{2,0},{3,1},{4,6},{5,7},{6,4},{7,5},{8,10},{9,11},{10,... | collective-permute-start | bytes 3932168 | tf_op jit(solution)/shard_map/ppermute | solution.py:159
  18.4 73.4 %collective-permute-start.5 = (bf16[640,1024]{1,0:T(8,128)(2,1)S(1)}, bf16[640,1024]{1,0:T(8,128)(2,1)}, u32[]{:S(2)}, u32[]{:S(2)}) collective-permute-start(bf16[640,1024]{1,0:T(8,128)(2,1)S(1)} %copy-done.2), channel_id=1, source_target_pairs={{0,4},{4,0},{8,12},{12,8},{16,20},{20,16},{24,28},{28,24},{1,5},{5... | collective-permute-start | bytes 3932168 | tf_op jit(solution)/shard_map/ppermute | solution.py:159
  19.0 52.9 %collective-permute-start.7 = (bf16[1024,512]{1,0:T(8,128)(2,1)S(1)}, bf16[1024,512]{1,0:T(8,128)(2,1)}, u32[]{:S(2)}, u32[]{:S(2)}) collective-permute-start(bf16[1024,512]{1,0:T(8,128)(2,1)S(1)} %maximum_select_fusion), channel_id=1, source_target_pairs={{0,8},{4,12},{8,0},{12,4},{16,24},{20,28},{24,16},{28,20},{1,9},{5... | collective-permute-start | bytes 3145736 | tf_op jit(solution)/shard_map/ppermute | solution.py:180
  20.7 71.1 %collective-permute-start.8 = (bf16[1024,512]{1,0:T(8,128)(2,1)S(1)}, bf16[1024,512]{1,0:T(8,128)(2,1)}, u32[]{:S(2)}, u32[]{:S(2)}) collective-permute-start(bf16[1024,512]{1,0:T(8,128)(2,1)S(1)} %maximum_select_fusion), channel_id=1, source_target_pairs={{0,24},{4,28},{8,16},{12,20},{16,8},{20,12},{24,0},{28,4},{1,25},{... | collective-permute-start | bytes 3145736 | tf_op jit(solution)/shard_map/ppermute | solution.py:180
  32.2 36.8 %collective-permute-start.18 = (bf16[512,512]{1,0:T(8,128)(2,1)S(1)}, bf16[512,512]{1,0:T(8,128)(2,1)S(1)}, u32[]{:S(2)}, u32[]{:S(2)}) collective-permute-start(bf16[512,512]{1,0:T(8,128)(2,1)S(1)} %get-tuple-element.21), channel_id=1, source_target_pairs={{0,4},{4,0},{8,12},{12,8},{16,20},{20,16},{24,28},{28,24},{1,5},{5... | collective-permute-start | bytes 1572872 | tf_op jit(solution)/shard_map/ppermute | solution.py:159
  33.8 80.5 %collective-permute-start.13 = (bf16[1024,512]{1,0:T(8,128)(2,1)S(1)}, bf16[1024,512]{1,0:T(8,128)(2,1)}, u32[]{:S(2)}, u32[]{:S(2)}) collective-permute-start(bf16[1024,512]{1,0:T(8,128)(2,1)S(1)} %maximum_select_fusion.1), channel_id=1, source_target_pairs={{0,24},{4,28},{8,16},{12,20},{16,8},{20,12},{24,0},{28,4},{1,25},{... | collective-permute-start | bytes 3145736 | tf_op jit(solution)/shard_map/ppermute | solution.py:180
  70.5 22.0 %collective-permute-start.23 = (bf16[512,512]{1,0:T(8,128)(2,1)}, bf16[512,512]{1,0:T(8,128)(2,1)}, u32[]{:S(2)}, u32[]{:S(2)}) collective-permute-start(bf16[512,512]{1,0:T(8,128)(2,1)} %get-tuple-element.25), channel_id=1, source_target_pairs={{0,4},{4,0},{8,12},{12,8},{16,20},{20,16},{24,28},{28,24},{1,5},{5... | collective-permute-start | bytes 1572872 | tf_op jit(solution)/shard_map/ppermute | solution.py:159
  91.8 31.0 %collective-permute-start.9 = (bf16[640,1024]{1,0:T(8,128)(2,1)}, bf16[640,1024]{1,0:T(8,128)(2,1)}, u32[]{:S(2)}, u32[]{:S(2)}) collective-permute-start(bf16[640,1024]{1,0:T(8,128)(2,1)} %collective-permute-done.5.refs_4_), channel_id=1, source_target_pairs={{0,2},{1,3},{2,0},{3,1},{4,6},{5,7},{6,4},{7,5},{8,10},{9,11},{10,... | collective-permute-start | bytes 3932168 | tf_op jit(solution)/shard_map/ppermute | solution.py:159
  92.3 71.1 %collective-permute-start.6 = (bf16[640,1024]{1,0:T(8,128)(2,1)}, bf16[640,1024]{1,0:T(8,128)(2,1)}, u32[]{:S(2)}, u32[]{:S(2)}) collective-permute-start(bf16[640,1024]{1,0:T(8,128)(2,1)} %collective-permute-done.5.refs_4_), channel_id=1, source_target_pairs={{0,1},{1,0},{2,3},{3,2},{4,5},{5,4},{6,7},{7,6},{8,9},{9,8},{10,11... | collective-permute-start | bytes 3932168 | tf_op jit(solution)/shard_map/ppermute | solution.py:159
  92.3 26.1 %collective-permute-start.12 = (bf16[1024,512]{1,0:T(8,128)(2,1)S(1)}, bf16[1024,512]{1,0:T(8,128)(2,1)}, u32[]{:S(2)}, u32[]{:S(2)}) collective-permute-start(bf16[1024,512]{1,0:T(8,128)(2,1)S(1)} %maximum_select_fusion.1), channel_id=1, source_target_pairs={{0,8},{4,12},{8,0},{12,4},{16,24},{20,28},{24,16},{28,20},{1,9},{5... | collective-permute-start | bytes 3145736 | tf_op jit(solution)/shard_map/ppermute | solution.py:180
  92.5 63.8 %collective-permute-start.20 = (bf16[1024,512]{1,0:T(8,128)(2,1)}, bf16[1024,512]{1,0:T(8,128)(2,1)}, u32[]{:S(2)}, u32[]{:S(2)}) collective-permute-start(bf16[1024,512]{1,0:T(8,128)(2,1)} %maximum_select_fusion.2), channel_id=1, source_target_pairs={{0,24},{4,28},{8,16},{12,20},{16,8},{20,12},{24,0},{28,4},{1,25},{... | collective-permute-start | bytes 3145736 | tf_op jit(solution)/shard_map/ppermute | solution.py:180
  114.3 49.2 %collective-permute-start.19 = (bf16[1024,512]{1,0:T(8,128)(2,1)}, bf16[1024,512]{1,0:T(8,128)(2,1)}, u32[]{:S(2)}, u32[]{:S(2)}) collective-permute-start(bf16[1024,512]{1,0:T(8,128)(2,1)} %maximum_select_fusion.2), channel_id=1, source_target_pairs={{0,8},{4,12},{8,0},{12,4},{16,24},{20,28},{24,16},{28,20},{1,9},{5... | collective-permute-start | bytes 3145736 | tf_op jit(solution)/shard_map/ppermute | solution.py:180
  122.9 92.8 %collective-permute-start.1 = (bf16[640,1024]{1,0:T(8,128)(2,1)S(1)}, bf16[640,1024]{1,0:T(8,128)(2,1)S(1)}, u32[]{:S(2)}, u32[]{:S(2)}) collective-permute-start(bf16[640,1024]{1,0:T(8,128)(2,1)S(1)} %copy-done.2), channel_id=1, source_target_pairs={{0,1},{1,0},{2,3},{3,2},{4,5},{5,4},{6,7},{7,6},{8,9},{9,8},{10,11... | collective-permute-start | bytes 3932168 | tf_op jit(solution)/shard_map/ppermute | solution.py:159
  122.9 93.3 %collective-permute-start.3 = (bf16[640,1024]{1,0:T(8,128)(2,1)}, bf16[640,1024]{1,0:T(8,128)(2,1)}, u32[]{:S(2)}, u32[]{:S(2)}) collective-permute-start(bf16[640,1024]{1,0:T(8,128)(2,1)} %collective-permute-done.2.refs_2_), channel_id=1, source_target_pairs={{0,1},{1,0},{2,3},{3,2},{4,5},{5,4},{6,7},{7,6},{8,9},{9,8},{10,11... | collective-permute-start | bytes 3932168 | tf_op jit(solution)/shard_map/ppermute | solution.py:159
  156.3 29.6 %collective-permute-start.24 = (bf16[1024,512]{1,0:T(8,128)(2,1)}, bf16[1024,512]{1,0:T(8,128)(2,1)}, u32[]{:S(2)}, u32[]{:S(2)}) collective-permute-start(bf16[1024,512]{1,0:T(8,128)(2,1)} %get-tuple-element.26), channel_id=1, source_target_pairs={{0,8},{4,12},{8,0},{12,4},{16,24},{20,28},{24,16},{28,20},{1,9},{5... | collective-permute-start | bytes 3145736 | tf_op jit(solution)/shard_map/ppermute | solution.py:180
  163.5 47.2 %collective-permute-start.26 = (bf16[1024,512]{1,0:T(8,128)(2,1)}, bf16[1024,512]{1,0:T(8,128)(2,1)}, u32[]{:S(2)}, u32[]{:S(2)}) collective-permute-start(bf16[1024,512]{1,0:T(8,128)(2,1)} %get-tuple-element.26), channel_id=1, source_target_pairs={{0,24},{4,28},{8,16},{12,20},{16,8},{20,12},{24,0},{28,4},{1,25},{... | collective-permute-start | bytes 3145736 | tf_op jit(solution)/shard_map/ppermute | solution.py:180
  163.5 50.9 %collective-permute-start.10 = (bf16[640,1024]{1,0:T(8,128)(2,1)}, bf16[640,1024]{1,0:T(8,128)(2,1)}, u32[]{:S(2)}, u32[]{:S(2)}) collective-permute-start(bf16[640,1024]{1,0:T(8,128)(2,1)} %collective-permute-done.9.refs_6_), channel_id=1, source_target_pairs={{0,1},{1,0},{2,3},{3,2},{4,5},{5,4},{6,7},{7,6},{8,9},{9,8},{10,11... | collective-permute-start | bytes 3932168 | tf_op jit(solution)/shard_map/ppermute | solution.py:159
  185.9 49.5 %collective-permute-start.17 = (bf16[512,512]{1,0:T(8,128)(2,1)S(1)}, bf16[512,512]{1,0:T(8,128)(2,1)S(1)}, u32[]{:S(2)}, u32[]{:S(2)}) collective-permute-start(bf16[512,512]{1,0:T(8,128)(2,1)S(1)} %slice.190), channel_id=1, source_target_pairs={{0,8},{4,12},{8,0},{12,4},{16,24},{20,28},{24,16},{28,20},{1,9},{5... | collective-permute-start | bytes 1572872 | tf_op jit(solution)/shard_map/ppermute | solution.py:180
  210.7 26.1 %collective-permute-start.16 = (bf16[512,512]{1,0:T(8,128)(2,1)S(1)}, bf16[512,512]{1,0:T(8,128)(2,1)S(1)}, u32[]{:S(2)}, u32[]{:S(2)}) collective-permute-start(bf16[512,512]{1,0:T(8,128)(2,1)S(1)} %slice.189), channel_id=1, source_target_pairs={{0,24},{4,28},{8,16},{12,20},{16,8},{20,12},{24,0},{28,4},{1,25},{... | collective-permute-start | bytes 1572872 | tf_op jit(solution)/shard_map/ppermute | solution.py:180
  214.3 32.3 %collective-permute-start.15 = (bf16[512,512]{1,0:T(8,128)(2,1)S(1)}, bf16[512,512]{1,0:T(8,128)(2,1)S(1)}, u32[]{:S(2)}, u32[]{:S(2)}) collective-permute-start(bf16[512,512]{1,0:T(8,128)(2,1)S(1)} %slice.188), channel_id=1, source_target_pairs={{0,8},{4,12},{8,0},{12,4},{16,24},{20,28},{24,16},{28,20},{1,9},{5... | collective-permute-start | bytes 1572872 | tf_op jit(solution)/shard_map/ppermute | solution.py:180
  215.7 43.5 %collective-permute-start.14 = (bf16[512,512]{1,0:T(8,128)(2,1)S(1)}, bf16[512,512]{1,0:T(8,128)(2,1)S(1)}, u32[]{:S(2)}, u32[]{:S(2)}) collective-permute-start(bf16[512,512]{1,0:T(8,128)(2,1)S(1)} %slice.187), channel_id=1, source_target_pairs={{0,24},{4,28},{8,16},{12,20},{16,8},{20,12},{24,0},{28,4},{1,25},{... | collective-permute-start | bytes 1572872 | tf_op jit(solution)/shard_map/ppermute | solution.py:180
  216.2 53.8 %collective-permute-start.22 = (bf16[512,512]{1,0:T(8,128)(2,1)S(1)}, bf16[512,512]{1,0:T(8,128)(2,1)S(1)}, u32[]{:S(2)}, u32[]{:S(2)}) collective-permute-start(bf16[512,512]{1,0:T(8,128)(2,1)S(1)} %slice.192), channel_id=1, source_target_pairs={{0,8},{4,12},{8,0},{12,4},{16,24},{20,28},{24,16},{28,20},{1,9},{5... | collective-permute-start | bytes 1572872 | tf_op jit(solution)/shard_map/ppermute | solution.py:180
  235.4 57.5 %collective-permute-start.21 = (bf16[512,512]{1,0:T(8,128)(2,1)S(1)}, bf16[512,512]{1,0:T(8,128)(2,1)S(1)}, u32[]{:S(2)}, u32[]{:S(2)}) collective-permute-start(bf16[512,512]{1,0:T(8,128)(2,1)S(1)} %slice.191), channel_id=1, source_target_pairs={{0,24},{4,28},{8,16},{12,20},{16,8},{20,12},{24,0},{28,4},{1,25},{... | collective-permute-start | bytes 1572872 | tf_op jit(solution)/shard_map/ppermute | solution.py:180
  238.4 63.1 %collective-permute-start.25 = (bf16[512,512]{1,0:T(8,128)(2,1)S(1)}, bf16[512,512]{1,0:T(8,128)(2,1)S(1)}, u32[]{:S(2)}, u32[]{:S(2)}) collective-permute-start(bf16[512,512]{1,0:T(8,128)(2,1)S(1)} %slice.193), channel_id=1, source_target_pairs={{0,24},{4,28},{8,16},{12,20},{16,8},{20,12},{24,0},{28,4},{1,25},{... | collective-permute-start | bytes 1572872 | tf_op jit(solution)/shard_map/ppermute | solution.py:180
  261.3 64.0 %collective-permute-start.27 = (bf16[512,512]{1,0:T(8,128)(2,1)S(1)}, bf16[512,512]{1,0:T(8,128)(2,1)S(1)}, u32[]{:S(2)}, u32[]{:S(2)}) collective-permute-start(bf16[512,512]{1,0:T(8,128)(2,1)S(1)} %slice.194), channel_id=1, source_target_pairs={{0,8},{4,12},{8,0},{12,4},{16,24},{20,28},{24,16},{28,20},{1,9},{5... | collective-permute-start | bytes 1572872 | tf_op jit(solution)/shard_map/ppermute | solution.py:180
  338.0 15.0 %collective-permute-start.32 = (bf16[1280,512]{0,1:T(8,128)(2,1)}, bf16[1280,512]{0,1:T(8,128)(2,1)}, u32[]{:S(2)}, u32[]{:S(2)}) collective-permute-start(bf16[1280,512]{0,1:T(8,128)(2,1)} %convolution_convert_fusion.1), channel_id=1, source_target_pairs={{0,1},{1,0},{2,3},{3,2},{4,5},{5,4},{6,7},{7,6},{8,9},{9,8},{10,11... | collective-permute-start | bytes 3932168 | tf_op jit(solution)/shard_map/ppermute | solution.py:159
  341.1 29.0 %collective-permute-start.28 = (bf16[1280,512]{0,1:T(8,128)(2,1)}, bf16[1280,512]{0,1:T(8,128)(2,1)}, u32[]{:S(2)}, u32[]{:S(2)}) collective-permute-start(bf16[1280,512]{0,1:T(8,128)(2,1)} %convolution_convert_fusion.3), channel_id=1, source_target_pairs={{0,1},{1,0},{2,3},{3,2},{4,5},{5,4},{6,7},{7,6},{8,9},{9,8},{10,11... | collective-permute-start | bytes 3932168 | tf_op jit(solution)/shard_map/ppermute | solution.py:159
  345.1 32.0 %collective-permute-start.30 = (bf16[1280,512]{0,1:T(8,128)(2,1)}, bf16[1280,512]{0,1:T(8,128)(2,1)}, u32[]{:S(2)}, u32[]{:S(2)}) collective-permute-start(bf16[1280,512]{0,1:T(8,128)(2,1)} %fusion.7), channel_id=1, source_target_pairs={{0,2},{1,3},{2,0},{3,1},{4,6},{5,7},{6,4},{7,5},{8,10},{9,11},{10,... | collective-permute-start | bytes 3932168 | tf_op jit(solution)/shard_map/ppermute | solution.py:159
  351.5 17.8 %collective-permute-start.35 = (bf16[640,512]{0,1:T(8,128)(2,1)}, bf16[640,512]{0,1:T(8,128)(2,1)S(1)}, u32[]{:S(2)}, u32[]{:S(2)}) collective-permute-start(bf16[640,512]{0,1:T(8,128)(2,1)} %slice.247), channel_id=1, source_target_pairs={{0,4},{4,0},{8,12},{12,8},{16,20},{20,16},{24,28},{28,24},{1,5},{5... | collective-permute-start | bytes 1966088 | tf_op jit(solution)/shard_map/ppermute | solution.py:159
  355.6 27.7 %collective-permute-start.33 = (bf16[640,512]{0,1:T(8,128)(2,1)S(1)}, bf16[640,512]{0,1:T(8,128)(2,1)S(1)}, u32[]{:S(2)}, u32[]{:S(2)}) collective-permute-start(bf16[640,512]{0,1:T(8,128)(2,1)S(1)} %slice.248), channel_id=1, source_target_pairs={{0,4},{4,0},{8,12},{12,8},{16,20},{20,16},{24,28},{28,24},{1,5},{5... | collective-permute-start | bytes 1966088 | tf_op jit(solution)/shard_map/ppermute | solution.py:159
  369.5 20.5 %collective-permute-start.36 = (bf16[640,512]{0,1:T(8,128)(2,1)S(1)}, bf16[640,512]{0,1:T(8,128)(2,1)S(1)}, u32[]{:S(2)}, u32[]{:S(2)}) collective-permute-start(bf16[640,512]{0,1:T(8,128)(2,1)S(1)} %fusion.26), channel_id=1, source_target_pairs={{0,2},{1,3},{2,0},{3,1},{4,6},{5,7},{6,4},{7,5},{8,10},{9,11},{10,... | collective-permute-start | bytes 1966088 | tf_op jit(solution)/shard_map/ppermute | solution.py:159
  380.0 16.1 %collective-permute-start.31 = (bf16[640,512]{0,1:T(8,128)(2,1)S(1)}, bf16[640,512]{0,1:T(8,128)(2,1)S(1)}, u32[]{:S(2)}, u32[]{:S(2)}) collective-permute-start(bf16[640,512]{0,1:T(8,128)(2,1)S(1)} %slice.249), channel_id=1, source_target_pairs={{0,4},{4,0},{8,12},{12,8},{16,20},{20,16},{24,28},{28,24},{1,5},{5... | collective-permute-start | bytes 1966088 | tf_op jit(solution)/shard_map/ppermute | solution.py:159
  (21 other events, 507.7 us)
